TPU v7x, 32 devices: a whole 2x2x4 slice. The times are simulated.
32 devices in a mesh: row: 4 (over x, core), col: 8 (over z, y).
Axes of the slice: x: 2, y: 2, z: 4, core: 2. Of those that a mesh axis runs over, the one named last changes fastest.
Arguments:
- features: bfloat16 [8, 4, 128, 256], P('col', 'row'), may hold values from -6 to 6
- weight: bfloat16 [256, 256], replicated, may hold values from -0.375 to 0.375
- out_bias: float32 [256], replicated, may hold values from -3 to 3
- tile_values: bfloat16 [4, 8, 8, 3, 128, 128], P('row', 'col'), may hold values from -0.109375 to 0.109375
- tile_cols: int32 [4, 8, 8, 3], P('row', 'col'), may hold values from 0 to 3, as said below
- tile_counts: int32 [4, 8, 8], P('row', 'col'), may hold values from 1 to 3, as said below
- cotangent: bfloat16 [4, 8, 128, 256], P('row', 'col'), may hold values from -6 to 6
Outputs:
- activated: bfloat16 [4, 8, 128, 256], P('row', 'col')
- feature_grad: bfloat16 [8, 4, 128, 256], P('col', 'row')
Inputs may be any that keep to these rules, and one draw needn't show every extreme that they name: `tile_cols`: the 3 column tile numbers of one row tile are distinct. `tile_counts`: in every device's block some row tile has all 3 slots live; slots at or past a row tile's count are unused.
All inputs are finite; a program needn't handle non-finite values.
Results may differ from a plain program's by a relative error of at most 0.03.
Values may be sent and summed in bfloat16 or wider, within the bound.
No kernel may reach another device: no remote copies, remote signals or barrier semaphores. Data moves between devices by JAX's collectives and lax.ppermute only.
A program may use at most 64 MiB of HBM per device.

v0:
```python
import jax
import jax.numpy as jnp
from jax import lax
from jax.sharding import PartitionSpec as P


def silu_slope(preact):
    sigmoid_z = jax.nn.sigmoid(preact)
    return (preact * sigmoid_z, sigmoid_z * (1.0 + preact * (1.0 - sigmoid_z)))


def shards(features, weight, out_bias, tile_values, tile_cols, tile_counts, cotangent):
    tile_size = tile_values.shape[-1]
    width = weight.shape[1]
    sub_rows = features.shape[2]
    slot_count = tile_values.shape[3]
    row_tiles = tile_values.shape[2]
    slot_ids = jnp.arange(slot_count, dtype=jnp.int32)
    live = (slot_ids[None, :] < tile_counts[0, 0][:, None]).astype(jnp.bfloat16)
    tile_set = tile_values[0, 0] * live[:, :, None, None]
    col_index = tile_cols[0, 0]
    projected = jnp.dot(features[0, 0], weight, preferred_element_type=jnp.float32).astype(
        jnp.bfloat16
    )
    feat_panel = lax.all_gather(projected, "row", axis=0, tiled=True)
    col_tiles = feat_panel.shape[0] // tile_size
    gathered = feat_panel.reshape(col_tiles, tile_size, width)[col_index]
    product = jnp.einsum("tkij,tkjf->tif", tile_set, gathered, preferred_element_type=jnp.float32)
    preact = (
        lax.psum_scatter(
            product.reshape(sub_rows * lax.axis_size("col"), width).astype(jnp.bfloat16),
            "col",
            scatter_dimension=0,
            tiled=True,
        ).astype(jnp.float32)
        + out_bias
    )
    activated, slope = silu_slope(preact)
    pre_grad = (cotangent[0, 0].astype(jnp.float32) * slope).astype(jnp.bfloat16)
    grad_panel = lax.all_gather(pre_grad, "col", axis=0, tiled=True)
    grad_tiles = grad_panel.reshape(row_tiles, tile_size, width)
    back_terms = jnp.zeros((col_tiles, tile_size, width), jnp.float32)
    for slot in range(slot_count):
        contrib = jnp.einsum(
            "tij,tif->tjf", tile_set[:, slot], grad_tiles, preferred_element_type=jnp.float32
        )
        back_terms = back_terms + jax.ops.segment_sum(
            contrib, col_index[:, slot], num_segments=col_tiles
        )
    spread = lax.psum_scatter(
        back_terms.reshape(col_tiles * tile_size, width).astype(jnp.bfloat16),
        "row",
        scatter_dimension=0,
        tiled=True,
    )
    feature_grad = jnp.dot(spread, weight.T, preferred_element_type=jnp.float32)
    return (
        activated.astype(jnp.bfloat16)[None, None],
        feature_grad.astype(jnp.bfloat16)[None, None],
    )


def solution(mesh):
    in_specs = (
        P("col", "row", None, None),
        P(),
        P(),
        P("row", "col", None, None, None, None),
        P("row", "col", None, None),
        P("row", "col", None),
        P("row", "col", None, None),
    )
    out_specs = (P("row", "col", None, None), P("col", "row", None, None))
    return jax.shard_map(shards, mesh=mesh, in_specs=in_specs, out_specs=out_specs, check_vma=False)
```

profile of v0, /device:TPU:0, one launch (start us, length us, event | category | flops | bytes accessed | tf_op | source)
XLA Modules:
  0.0 151.0 jit_solution(7493896818670202049)
XLA Ops:
  7.2 0.0 copy-start
  7.2 0.0 copy-start.5
  7.2 0.0 copy-start.1
  7.2 0.0 copy-start.3
  7.2 0.0 reduce-scatter.3.cloned.1.call-start
  7.3 1.5 %copy.12 = bf16[1,1,8,3,128,128]{4,5,2,3,1,0:T(8,128)(2,1)S(1)} copy(bf16[1,1,8,3,128,128]{5,4,3,2,1,0:T(8,128)(2,1)} %param.10) | data formatting | bytes 1572864 | tf_op args[3]
  8.8 0.0 copy-done.5
  8.8 0.0 copy-done
  8.8 0.0 copy-done.1
  8.8 0.2 convolution_convert_fusion.1
  9.0 7.2 %all_gather.6 = bf16[512,256]{1,0:T(8,128)(2,1)S(1)} all-gather(bf16[128,256]{1,0:T(8,128)(2,1)S(1)} %convolution_convert_fusion.1), channel_id=1, replica_groups=mesh['row'=4,'col'=8] {'row'}, dimensions={0}, use_global_device_ids=true | all-gather | bytes 327680 | tf_op jit(solution)/shard_map/all_gather | solution.py:25
  16.2 0.0 copy-done.3
  16.2 0.1 copy.13
  16.3 0.1 reshape.75
  16.4 0.1 bitcast_multiply_fusion
  16.5 0.6 gather_fusion
  17.2 0.0 copy-start.2
  17.2 0.0 copy-start.4
  17.2 1.3 fusion.5
  18.5 0.0 reduce-scatter.3.cloned.1.call-update
  18.5 0.0 reduce-scatter.5.cloned.1.call-start
  18.6 63.8 %reduce-scatter.3.cloned.1.call-done = bf16[128,256]{1,0:T(8,128)(2,1)} async-done(((bf16[1024,256]{1,0:T(8,128)(2,1)}), bf16[128,256]{1,0:T(8,128)(2,1)}) %reduce-scatter.3.cloned.1.call-update) | async-done | bytes 65552 | tf_op jit(solution)/shard_map/reduce_scatter | solution.py:30
  82.4 0.0 copy-done.2
  82.4 0.0 copy-done.4
  82.4 1.5 %fusion.12 = (bf16[128,256]{1,0:T(8,128)(2,1)S(1)}, bf16[1,1,128,256]{3,2,1,0:T(8,128)(2,1)}) fusion(bf16[128,256]{1,0:T(8,128)(2,1)} %reduce-scatter.3.cloned.1.call-done, bf16[1,1,128,256]{3,2,1,0:T(8,128)(2,1)S(1)} %copy-done.2, f32[256]{0:T(256)S(1)} %copy-done.4), kind=kLoop, calls=%fused_computation.19 | loop fusion | flops 458752 | bytes 263168 | tf_op jit(solution)/shard_map/convert_element_type | solution.py:39
  83.9 31.5 %all_gather.7 = bf16[1024,256]{1,0:T(8,128)(2,1)S(1)} all-gather(bf16[128,256]{1,0:T(8,128)(2,1)S(1)} %get-tuple-element.2), channel_id=1, replica_groups=mesh['row'=4,'col'=8] {'col'}, dimensions={0}, use_global_device_ids=true | all-gather | bytes 589824 | tf_op jit(solution)/shard_map/all_gather | solution.py:40
  115.4 0.3 fusion.11
  115.7 1.3 fusion.10
  117.0 0.3 fusion.9
  117.3 1.3 scatter_fusion
  118.7 2.5 %scatter_fusion.1 = f32[4,128,256]{2,1,0:T(8,128)S(1)} fusion(f32[4,128,256]{2,1,0:T(8,128)S(1)} %broadcast.43.clone.1, s32[8]{0:T(128)S(1)} %get-tuple-element.5, f32[8,128,256]{2,1,0:T(8,128)} %fusion.10), kind=kCustom, calls=%fused_computation.2 | custom fusion | flops 262144 | bytes 3145760 | tf_op jit(solution)/shard_map/scatter-add | solution.py:47
  121.2 0.1 add.44
  121.2 1.3 scatter_fusion.2
  122.6 0.7 convert_element_type.49
  123.3 0.0 reduce-scatter.5.cloned.1.call-update
  123.3 19.2 %reduce-scatter.5.cloned.1.call-done = bf16[128,256]{1,0:T(8,128)(2,1)} async-done(((bf16[512,256]{1,0:T(8,128)(2,1)}), bf16[128,256]{1,0:T(8,128)(2,1)}) %reduce-scatter.5.cloned.1.call-update) | async-done | bytes 65552 | tf_op jit(solution)/shard_map/reduce_scatter | solution.py:50
  142.5 1.7 %fusion.8 = bf16[1,1,128,256]{3,2,1,0:T(8,128)(2,1)} fusion(bf16[128,256]{1,0:T(8,128)(2,1)} %reduce-scatter.5.cloned.1.call-done, bf16[256,256]{1,0:T(8,128)(2,1)S(1)} %copy-done), kind=kOutput, calls=%fused_computation.10 | convolution fusion | flops 16809984 | bytes 262144 | tf_op jit(solution)/shard_map/dot_general | solution.py:56
  (7 shorter events, 0.1 us)
Async XLA Ops:
  7.2 1.7 %copy-start = (bf16[256,256]{1,0:T(8,128)(2,1)S(1)}, bf16[256,256]{1,0:T(8,128)(2,1)}, u32[]{:S(2)}) copy-start(bf16[256,256]{1,0:T(8,128)(2,1)} %param.8) | copy-start | bytes 393220
  7.2 1.6 %copy-start.5 = (s32[1,1,8]{2,1,0:T(1,128)S(1)}, s32[1,1,8]{2,1,0:T(1,128)}, u32[]{:S(2)}) copy-start(s32[1,1,8]{2,1,0:T(1,128)} %param.12) | copy-start | bytes 100
  7.2 1.7 %copy-start.1 = (bf16[1,1,128,256]{3,2,1,0:T(8,128)(2,1)S(1)}, bf16[1,1,128,256]{3,2,1,0:T(8,128)(2,1)}, u32[]{:S(2)}) copy-start(bf16[1,1,128,256]{3,2,1,0:T(8,128)(2,1)} %param.7) | copy-start | bytes 196612
  7.2 9.0 %copy-start.3 = (s32[1,1,8,3]{2,1,3,0:T(1,128)S(1)}, s32[1,1,8,3]{2,1,3,0:T(1,128)}, u32[]{:S(2)}) copy-start(s32[1,1,8,3]{2,1,3,0:T(1,128)} %param.11) | copy-start | bytes 292
  7.2 75.2 %reduce-scatter.3.cloned.1.call-start = ((), (), s32[]{:S(2)}) async-start(), calls=%async_computation.2 | async-start | bytes 589824 | tf_op jit(solution)/shard_map/reduce_scatter | solution.py:30
  17.2 65.2 %copy-start.2 = (bf16[1,1,128,256]{3,2,1,0:T(8,128)(2,1)S(1)}, bf16[1,1,128,256]{3,2,1,0:T(8,128)(2,1)}, u32[]{:S(2)}) copy-start(bf16[1,1,128,256]{3,2,1,0:T(8,128)(2,1)} %param.13) | copy-start | bytes 196612
  17.2 65.2 %copy-start.4 = (f32[256]{0:T(256)S(1)}, f32[256]{0:T(256)}, u32[]{:S(2)}) copy-start(f32[256]{0:T(256)} %param.9) | copy-start | bytes 3076
  18.5 124.0 %reduce-scatter.5.cloned.1.call-start = ((), (), s32[]{:S(2)}) async-start(), calls=%async_computation.3 | async-start | bytes 327680 | tf_op jit(solution)/shard_map/reduce_scatter | solution.py:50
Sparse Core Ops, SparseCore 0:
  18.6 63.6 reduce-scatter.2
  123.4 18.9 reduce-scatter.4
where the time goes:
time: 151 us
  waiting for transfers between devices  83 us (55%)
  blocking collectives  38.7 us (26%)
  between operations  14.2 us (9%)
  other arithmetic  7.56 us (5%)
  matrix products  4.96 us (3%)
  local copies, waits for them, and re-layouts  2.47 us (2%)
    reduce_scatter x1, waiting for transfers between devices, shards(): lax.psum_scatter(product.reshape(sub_rows * lax.axis_size('col'), width)....  63.8 us
    all_gather x1, blocking collectives, shards(): grad_panel = lax.all_gather(pre_grad, 'col', axis=0, tiled=True)  31.5 us
    reduce_scatter x1, waiting for transfers between devices, shards(): lax.psum_scatter(back_terms.reshape(col_tiles * tile_size, width).astype(...  19.2 us
    all_gather x1, blocking collectives, shards(): feat_panel = lax.all_gather(projected, 'row', axis=0, tiled=True)  7.19 us
    scatter-add x3, other arithmetic, shards(): jax.ops.segment_sum(contrib, col_index[:, slot], num_segments=col_tiles)  5.1 us
  transfers between devices with their start and end apart: 2, of which 2 were waited for; matrix products, arithmetic and copies ran while one was open for 0% of the time, Pallas kernels for 0%

commit v1 on v0

v1 whole, which is shorter than its diff:
```python
import jax
import jax.numpy as jnp
from jax import lax
from jax.sharding import PartitionSpec as P


def silu_slope(preact):
    sigmoid_z = jax.nn.sigmoid(preact)
    return (preact * sigmoid_z, sigmoid_z * (1.0 + preact * (1.0 - sigmoid_z)))


def shift(value, axis, step):
    size = lax.axis_size(axis)
    return lax.ppermute(value, axis, [(i, (i + step) % size) for i in range(size)])


def gather_all(value, axis):
    size = lax.axis_size(axis)
    me = lax.axis_index(axis)
    parts = [value] + [shift(value, axis, -step) for step in range(1, size)]
    stacked = jnp.stack(parts)
    return stacked[(jnp.arange(size) - me) % size]


def scatter_sum(value, axis):
    size = lax.axis_size(axis)
    me = lax.axis_index(axis)
    total = lax.dynamic_index_in_dim(value, me, 0, False).astype(jnp.float32)
    for step in range(1, size):
        part = lax.dynamic_index_in_dim(value, (me + step) % size, 0, False)
        total = total + shift(part, axis, step).astype(jnp.float32)
    return total


def shards(features, weight, out_bias, tile_values, tile_cols, tile_counts, cotangent):
    tile_size = tile_values.shape[-1]
    width = weight.shape[1]
    slot_count = tile_values.shape[3]
    row_tiles = tile_values.shape[2]
    slot_ids = jnp.arange(slot_count, dtype=jnp.int32)
    live = (slot_ids[None, :] < tile_counts[0, 0][:, None]).astype(jnp.bfloat16)
    tile_set = tile_values[0, 0] * live[:, :, None, None]
    col_index = tile_cols[0, 0]
    projected = jnp.dot(features[0, 0], weight, preferred_element_type=jnp.float32).astype(
        jnp.bfloat16
    )
    panel = lax.all_gather(projected, "row", axis=0)
    col_tiles = panel.shape[0]
    gathered = panel[col_index]
    product = jnp.einsum("tkij,tkjf->tif", tile_set, gathered, preferred_element_type=jnp.float32)
    preact = scatter_sum(product.astype(jnp.bfloat16), "col") + out_bias
    activated, slope = silu_slope(preact)
    pre_grad = (cotangent[0, 0].astype(jnp.float32) * slope).astype(jnp.bfloat16)
    grad_tiles = gather_all(pre_grad, "col")
    back_terms = jnp.zeros((col_tiles, tile_size, width), jnp.float32)
    for slot in range(slot_count):
        contrib = jnp.einsum(
            "tij,tif->tjf", tile_set[:, slot], grad_tiles, preferred_element_type=jnp.float32
        )
        back_terms = back_terms + jax.ops.segment_sum(
            contrib, col_index[:, slot], num_segments=col_tiles
        )
    spread = scatter_sum(back_terms.astype(jnp.bfloat16), "row").astype(jnp.bfloat16)
    feature_grad = jnp.dot(spread, weight.T, preferred_element_type=jnp.float32)
    return (
        activated.astype(jnp.bfloat16)[None, None],
        feature_grad.astype(jnp.bfloat16)[None, None],
    )


def solution(mesh):
    in_specs = (
        P("col", "row", None, None),
        P(),
        P(),
        P("row", "col", None, None, None, None),
        P("row", "col", None, None),
        P("row", "col", None),
        P("row", "col", None, None),
    )
    out_specs = (P("row", "col", None, None), P("col", "row", None, None))
    return jax.shard_map(shards, mesh=mesh, in_specs=in_specs, out_specs=out_specs, check_vma=False)
```

time: 151 us -> 61.1 us (0.40)
  waiting for transfers between devices: 83 us -> 17.7 us
  blocking collectives: 38.7 us -> 7.19 us
  starting transfers between devices: 0.08 us -> 21.7 us
  between operations: 14.2 us -> 1.1 us
  matrix products: 4.96 us -> 3.31 us
    reduce_scatter x2 -> x0, waiting for transfers between devices: 82.9 us -> none  [the longest x1 63.8 us: shards(): lax.psum_scatter(product.reshape(sub_rows * lax.axis_size('col'), width)....]
    all_gather x2 -> x1, blocking collectives: 38.7 us -> 7.19 us  [shards(): panel = lax.all_gather(projected, 'row', axis=0)]
    ppermute x0 -> x17, starting transfers between devices: none -> 21.7 us  [shift(): lax.ppermute(value, axis, [(i, (i + step) % size) for i in range(size)])]
    ppermute x0 -> x17, waiting for transfers between devices: none -> 17.7 us  [shift(): lax.ppermute(value, axis, [(i, (i + step) % size) for i in range(size)])]
    convert_element_type x2 -> x1, other arithmetic: 2.26 us -> 0.03 us  [shards(): back_terms.astype(jnp.bfloat16)]
  transfers between devices with their start and end apart: 2 -> 17, of which waited for: 2 -> 7; matrix products, arithmetic and copies ran while one was open for 0% -> 1% of each run, Pallas kernels for 0% -> 0%
where the time goes in v1:
time: 61.1 us; the launch traced here: 60.9 us
  starting transfers between devices  21.7 us (36%)
  waiting for transfers between devices  17.7 us (29%)
  blocking collectives  7.19 us (12%)
  other arithmetic  6.79 us (11%)
  matrix products  3.31 us (5%)
  local copies, waits for them, and re-layouts  3.13 us (5%)
  between operations  1.1 us (2%)
    ppermute x17, starting transfers between devices, shift(): lax.ppermute(value, axis, [(i, (i + step) % size) for i in range(size)])  21.7 us
    ppermute x17, waiting for transfers between devices, shift(): lax.ppermute(value, axis, [(i, (i + step) % size) for i in range(size)])  17.7 us
    all_gather x1, blocking collectives, shards(): panel = lax.all_gather(projected, 'row', axis=0)  7.19 us
    scatter-add x3, other arithmetic, shards(): jax.ops.segment_sum(contrib, col_index[:, slot], num_segments=col_tiles)  5.09 us
    dot_general x3, matrix products, shards(): jnp.einsum('tij,tif->tjf', tile_set[:, slot], grad_tiles, preferred_eleme...  1.83 us
    unnamed x22, local copies, waits for them, and re-layouts  1.58 us
  transfers between devices with their start and end apart: 17, of which 7 were waited for; matrix products, arithmetic and copies ran while one was open for 1% of the time, Pallas kernels for 0%

profile of v1, /device:TPU:0, one launch (start us, length us, event | category | flops | bytes accessed | tf_op | source)
XLA Modules:
  0.0 60.9 jit_solution(17552345868794549637)
XLA Ops:
  0.6 0.0 copy-start
  0.6 0.0 copy-start.6
  0.7 0.0 copy-start.3
  0.7 0.0 copy-start.4
  0.8 1.5 %copy.12 = bf16[1,1,8,3,128,128]{4,5,2,3,1,0:T(8,128)(2,1)S(1)} copy(bf16[1,1,8,3,128,128]{5,4,3,2,1,0:T(8,128)(2,1)} %param.10) | data formatting | bytes 1572864 | tf_op args[3]
  2.3 0.0 copy-done.6
  2.3 0.0 copy-done
  2.3 0.0 copy-done.3
  2.3 0.2 convolution_convert_fusion.1
  2.5 7.2 %all-gather = bf16[512,256]{1,0:T(8,128)(2,1)S(1)} all-gather(bf16[128,256]{1,0:T(8,128)(2,1)S(1)} %convolution_convert_fusion.1), channel_id=2, replica_groups=mesh['row'=4,'col'=8] {'row'}, dimensions={0}, use_global_device_ids=true | all-gather | bytes 327680 | tf_op jit(solution)/shard_map/all_gather | solution.py:47
  9.7 0.0 copy-done.4
  9.7 0.1 copy.13
  9.8 0.1 reshape.118
  9.9 0.1 bitcast_multiply_fusion
  10.0 0.6 %gather_fusion = bf16[24,128,256]{2,1,0:T(8,128)(2,1)S(1)} fusion(bf16[4,128,256]{2,1,0:T(8,128)(2,1)S(1)} %bitcast.96, s32[1024]{0:T(1024)S(1)} %pad_clamp_fusion.1), kind=kCustom, calls=%fused_computation | custom fusion | bytes 3145824 | tf_op jit(solution)/shard_map/gather | solution.py:49
  10.6 0.0 copy-start.2
  10.7 0.0 copy-start.5
  10.7 0.5 fusion.5
  11.3 4.6 %collective-permute-start.6 = (bf16[128,256]{1,0:T(8,128)(2,1)S(1)}, bf16[128,256]{1,0:T(8,128)(2,1)S(1)}, u32[]{:S(2)}, u32[]{:S(2)}) collective-permute-start(bf16[128,256]{1,0:T(8,128)(2,1)S(1)} %get-tuple-element.6), channel_id=1, source_target_pairs={{0,7},{1,0},{2,1},{3,2},{4,3},{5,4},{6,5},{7,6},{8,15},{9,8},{10,9... | collective-permute-start | bytes 196616 | tf_op jit(solution)/shard_map/ppermute | solution.py:14
  15.9 0.4 collective-permute-start.5
  16.4 0.0 collective-permute-start.4
  16.4 3.0 %collective-permute-start.3 = (bf16[128,256]{1,0:T(8,128)(2,1)S(1)}, bf16[128,256]{1,0:T(8,128)(2,1)S(1)}, u32[]{:S(2)}, u32[]{:S(2)}) collective-permute-start(bf16[128,256]{1,0:T(8,128)(2,1)S(1)} %get-tuple-element.9), channel_id=1, source_target_pairs={{0,4},{1,5},{2,6},{3,7},{4,0},{5,1},{6,2},{7,3},{8,12},{9,13},{10,... | collective-permute-start | bytes 196616 | tf_op jit(solution)/shard_map/ppermute | solution.py:14
  19.3 0.0 collective-permute-start.2
  19.4 0.0 collective-permute-done.6
  19.4 1.9 %collective-permute-start.1 = (bf16[128,256]{1,0:T(8,128)(2,1)S(1)}, bf16[128,256]{1,0:T(8,128)(2,1)S(1)}, u32[]{:S(2)}, u32[]{:S(2)}) collective-permute-start(bf16[128,256]{1,0:T(8,128)(2,1)S(1)} %get-tuple-element.11), channel_id=1, source_target_pairs={{0,2},{1,3},{2,4},{3,5},{4,6},{5,7},{6,0},{7,1},{8,10},{9,11},{10,... | collective-permute-start | bytes 196616 | tf_op jit(solution)/shard_map/ppermute | solution.py:14
  21.3 0.0 collective-permute-done.5
  21.3 1.1 %collective-permute-start = (bf16[128,256]{1,0:T(8,128)(2,1)S(1)}, bf16[128,256]{1,0:T(8,128)(2,1)S(1)}, u32[]{:S(2)}, u32[]{:S(2)}) collective-permute-start(bf16[128,256]{1,0:T(8,128)(2,1)S(1)} %get-tuple-element.5), channel_id=1, source_target_pairs={{0,1},{1,2},{2,3},{3,4},{4,5},{5,6},{6,7},{7,0},{8,9},{9,10},{10,1... | collective-permute-start | bytes 196616 | tf_op jit(solution)/shard_map/ppermute | solution.py:14
  22.4 0.0 collective-permute-done.4
  22.4 5.6 %collective-permute-done.3 = bf16[128,256]{1,0:T(8,128)(2,1)S(1)} collective-permute-done((bf16[128,256]{1,0:T(8,128)(2,1)S(1)}, bf16[128,256]{1,0:T(8,128)(2,1)S(1)}, u32[]{:S(2)}, u32[]{:S(2)}) %collective-permute-start.3) | collective-permute-done | bytes 65568 | tf_op jit(solution)/shard_map/ppermute | solution.py:14
  28.0 2.5 %collective-permute-done.2 = bf16[128,256]{1,0:T(8,128)(2,1)S(1)} collective-permute-done((bf16[128,256]{1,0:T(8,128)(2,1)S(1)}, bf16[128,256]{1,0:T(8,128)(2,1)S(1)}, u32[]{:S(2)}, u32[]{:S(2)}) %collective-permute-start.2) | collective-permute-done | bytes 65568 | tf_op jit(solution)/shard_map/ppermute | solution.py:14
  30.5 0.0 collective-permute-done.1
  30.5 0.0 collective-permute-done
  30.5 0.8 %bitcast_dynamic-update-slice_fusion.7 = (bf16[8,128,256]{2,1,0:T(8,128)(2,1)S(1)}, bf16[128,256]{1,0:T(8,128)(2,1)S(1)}, f32[128,256]{1,0:T(8,128)}) fusion(bf16[1,1,128,256]{3,2,1,0:T(8,128)(2,1)S(1)} %copy-done.2, f32[256]{0:T(256)S(1)} %copy-done.5, bf16[128,256]{1,0:T(8,128)(2,1)S(1)} %collective-permute-done.6, ...), kind=kLoop, calls=%fused_computation.43 | loop fusion | flops 851967 | bytes 852996
  31.3 0.0 collective-permute-start.7
  31.3 1.6 %collective-permute-start.8 = (bf16[128,256]{1,0:T(8,128)(2,1)S(1)}, bf16[128,256]{1,0:T(8,128)(2,1)S(1)}, u32[]{:S(2)}, u32[]{:S(2)}) collective-permute-start(bf16[128,256]{1,0:T(8,128)(2,1)S(1)} %get-tuple-element.3), channel_id=1, source_target_pairs={{0,6},{1,7},{2,0},{3,1},{4,2},{5,3},{6,4},{7,5},{8,14},{9,15},{10,... | collective-permute-start | bytes 196616 | tf_op jit(solution)/shard_map/ppermute | solution.py:14
  32.9 0.8 %collective-permute-start.9 = (bf16[128,256]{1,0:T(8,128)(2,1)S(1)}, bf16[128,256]{1,0:T(8,128)(2,1)S(1)}, u32[]{:S(2)}, u32[]{:S(2)}) collective-permute-start(bf16[128,256]{1,0:T(8,128)(2,1)S(1)} %get-tuple-element.3), channel_id=1, source_target_pairs={{0,5},{1,6},{2,7},{3,0},{4,1},{5,2},{6,3},{7,4},{8,13},{9,14},{10,... | collective-permute-start | bytes 196616 | tf_op jit(solution)/shard_map/ppermute | solution.py:14
  33.7 2.1 %collective-permute-start.10 = (bf16[128,256]{1,0:T(8,128)(2,1)S(1)}, bf16[128,256]{1,0:T(8,128)(2,1)S(1)}, u32[]{:S(2)}, u32[]{:S(2)}) collective-permute-start(bf16[128,256]{1,0:T(8,128)(2,1)S(1)} %get-tuple-element.3), channel_id=1, source_target_pairs={{0,4},{1,5},{2,6},{3,7},{4,0},{5,1},{6,2},{7,3},{8,12},{9,13},{10,... | collective-permute-start | bytes 196616 | tf_op jit(solution)/shard_map/ppermute | solution.py:14
  35.8 1.1 %collective-permute-start.11 = (bf16[128,256]{1,0:T(8,128)(2,1)S(1)}, bf16[128,256]{1,0:T(8,128)(2,1)S(1)}, u32[]{:S(2)}, u32[]{:S(2)}) collective-permute-start(bf16[128,256]{1,0:T(8,128)(2,1)S(1)} %get-tuple-element.3), channel_id=1, source_target_pairs={{0,3},{1,4},{2,5},{3,6},{4,7},{5,0},{6,1},{7,2},{8,11},{9,12},{10,... | collective-permute-start | bytes 196616 | tf_op jit(solution)/shard_map/ppermute | solution.py:14
  37.0 0.0 collective-permute-done.7
  37.0 1.1 %collective-permute-start.12 = (bf16[128,256]{1,0:T(8,128)(2,1)S(1)}, bf16[128,256]{1,0:T(8,128)(2,1)S(1)}, u32[]{:S(2)}, u32[]{:S(2)}) collective-permute-start(bf16[128,256]{1,0:T(8,128)(2,1)S(1)} %get-tuple-element.3), channel_id=1, source_target_pairs={{0,2},{1,3},{2,4},{3,5},{4,6},{5,7},{6,0},{7,1},{8,10},{9,11},{10,... | collective-permute-start | bytes 196616 | tf_op jit(solution)/shard_map/ppermute | solution.py:14
  38.1 0.0 collective-permute-done.8
  38.1 2.0 %collective-permute-start.13 = (bf16[128,256]{1,0:T(8,128)(2,1)S(1)}, bf16[128,256]{1,0:T(8,128)(2,1)S(1)}, u32[]{:S(2)}, u32[]{:S(2)}) collective-permute-start(bf16[128,256]{1,0:T(8,128)(2,1)S(1)} %get-tuple-element.3), channel_id=1, source_target_pairs={{0,1},{1,2},{2,3},{3,4},{4,5},{5,6},{6,7},{7,0},{8,9},{9,10},{10,1... | collective-permute-start | bytes 196616 | tf_op jit(solution)/shard_map/ppermute | solution.py:14
  40.1 0.0 collective-permute-done.9
  40.2 4.1 %collective-permute-done.10 = bf16[128,256]{1,0:T(8,128)(2,1)S(1)} collective-permute-done((bf16[128,256]{1,0:T(8,128)(2,1)S(1)}, bf16[128,256]{1,0:T(8,128)(2,1)S(1)}, u32[]{:S(2)}, u32[]{:S(2)}) %collective-permute-start.10) | collective-permute-done | bytes 65568 | tf_op jit(solution)/shard_map/ppermute | solution.py:14
  44.3 2.1 %collective-permute-done.11 = bf16[128,256]{1,0:T(8,128)(2,1)S(1)} collective-permute-done((bf16[128,256]{1,0:T(8,128)(2,1)S(1)}, bf16[128,256]{1,0:T(8,128)(2,1)S(1)}, u32[]{:S(2)}, u32[]{:S(2)}) %collective-permute-start.11) | collective-permute-done | bytes 65568 | tf_op jit(solution)/shard_map/ppermute | solution.py:14
  46.4 0.0 collective-permute-done.12
  46.4 0.0 collective-permute-done.13
  46.4 0.6 gather_fusion.1
  47.0 0.3 fusion.11
  47.3 1.3 %fusion.10 = f32[8,128,256]{2,1,0:T(8,128)} fusion(bf16[8,128,256]{2,1,0:T(8,128)(2,1)S(1)} %gather_fusion.1, bf16[8,3,128,128]{2,3,0,1:T(8,128)(2,1)S(1)} %bitcast_multiply_fusion), kind=kOutput, calls=%fused_computation.16 | convolution fusion | flops 67108864 | bytes 1835008 | tf_op jit(solution)/shard_map/tij,tif->tjf/dot_general | solution.py:57
  48.6 0.3 fusion.9
  48.9 1.3 %scatter_fusion = f32[4,128,256]{2,1,0:T(8,128)S(1)} fusion(f32[4,128,256]{2,1,0:T(8,128)S(1)} %broadcast.116.clone, s32[8]{0:T(128)S(1)} %get-tuple-element.17, f32[8,128,256]{2,1,0:T(8,128)S(1)} %fusion.11), kind=kCustom, calls=%fused_computation.2 | custom fusion | flops 262144 | bytes 3145760 | tf_op jit(solution)/shard_map/scatter-add | solution.py:60
  50.3 2.5 %scatter_fusion.1 = f32[4,128,256]{2,1,0:T(8,128)S(1)} fusion(f32[4,128,256]{2,1,0:T(8,128)S(1)} %broadcast.116.clone.1, s32[8]{0:T(128)S(1)} %get-tuple-element.16, f32[8,128,256]{2,1,0:T(8,128)} %fusion.10), kind=kCustom, calls=%fused_computation.3 | custom fusion | flops 262144 | bytes 3145760 | tf_op jit(solution)/shard_map/scatter-add | solution.py:60
  52.7 0.1 add.223
  52.8 0.0 copy-start.1
  52.8 1.3 %scatter_fusion.2 = f32[4,128,256]{2,1,0:T(8,128)S(1)} fusion(f32[4,128,256]{2,1,0:T(8,128)S(1)} %add.223, s32[8]{0:T(128)S(1)} %get-tuple-element.15, f32[8,128,256]{2,1,0:T(8,128)S(1)} %fusion.9), kind=kCustom, calls=%fused_computation.4 | custom fusion | flops 262144 | bytes 3145760 | tf_op jit(solution)/shard_map/scatter-add | solution.py:60
  54.2 0.8 %collective-permute-start.16 = (bf16[128,256]{1,0:T(8,128)(2,1)S(1)}, bf16[128,256]{1,0:T(8,128)(2,1)S(1)}, u32[]{:S(2)}, u32[]{:S(2)}) collective-permute-start(bf16[128,256]{1,0:T(8,128)(2,1)S(1)} %get-tuple-element.13), channel_id=1, source_target_pairs={{0,24},{8,0},{16,8},{24,16},{1,25},{9,1},{17,9},{25,17},{2,26},{10... | collective-permute-start | bytes 196616 | tf_op jit(solution)/shard_map/ppermute | solution.py:14
  55.0 0.8 %collective-permute-start.15 = (bf16[128,256]{1,0:T(8,128)(2,1)S(1)}, bf16[128,256]{1,0:T(8,128)(2,1)S(1)}, u32[]{:S(2)}, u32[]{:S(2)}) collective-permute-start(bf16[128,256]{1,0:T(8,128)(2,1)S(1)} %get-tuple-element.14), channel_id=1, source_target_pairs={{0,16},{8,24},{16,0},{24,8},{1,17},{9,25},{17,1},{25,9},{2,18},{10... | collective-permute-start | bytes 196616 | tf_op jit(solution)/shard_map/ppermute | solution.py:14
  55.8 0.2 collective-permute-start.14
  56.0 0.7 %fusion.27 = bf16[1,1,128,256]{3,2,1,0:T(8,128)(2,1)} fusion(f32[128,256]{1,0:T(8,128)S(1)} %copy-done.1), kind=kLoop, calls=%fused_computation.56 | loop fusion | flops 163840 | bytes 196608 | tf_op jit(solution)/shard_map/broadcast_in_dim | solution.py:66
  56.7 0.5 collective-permute-done.16
  57.2 2.7 %collective-permute-done.15 = bf16[128,256]{1,0:T(8,128)(2,1)S(1)} collective-permute-done((bf16[128,256]{1,0:T(8,128)(2,1)S(1)}, bf16[128,256]{1,0:T(8,128)(2,1)S(1)}, u32[]{:S(2)}, u32[]{:S(2)}) %collective-permute-start.15) | collective-permute-done | bytes 65568 | tf_op jit(solution)/shard_map/ppermute | solution.py:14
  59.9 0.2 collective-permute-done.14
  60.1 0.8 %fusion.8 = bf16[1,1,128,256]{3,2,1,0:T(8,128)(2,1)} fusion(bf16[256,256]{1,0:T(8,128)(2,1)S(1)} %copy-done, bf16[128,256]{1,0:T(8,128)(2,1)S(1)} %collective-permute-done.16, bf16[128,256]{1,0:T(8,128)(2,1)S(1)} %collective-permute-done.15, bf16[128,256]{1,0:T(8,128)(2,1)S(1)} %collective-permute-done.14, ...), kind=kOutput, calls=%fused_computation.11 | convolution fusion | flops 17072128 | bytes 458756 | tf_op jit(solution)/shard_map/dot_general | solution.py:64
  (22 shorter events, 0.3 us)
Async XLA Ops:
  0.6 1.7 %copy-start = (bf16[256,256]{1,0:T(8,128)(2,1)S(1)}, bf16[256,256]{1,0:T(8,128)(2,1)}, u32[]{:S(2)}) copy-start(bf16[256,256]{1,0:T(8,128)(2,1)} %param.8) | copy-start | bytes 393220
  0.6 1.6 %copy-start.6 = (s32[1,1,8]{2,1,0:T(1,128)S(1)}, s32[1,1,8]{2,1,0:T(1,128)}, u32[]{:S(2)}) copy-start(s32[1,1,8]{2,1,0:T(1,128)} %param.12) | copy-start | bytes 100
  0.7 1.7 %copy-start.3 = (bf16[1,1,128,256]{3,2,1,0:T(8,128)(2,1)S(1)}, bf16[1,1,128,256]{3,2,1,0:T(8,128)(2,1)}, u32[]{:S(2)}) copy-start(bf16[1,1,128,256]{3,2,1,0:T(8,128)(2,1)} %param.7) | copy-start | bytes 196612
  0.7 9.0 %copy-start.4 = (s32[1,1,8,3]{2,1,3,0:T(1,128)S(1)}, s32[1,1,8,3]{2,1,3,0:T(1,128)}, u32[]{:S(2)}) copy-start(s32[1,1,8,3]{2,1,3,0:T(1,128)} %param.11) | copy-start | bytes 292
  10.6 19.8 %copy-start.2 = (bf16[1,1,128,256]{3,2,1,0:T(8,128)(2,1)S(1)}, bf16[1,1,128,256]{3,2,1,0:T(8,128)(2,1)}, u32[]{:S(2)}) copy-start(bf16[1,1,128,256]{3,2,1,0:T(8,128)(2,1)} %param.13) | copy-start | bytes 196612
  10.7 19.8 %copy-start.5 = (f32[256]{0:T(256)S(1)}, f32[256]{0:T(256)}, u32[]{:S(2)}) copy-start(f32[256]{0:T(256)} %param.9) | copy-start | bytes 3076
  11.3 8.1 %collective-permute-start.6 = (bf16[128,256]{1,0:T(8,128)(2,1)S(1)}, bf16[128,256]{1,0:T(8,128)(2,1)S(1)}, u32[]{:S(2)}, u32[]{:S(2)}) collective-permute-start(bf16[128,256]{1,0:T(8,128)(2,1)S(1)} %get-tuple-element.6), channel_id=1, source_target_pairs={{0,7},{1,0},{2,1},{3,2},{4,3},{5,4},{6,5},{7,6},{8,15},{9,8},{10,9... | collective-permute-start | bytes 196616 | tf_op jit(solution)/shard_map/ppermute | solution.py:14
  15.9 5.4 %collective-permute-start.5 = (bf16[128,256]{1,0:T(8,128)(2,1)S(1)}, bf16[128,256]{1,0:T(8,128)(2,1)S(1)}, u32[]{:S(2)}, u32[]{:S(2)}) collective-permute-start(bf16[128,256]{1,0:T(8,128)(2,1)S(1)} %get-tuple-element.7), channel_id=1, source_target_pairs={{0,6},{1,7},{2,0},{3,1},{4,2},{5,3},{6,4},{7,5},{8,14},{9,15},{10,... | collective-permute-start | bytes 196616 | tf_op jit(solution)/shard_map/ppermute | solution.py:14
  16.4 6.1 %collective-permute-start.4 = (bf16[128,256]{1,0:T(8,128)(2,1)S(1)}, bf16[128,256]{1,0:T(8,128)(2,1)S(1)}, u32[]{:S(2)}, u32[]{:S(2)}) collective-permute-start(bf16[128,256]{1,0:T(8,128)(2,1)S(1)} %get-tuple-element.8), channel_id=1, source_target_pairs={{0,5},{1,6},{2,7},{3,0},{4,1},{5,2},{6,3},{7,4},{8,13},{9,14},{10,... | collective-permute-start | bytes 196616 | tf_op jit(solution)/shard_map/ppermute | solution.py:14
  16.4 11.7 %collective-permute-start.3 = (bf16[128,256]{1,0:T(8,128)(2,1)S(1)}, bf16[128,256]{1,0:T(8,128)(2,1)S(1)}, u32[]{:S(2)}, u32[]{:S(2)}) collective-permute-start(bf16[128,256]{1,0:T(8,128)(2,1)S(1)} %get-tuple-element.9), channel_id=1, source_target_pairs={{0,4},{1,5},{2,6},{3,7},{4,0},{5,1},{6,2},{7,3},{8,12},{9,13},{10,... | collective-permute-start | bytes 196616 | tf_op jit(solution)/shard_map/ppermute | solution.py:14
  19.3 11.1 %collective-permute-start.2 = (bf16[128,256]{1,0:T(8,128)(2,1)S(1)}, bf16[128,256]{1,0:T(8,128)(2,1)S(1)}, u32[]{:S(2)}, u32[]{:S(2)}) collective-permute-start(bf16[128,256]{1,0:T(8,128)(2,1)S(1)} %get-tuple-element.10), channel_id=1, source_target_pairs={{0,3},{1,4},{2,5},{3,6},{4,7},{5,0},{6,1},{7,2},{8,11},{9,12},{10,... | collective-permute-start | bytes 196616 | tf_op jit(solution)/shard_map/ppermute | solution.py:14
  19.4 11.1 %collective-permute-start.1 = (bf16[128,256]{1,0:T(8,128)(2,1)S(1)}, bf16[128,256]{1,0:T(8,128)(2,1)S(1)}, u32[]{:S(2)}, u32[]{:S(2)}) collective-permute-start(bf16[128,256]{1,0:T(8,128)(2,1)S(1)} %get-tuple-element.11), channel_id=1, source_target_pairs={{0,2},{1,3},{2,4},{3,5},{4,6},{5,7},{6,0},{7,1},{8,10},{9,11},{10,... | collective-permute-start | bytes 196616 | tf_op jit(solution)/shard_map/ppermute | solution.py:14
  21.3 9.2 %collective-permute-start = (bf16[128,256]{1,0:T(8,128)(2,1)S(1)}, bf16[128,256]{1,0:T(8,128)(2,1)S(1)}, u32[]{:S(2)}, u32[]{:S(2)}) collective-permute-start(bf16[128,256]{1,0:T(8,128)(2,1)S(1)} %get-tuple-element.5), channel_id=1, source_target_pairs={{0,1},{1,2},{2,3},{3,4},{4,5},{5,6},{6,7},{7,0},{8,9},{9,10},{10,1... | collective-permute-start | bytes 196616 | tf_op jit(solution)/shard_map/ppermute | solution.py:14
  31.3 5.7 %collective-permute-start.7 = (bf16[128,256]{1,0:T(8,128)(2,1)S(1)}, bf16[128,256]{1,0:T(8,128)(2,1)S(1)}, u32[]{:S(2)}, u32[]{:S(2)}) collective-permute-start(bf16[128,256]{1,0:T(8,128)(2,1)S(1)} %get-tuple-element.3), channel_id=1, source_target_pairs={{0,7},{1,0},{2,1},{3,2},{4,3},{5,4},{6,5},{7,6},{8,15},{9,8},{10,9... | collective-permute-start | bytes 196616 | tf_op jit(solution)/shard_map/ppermute | solution.py:14
  31.3 6.8 %collective-permute-start.8 = (bf16[128,256]{1,0:T(8,128)(2,1)S(1)}, bf16[128,256]{1,0:T(8,128)(2,1)S(1)}, u32[]{:S(2)}, u32[]{:S(2)}) collective-permute-start(bf16[128,256]{1,0:T(8,128)(2,1)S(1)} %get-tuple-element.3), channel_id=1, source_target_pairs={{0,6},{1,7},{2,0},{3,1},{4,2},{5,3},{6,4},{7,5},{8,14},{9,15},{10,... | collective-permute-start | bytes 196616 | tf_op jit(solution)/shard_map/ppermute | solution.py:14
  32.9 7.3 %collective-permute-start.9 = (bf16[128,256]{1,0:T(8,128)(2,1)S(1)}, bf16[128,256]{1,0:T(8,128)(2,1)S(1)}, u32[]{:S(2)}, u32[]{:S(2)}) collective-permute-start(bf16[128,256]{1,0:T(8,128)(2,1)S(1)} %get-tuple-element.3), channel_id=1, source_target_pairs={{0,5},{1,6},{2,7},{3,0},{4,1},{5,2},{6,3},{7,4},{8,13},{9,14},{10,... | collective-permute-start | bytes 196616 | tf_op jit(solution)/shard_map/ppermute | solution.py:14
  33.7 10.6 %collective-permute-start.10 = (bf16[128,256]{1,0:T(8,128)(2,1)S(1)}, bf16[128,256]{1,0:T(8,128)(2,1)S(1)}, u32[]{:S(2)}, u32[]{:S(2)}) collective-permute-start(bf16[128,256]{1,0:T(8,128)(2,1)S(1)} %get-tuple-element.3), channel_id=1, source_target_pairs={{0,4},{1,5},{2,6},{3,7},{4,0},{5,1},{6,2},{7,3},{8,12},{9,13},{10,... | collective-permute-start | bytes 196616 | tf_op jit(solution)/shard_map/ppermute | solution.py:14
  35.8 10.5 %collective-permute-start.11 = (bf16[128,256]{1,0:T(8,128)(2,1)S(1)}, bf16[128,256]{1,0:T(8,128)(2,1)S(1)}, u32[]{:S(2)}, u32[]{:S(2)}) collective-permute-start(bf16[128,256]{1,0:T(8,128)(2,1)S(1)} %get-tuple-element.3), channel_id=1, source_target_pairs={{0,3},{1,4},{2,5},{3,6},{4,7},{5,0},{6,1},{7,2},{8,11},{9,12},{10,... | collective-permute-start | bytes 196616 | tf_op jit(solution)/shard_map/ppermute | solution.py:14
  37.0 9.4 %collective-permute-start.12 = (bf16[128,256]{1,0:T(8,128)(2,1)S(1)}, bf16[128,256]{1,0:T(8,128)(2,1)S(1)}, u32[]{:S(2)}, u32[]{:S(2)}) collective-permute-start(bf16[128,256]{1,0:T(8,128)(2,1)S(1)} %get-tuple-element.3), channel_id=1, source_target_pairs={{0,2},{1,3},{2,4},{3,5},{4,6},{5,7},{6,0},{7,1},{8,10},{9,11},{10,... | collective-permute-start | bytes 196616 | tf_op jit(solution)/shard_map/ppermute | solution.py:14
  38.1 8.3 %collective-permute-start.13 = (bf16[128,256]{1,0:T(8,128)(2,1)S(1)}, bf16[128,256]{1,0:T(8,128)(2,1)S(1)}, u32[]{:S(2)}, u32[]{:S(2)}) collective-permute-start(bf16[128,256]{1,0:T(8,128)(2,1)S(1)} %get-tuple-element.3), channel_id=1, source_target_pairs={{0,1},{1,2},{2,3},{3,4},{4,5},{5,6},{6,7},{7,0},{8,9},{9,10},{10,1... | collective-permute-start | bytes 196616 | tf_op jit(solution)/shard_map/ppermute | solution.py:14
  52.8 3.2 %copy-start.1 = (f32[128,256]{1,0:T(8,128)S(1)}, f32[128,256]{1,0:T(8,128)}, u32[]{:S(2)}) copy-start(f32[128,256]{1,0:T(8,128)} %get-tuple-element.4) | copy-start | bytes 393220
  54.2 3.0 %collective-permute-start.16 = (bf16[128,256]{1,0:T(8,128)(2,1)S(1)}, bf16[128,256]{1,0:T(8,128)(2,1)S(1)}, u32[]{:S(2)}, u32[]{:S(2)}) collective-permute-start(bf16[128,256]{1,0:T(8,128)(2,1)S(1)} %get-tuple-element.13), channel_id=1, source_target_pairs={{0,24},{8,0},{16,8},{24,16},{1,25},{9,1},{17,9},{25,17},{2,26},{10... | collective-permute-start | bytes 196616 | tf_op jit(solution)/shard_map/ppermute | solution.py:14
  55.0 4.9 %collective-permute-start.15 = (bf16[128,256]{1,0:T(8,128)(2,1)S(1)}, bf16[128,256]{1,0:T(8,128)(2,1)S(1)}, u32[]{:S(2)}, u32[]{:S(2)}) collective-permute-start(bf16[128,256]{1,0:T(8,128)(2,1)S(1)} %get-tuple-element.14), channel_id=1, source_target_pairs={{0,16},{8,24},{16,0},{24,8},{1,17},{9,25},{17,1},{25,9},{2,18},{10... | collective-permute-start | bytes 196616 | tf_op jit(solution)/shard_map/ppermute | solution.py:14
  55.8 4.3 %collective-permute-start.14 = (bf16[128,256]{1,0:T(8,128)(2,1)S(1)}, bf16[128,256]{1,0:T(8,128)(2,1)S(1)}, u32[]{:S(2)}, u32[]{:S(2)}) collective-permute-start(bf16[128,256]{1,0:T(8,128)(2,1)S(1)} %get-tuple-element.12), channel_id=1, source_target_pairs={{0,8},{8,16},{16,24},{24,0},{1,9},{9,17},{17,25},{25,1},{2,10},{10... | collective-permute-start | bytes 196616 | tf_op jit(solution)/shard_map/ppermute | solution.py:14

commit v2 on v0

v2 whole, which is shorter than its diff:
```python
import jax
import jax.numpy as jnp
from jax import lax
from jax.experimental import pallas as pl
from jax.experimental.pallas import tpu as pltpu
from jax.sharding import PartitionSpec as P

BOTH = ("row", "col")
HBM = pl.BlockSpec(memory_space=pltpu.HBM)


def silu_slope(preact):
    sigmoid_z = jax.nn.sigmoid(preact)
    return (preact * sigmoid_z, sigmoid_z * (1.0 + preact * (1.0 - sigmoid_z)))


def swap(value, row=0, col=0):
    rows, cols = lax.axis_size("row"), lax.axis_size("col")
    pairs = [(r * cols + c, (r ^ row) * cols + (c ^ col)) for r in range(rows) for c in range(cols)]
    return lax.ppermute(value, BOTH, pairs)


def limit(count):
    return 56 * 1024 * 1024 if count * 2 > 6 * 1024 * 1024 else 8 * 1024 * 1024


def front_kernel(cols_hbm, counts_hbm, tiles_hbm, feat_hbm, cot_hbm, bias_hbm, dense, dense_t, feat, cot, bias, cols, counts, tiles, sems):
    row_tiles, slots, tile, _ = tiles.shape
    me_row, me_col = lax.axis_index("row"), lax.axis_index("col")
    copies = [
        pltpu.make_async_copy(source, target, sems.at[i])
        for i, (source, target) in enumerate(
            (
                (cols_hbm.at[0, 0], cols),
                (counts_hbm.at[0], counts),
                (tiles_hbm.at[0, 0], tiles),
                (feat_hbm.at[0, 0], feat),
                (cot_hbm.at[0, 0], cot),
                (bias_hbm, bias),
            )
        )
    ]
    for copy in copies:
        copy.start()
    dense[...] = jnp.zeros(dense.shape, dense.dtype)
    dense_t[...] = jnp.zeros(dense_t.shape, dense_t.dtype)
    for copy in copies:
        copy.wait()

    def place(position):
        row_tile = position ^ me_col
        start = pl.multiple_of(position * tile, tile)
        for slot in range(slots):

            @pl.when(slot < counts[0, row_tile])
            def _():
                column = pl.multiple_of((cols[row_tile, slot] ^ me_row) * tile, tile)
                value = tiles[row_tile, slot]
                dense[pl.ds(start, tile), pl.ds(column, tile)] = value
                dense_t[pl.ds(column, tile), pl.ds(start, tile)] = value.T

    if row_tiles <= 8:
        for position in range(row_tiles):
            place(position)
    else:
        pl.loop(0, row_tiles)(place)


def front(tile_cols, tile_counts, tile_values, features, cotangent, out_bias):
    row_tiles, slots, tile, _ = tile_values.shape[2:]
    height, width = row_tiles * tile, lax.axis_size("row") * tile
    kind = tile_values.dtype
    return pl.pallas_call(
        front_kernel,
        in_specs=[HBM] * 6,
        out_shape=(
            jax.ShapeDtypeStruct((height, width), kind),
            jax.ShapeDtypeStruct((width, height), kind),
            jax.ShapeDtypeStruct(features.shape[2:], features.dtype),
            jax.ShapeDtypeStruct(cotangent.shape[2:], cotangent.dtype),
            jax.ShapeDtypeStruct((1, *out_bias.shape), out_bias.dtype),
        ),
        scratch_shapes=[
            pltpu.SMEM((row_tiles, slots), jnp.int32),
            pltpu.SMEM((1, row_tiles), jnp.int32),
            pltpu.VMEM((row_tiles, slots, tile, tile), kind),
            pltpu.SemaphoreType.DMA((6,)),
        ],
        compiler_params=pltpu.CompilerParams(vmem_limit_bytes=limit(height * width)),
        cost_estimate=pl.CostEstimate(flops=0, bytes_accessed=tile_values.size * 2, transcendentals=0),
    )(tile_cols, tile_counts, tile_values, features, cotangent, out_bias.reshape(1, -1))


def forward_kernel(count, *refs):
    pieces, (weight, dense), outs, projected = refs[:count], refs[count : count + 2], refs[count + 2 : -1], refs[-1]
    tile = pieces[0].shape[0]
    for j, piece in enumerate(pieces):
        value = jnp.dot(piece[...], weight[...], preferred_element_type=jnp.float32)
        projected[j * tile : (j + 1) * tile] = value.astype(projected.dtype)
    for p, out in enumerate(outs):
        value = jnp.dot(dense[p * tile : (p + 1) * tile], projected[...], preferred_element_type=jnp.float32)
        out[...] = value.astype(out.dtype)


def forward(pieces, weight, dense):
    tile, width = pieces[0].shape
    return pl.pallas_call(
        lambda *refs: forward_kernel(len(pieces), *refs),
        out_shape=[jax.ShapeDtypeStruct((tile, width), jnp.bfloat16)] * (dense.shape[0] // tile),
        scratch_shapes=[pltpu.VMEM((len(pieces) * tile, width), jnp.bfloat16)],
        compiler_params=pltpu.CompilerParams(vmem_limit_bytes=limit(dense.size)),
        cost_estimate=pl.CostEstimate(flops=2 * dense.size * width, bytes_accessed=0, transcendentals=0),
    )(*pieces, weight, dense)


def backward_kernel(count, *refs):
    pieces, dense_t, outs, grads = refs[:count], refs[count], refs[count + 1 : -1], refs[-1]
    tile = pieces[0].shape[0]
    for p, piece in enumerate(pieces):
        grads[p * tile : (p + 1) * tile] = piece[...]
    for j, out in enumerate(outs):
        value = jnp.dot(dense_t[j * tile : (j + 1) * tile], grads[...], preferred_element_type=jnp.float32)
        out[...] = value.astype(out.dtype)


def backward(pieces, dense_t):
    tile, width = pieces[0].shape
    return pl.pallas_call(
        lambda *refs: backward_kernel(len(pieces), *refs),
        out_shape=[jax.ShapeDtypeStruct((tile, width), jnp.bfloat16)] * (dense_t.shape[0] // tile),
        scratch_shapes=[pltpu.VMEM((len(pieces) * tile, width), jnp.bfloat16)],
        compiler_params=pltpu.CompilerParams(vmem_limit_bytes=limit(dense_t.size)),
        cost_estimate=pl.CostEstimate(flops=2 * dense_t.size * width, bytes_accessed=0, transcendentals=0),
    )(*pieces, dense_t)


def shards(features, weight, out_bias, tile_values, tile_cols, tile_counts, cotangent):
    far = lax.axis_size("col") // 2
    near = (3, 1, 2) if far == 4 else range(1, far)
    rows = range(1, lax.axis_size("row"))
    pieces = {s: swap(features[0, 0], row=s) for s in reversed(rows)}
    dense, dense_t, feat, cot, bias = front(
        tile_cols, tile_counts, tile_values, features, cotangent, out_bias
    )
    pieces[0] = feat
    product = forward([pieces[s] for s in range(len(pieces))], weight, dense)
    half = {}
    for p in (far, 0):
        total = product[p].astype(jnp.float32)
        for s in near:
            total = total + swap(product[p ^ s], col=s).astype(jnp.float32)
        half[p] = total
    other = swap(half[far].astype(jnp.bfloat16), col=far)
    preact = half[0] + other.astype(jnp.float32) + bias
    grads = {0: (cot.astype(jnp.float32) * silu_slope(preact)[1]).astype(jnp.bfloat16)}
    grads[far] = swap(grads[0], col=far)
    preact, grads[far] = lax.optimization_barrier((preact, grads[far]))
    activated = silu_slope(preact)[0].astype(jnp.bfloat16)
    for p in (0, far):
        for s in near:
            grads[p ^ s] = swap(grads[p], col=s)
    back = backward([grads[p] for p in range(2 * far)], dense_t)
    spread = back[0].astype(jnp.float32)
    for s in reversed(rows):
        spread = spread + swap(back[s], row=s).astype(jnp.float32)
    feature_grad = jnp.dot(spread.astype(jnp.bfloat16), weight.T, preferred_element_type=jnp.float32)
    return activated[None, None], feature_grad.astype(jnp.bfloat16)[None, None]


def solution(mesh):
    in_specs = (
        P("col", "row", None, None),
        P(),
        P(),
        P("row", "col", None, None, None, None),
        P("row", "col", None, None),
        P("row", "col", None),
        P("row", "col", None, None),
    )
    out_specs = (P("row", "col", None, None), P("col", "row", None, None))
    return jax.shard_map(shards, mesh=mesh, in_specs=in_specs, out_specs=out_specs, check_vma=False)
```

time: 151 us -> 44.2 us (0.29)
  waiting for transfers between devices: 83 us -> 10.6 us
  blocking collectives: 38.7 us -> 0 us
  starting transfers between devices: 0.08 us -> 23.9 us
  between operations: 14.2 us -> 0.73 us
  other arithmetic: 7.56 us -> 0.82 us
  matrix products: 4.96 us -> 0.84 us
  Pallas kernels: 0 us -> 3.33 us
    reduce_scatter x2 -> x0, waiting for transfers between devices: 82.9 us -> none  [the longest x1 63.8 us: shards(): lax.psum_scatter(product.reshape(sub_rows * lax.axis_size('col'), width)....]
    all_gather x2 -> x0, blocking collectives: 38.7 us -> none  [the longest x1 31.5 us: shards(): grad_panel = lax.all_gather(pre_grad, 'col', axis=0, tiled=True)]
    ppermute x0 -> x20, starting transfers between devices: none -> 23.9 us  [swap(): return lax.ppermute(value, BOTH, pairs)]
    ppermute x0 -> x20, waiting for transfers between devices: none -> 10.6 us  [swap(): return lax.ppermute(value, BOTH, pairs)]
    scatter-add x3 -> x0, other arithmetic: 5.1 us -> none  [shards(): jax.ops.segment_sum(contrib, col_index[:, slot], num_segments=col_tiles)]
    dot_general x6 -> x1, matrix products: 4.96 us -> 0.84 us  [shards(): jnp.dot(spread.astype(jnp.bfloat16), weight.T, preferred_element_type=jnp...]
    pallas_call x0 -> x3, Pallas kernels: none -> 3.33 us  [the longest x1 2.25 us: front(): pl.pallas_call(front_kernel, in_specs=[HBM] * 6, out_shape=(jax.ShapeDtyp...]
    convert_element_type x3 -> x2, other arithmetic: 2.26 us -> 0.14 us  [the longest x1 0.1 us: shards(): (cot.astype(jnp.float32) * silu_slope(preact)[1]).astype(jnp.bfloat16)]
  transfers between devices with their start and end apart: 2 -> 20, of which waited for: 2 -> 9; matrix products, arithmetic and copies ran while one was open for 0% -> 2% of each run, Pallas kernels for 0% -> 5%
where the time goes in v2:
time: 44.2 us; the launch traced here: 43.7 us
  starting transfers between devices  23.9 us (54%)
  waiting for transfers between devices  10.6 us (24%)
  local copies, waits for them, and re-layouts  3.58 us (8%)
  Pallas kernels  3.33 us (8%)
  matrix products  0.84 us (2%)
  other arithmetic  0.82 us (2%)
  between operations  0.73 us (2%)
    ppermute x20, starting transfers between devices, swap(): return lax.ppermute(value, BOTH, pairs)  23.9 us
    ppermute x20, waiting for transfers between devices, swap(): return lax.ppermute(value, BOTH, pairs)  10.6 us
    unnamed x15, local copies, waits for them, and re-layouts  3.58 us
    pallas_call x1, Pallas kernels, front(): pl.pallas_call(front_kernel, in_specs=[HBM] * 6, out_shape=(jax.ShapeDtyp...  2.25 us
  transfers between devices with their start and end apart: 20, of which 9 were waited for; matrix products, arithmetic and copies ran while one was open for 2% of the time, Pallas kernels for 5%

profile of v2, /device:TPU:0, one launch (start us, length us, event | category | flops | bytes accessed | tf_op | source)
XLA Modules:
  0.0 43.7 jit_solution(2954536219438607645)
XLA Ops:
  0.6 0.0 copy-start.6
  0.6 2.4 %collective-permute-start.2 = (bf16[128,256]{1,0:T(8,128)(2,1)}, bf16[128,256]{1,0:T(8,128)(2,1)S(1)}, u32[]{:S(2)}, u32[]{:S(2)}) collective-permute-start(bf16[128,256]{1,0:T(8,128)(2,1)} %bitcast.8), channel_id=1, source_target_pairs={{0,24},{1,25},{2,26},{3,27},{4,28},{5,29},{6,30},{7,31},{8,16},{9,... | collective-permute-start | bytes 196616 | tf_op jit(solution)/shard_map/ppermute | solution.py:20
  3.1 0.6 %collective-permute-start.1 = (bf16[128,256]{1,0:T(8,128)(2,1)}, bf16[128,256]{1,0:T(8,128)(2,1)S(1)}, u32[]{:S(2)}, u32[]{:S(2)}) collective-permute-start(bf16[128,256]{1,0:T(8,128)(2,1)} %bitcast.9), channel_id=1, source_target_pairs={{0,16},{1,17},{2,18},{3,19},{4,20},{5,21},{6,22},{7,23},{8,24},{9,... | collective-permute-start | bytes 196616 | tf_op jit(solution)/shard_map/ppermute | solution.py:20
  3.7 0.0 collective-permute-start
  3.8 0.0 copy-done.6
  3.8 0.1 copy.9.cols_hbm
  3.8 0.0 copy-start.4
  3.8 0.0 copy-start.5
  3.9 0.7 %copy-done.4 = f32[256]{0:T(256)S(1)} copy-done((f32[256]{0:T(256)S(1)}, f32[256]{0:T(256)}, u32[]{:S(2)}) %copy-start.4) | copy-done | bytes 1048
  4.5 0.0 copy-done.5
  4.5 0.0 copy-start
  4.5 1.1 %copy-done = bf16[1,1,8,3,128,128]{5,4,3,2,1,0:T(8,128)(2,1)S(1)} copy-done((bf16[1,1,8,3,128,128]{5,4,3,2,1,0:T(8,128)(2,1)S(1)}, bf16[1,1,8,3,128,128]{5,4,3,2,1,0:T(8,128)(2,1)}, u32[]{:S(2)}) %copy-start) | copy-done | bytes 786456
  5.7 0.0 copy-start.2
  5.7 0.8 %copy-done.2 = bf16[1,1,128,256]{3,2,1,0:T(8,128)(2,1)S(1)} copy-done((bf16[1,1,128,256]{3,2,1,0:T(8,128)(2,1)S(1)}, bf16[1,1,128,256]{3,2,1,0:T(8,128)(2,1)}, u32[]{:S(2)}) %copy-start.2) | copy-done | bytes 65560
  6.5 0.0 copy-start.3
  6.5 0.8 %copy-done.3 = bf16[1,1,128,256]{3,2,1,0:T(8,128)(2,1)S(1)} copy-done((bf16[1,1,128,256]{3,2,1,0:T(8,128)(2,1)S(1)}, bf16[1,1,128,256]{3,2,1,0:T(8,128)(2,1)}, u32[]{:S(2)}) %copy-start.3) | copy-done | bytes 65560
  7.3 0.0 copy-start.1
  7.3 2.3 %shard_map.86 = (bf16[1024,512]{1,0:T(8,128)(2,1)S(1)}, bf16[512,1024]{1,0:T(8,128)(2,1)S(1)}, bf16[128,256]{1,0:T(8,128)(2,1)S(1)}, bf16[128,256]{1,0:T(8,128)(2,1)S(1)}, f32[1,256]{1,0:T(1,128)S(1)}) custom-call(s32[1,1,8,3]{3,2,1,0:T(8,128)S(1)} %copy.9.cols_hbm, s32[1,1,8]{2,1,0:T(1,128)S(1)} %copy-done.5, bf16[1,1,8,3,128,128]{5,4,3,2,1,0:T(8,128)(2,1)S(1)} %copy-done, ...), custom_call_target="tpu_custom_call" | custom-call | bytes 786432 | tf_op jit(solution)/shard_map/pallas_call | solution.py:73
  9.6 0.0 collective-permute-done.2.refs_3_
  9.6 0.0 collective-permute-done.1.refs_2_
  9.6 0.0 collective-permute-done.refs_1_
  9.6 0.0 copy-done.1
  9.6 0.6 %shard_map.87 = (bf16[128,256]{1,0:T(8,128)(2,1)S(1)}, bf16[128,256]{1,0:T(8,128)(2,1)S(1)}, bf16[128,256]{1,0:T(8,128)(2,1)S(1)}, bf16[128,256]{1,0:T(8,128)(2,...) custom-call(bf16[128,256]{1,0:T(8,128)(2,1)S(1)} %get-tuple-element., ...), custom_call_target="tpu_custom_call" | custom-call | flops 268435456 | tf_op jit(solution)/shard_map/pallas_call | solution.py:107
  10.3 2.7 %collective-permute-start.6 = (bf16[128,256]{1,0:T(8,128)(2,1)S(1)}, bf16[128,256]{1,0:T(8,128)(2,1)S(1)}, u32[]{:S(2)}, u32[]{:S(2)}) collective-permute-start(bf16[128,256]{1,0:T(8,128)(2,1)S(1)} %get-tuple-element.28), channel_id=1, source_target_pairs={{0,3},{1,2},{2,1},{3,0},{4,7},{5,6},{6,5},{7,4},{8,11},{9,10},{10,... | collective-permute-start | bytes 196616 | tf_op jit(solution)/shard_map/ppermute | solution.py:20
  13.0 0.8 %collective-permute-start.7 = (bf16[128,256]{1,0:T(8,128)(2,1)S(1)}, bf16[128,256]{1,0:T(8,128)(2,1)S(1)}, u32[]{:S(2)}, u32[]{:S(2)}) collective-permute-start(bf16[128,256]{1,0:T(8,128)(2,1)S(1)} %get-tuple-element.29), channel_id=1, source_target_pairs={{0,1},{1,0},{2,3},{3,2},{4,5},{5,4},{6,7},{7,6},{8,9},{9,8},{10,11... | collective-permute-start | bytes 196616 | tf_op jit(solution)/shard_map/ppermute | solution.py:20
  13.8 0.1 collective-permute-start.8
  13.8 2.7 %collective-permute-start.3 = (bf16[128,256]{1,0:T(8,128)(2,1)S(1)}, bf16[128,256]{1,0:T(8,128)(2,1)S(1)}, u32[]{:S(2)}, u32[]{:S(2)}) collective-permute-start(bf16[128,256]{1,0:T(8,128)(2,1)S(1)} %get-tuple-element.24), channel_id=1, source_target_pairs={{0,3},{1,2},{2,1},{3,0},{4,7},{5,6},{6,5},{7,4},{8,11},{9,10},{10,... | collective-permute-start | bytes 196616 | tf_op jit(solution)/shard_map/ppermute | solution.py:20
  16.5 0.8 %collective-permute-start.4 = (bf16[128,256]{1,0:T(8,128)(2,1)S(1)}, bf16[128,256]{1,0:T(8,128)(2,1)S(1)}, u32[]{:S(2)}, u32[]{:S(2)}) collective-permute-start(bf16[128,256]{1,0:T(8,128)(2,1)S(1)} %get-tuple-element.25), channel_id=1, source_target_pairs={{0,1},{1,0},{2,3},{3,2},{4,5},{5,4},{6,7},{7,6},{8,9},{9,8},{10,11... | collective-permute-start | bytes 196616 | tf_op jit(solution)/shard_map/ppermute | solution.py:20
  17.3 0.0 collective-permute-done.6
  17.3 0.5 %collective-permute-start.5 = (bf16[128,256]{1,0:T(8,128)(2,1)S(1)}, bf16[128,256]{1,0:T(8,128)(2,1)S(1)}, u32[]{:S(2)}, u32[]{:S(2)}) collective-permute-start(bf16[128,256]{1,0:T(8,128)(2,1)S(1)} %get-tuple-element.26), channel_id=1, source_target_pairs={{0,2},{1,3},{2,0},{3,1},{4,6},{5,7},{6,4},{7,5},{8,10},{9,11},{10,... | collective-permute-start | bytes 196616 | tf_op jit(solution)/shard_map/ppermute | solution.py:20
  17.7 0.0 collective-permute-done.7
  17.8 0.6 %collective-permute-done.8 = bf16[128,256]{1,0:T(8,128)(2,1)S(1)} collective-permute-done((bf16[128,256]{1,0:T(8,128)(2,1)S(1)}, bf16[128,256]{1,0:T(8,128)(2,1)S(1)}, u32[]{:S(2)}, u32[]{:S(2)}) %collective-permute-start.8) | collective-permute-done | bytes 65568 | tf_op jit(solution)/shard_map/ppermute | solution.py:20
  18.4 2.5 %collective-permute-start.9 = (bf16[128,256]{1,0:T(8,128)(2,1)S(1)}, bf16[128,256]{1,0:T(8,128)(2,1)S(1)}, u32[]{:S(2)}, u32[]{:S(2)}) collective-permute-start(bf16[128,256]{1,0:T(8,128)(2,1)S(1)} %add_convert_fusion.1), channel_id=1, source_target_pairs={{0,4},{1,5},{2,6},{3,7},{4,0},{5,1},{6,2},{7,3},{8,12},{9,13},{10,... | collective-permute-start | bytes 196616 | tf_op jit(solution)/shard_map/ppermute | solution.py:20
  21.0 0.0 collective-permute-done.3
  21.0 0.0 collective-permute-done.4
  21.0 0.8 %collective-permute-done.5 = bf16[128,256]{1,0:T(8,128)(2,1)S(1)} collective-permute-done((bf16[128,256]{1,0:T(8,128)(2,1)S(1)}, bf16[128,256]{1,0:T(8,128)(2,1)S(1)}, u32[]{:S(2)}, u32[]{:S(2)}) %collective-permute-start.5) | collective-permute-done | bytes 65568 | tf_op jit(solution)/shard_map/ppermute | solution.py:20
  21.8 2.6 %collective-permute-done.9 = bf16[128,256]{1,0:T(8,128)(2,1)S(1)} collective-permute-done((bf16[128,256]{1,0:T(8,128)(2,1)S(1)}, bf16[128,256]{1,0:T(8,128)(2,1)S(1)}, u32[]{:S(2)}, u32[]{:S(2)}) %collective-permute-start.9) | collective-permute-done | bytes 65568 | tf_op jit(solution)/shard_map/ppermute | solution.py:20
  24.4 0.1 multiply_convert_fusion.1
  24.5 1.8 %collective-permute-start.10 = (bf16[128,256]{1,0:T(8,128)(2,1)S(1)}, bf16[128,256]{1,0:T(8,128)(2,1)S(1)}, u32[]{:S(2)}, u32[]{:S(2)}) collective-permute-start(bf16[128,256]{1,0:T(8,128)(2,1)S(1)} %get-tuple-element.40.refs_0_), channel_id=1, source_target_pairs={{0,4},{1,5},{2,6},{3,7},{4,0},{5,1},{6,2},{7,3},{8,12},{9,13},{10,... | collective-permute-start | bytes 196616 | tf_op jit(solution)/shard_map/ppermute | solution.py:20
  26.3 2.4 %collective-permute-start.13 = (bf16[128,256]{1,0:T(8,128)(2,1)S(1)}, bf16[128,256]{1,0:T(8,128)(2,1)S(1)}, u32[]{:S(2)}, u32[]{:S(2)}) collective-permute-start(bf16[128,256]{1,0:T(8,128)(2,1)S(1)} %get-tuple-element.40.refs_0_), channel_id=1, source_target_pairs={{0,3},{1,2},{2,1},{3,0},{4,7},{5,6},{6,5},{7,4},{8,11},{9,10},{10,... | collective-permute-start | bytes 196616 | tf_op jit(solution)/shard_map/ppermute | solution.py:20
  28.7 0.2 collective-permute-start.12
  29.0 0.8 %collective-permute-start.11 = (bf16[128,256]{1,0:T(8,128)(2,1)S(1)}, bf16[128,256]{1,0:T(8,128)(2,1)S(1)}, u32[]{:S(2)}, u32[]{:S(2)}) collective-permute-start(bf16[128,256]{1,0:T(8,128)(2,1)S(1)} %get-tuple-element.40.refs_0_), channel_id=1, source_target_pairs={{0,1},{1,0},{2,3},{3,2},{4,5},{5,4},{6,7},{7,6},{8,9},{9,8},{10,11... | collective-permute-start | bytes 196616 | tf_op jit(solution)/shard_map/ppermute | solution.py:20
  29.8 0.5 %collective-permute-done.10.refs_4_ = bf16[128,256]{1,0:T(8,128)(2,1)S(1)} collective-permute-done((bf16[128,256]{1,0:T(8,128)(2,1)S(1)}, bf16[128,256]{1,0:T(8,128)(2,1)S(1)}, u32[]{:S(2)}, u32[]{:S(2)}) %collective-permute-start.10) | collective-permute-done | bytes 65568 | tf_op jit(solution)/shard_map/ppermute | solution.py:20
  30.3 2.0 %collective-permute-start.16 = (bf16[128,256]{1,0:T(8,128)(2,1)S(1)}, bf16[128,256]{1,0:T(8,128)(2,1)S(1)}, u32[]{:S(2)}, u32[]{:S(2)}) collective-permute-start(bf16[128,256]{1,0:T(8,128)(2,1)S(1)} %collective-permute-done.10.refs_4_), channel_id=1, source_target_pairs={{0,3},{1,2},{2,1},{3,0},{4,7},{5,6},{6,5},{7,4},{8,11},{9,10},{10,... | collective-permute-start | bytes 196616 | tf_op jit(solution)/shard_map/ppermute | solution.py:20
  32.2 0.2 collective-permute-start.15
  32.5 0.0 collective-permute-done.13.refs_3_
  32.5 1.3 %collective-permute-start.14 = (bf16[128,256]{1,0:T(8,128)(2,1)S(1)}, bf16[128,256]{1,0:T(8,128)(2,1)S(1)}, u32[]{:S(2)}, u32[]{:S(2)}) collective-permute-start(bf16[128,256]{1,0:T(8,128)(2,1)S(1)} %collective-permute-done.10.refs_4_), channel_id=1, source_target_pairs={{0,1},{1,0},{2,3},{3,2},{4,5},{5,4},{6,7},{7,6},{8,9},{9,8},{10,11... | collective-permute-start | bytes 196616 | tf_op jit(solution)/shard_map/ppermute | solution.py:20
  33.8 0.0 collective-permute-done.12.refs_2_
  33.8 0.0 collective-permute-done.11.refs_1_
  33.8 1.7 %collective-permute-done.16.refs_7_ = bf16[128,256]{1,0:T(8,128)(2,1)S(1)} collective-permute-done((bf16[128,256]{1,0:T(8,128)(2,1)S(1)}, bf16[128,256]{1,0:T(8,128)(2,1)S(1)}, u32[]{:S(2)}, u32[]{:S(2)}) %collective-permute-start.16) | collective-permute-done | bytes 65568 | tf_op jit(solution)/shard_map/ppermute | solution.py:20
  35.4 1.1 %collective-permute-done.15.refs_6_ = bf16[128,256]{1,0:T(8,128)(2,1)S(1)} collective-permute-done((bf16[128,256]{1,0:T(8,128)(2,1)S(1)}, bf16[128,256]{1,0:T(8,128)(2,1)S(1)}, u32[]{:S(2)}, u32[]{:S(2)}) %collective-permute-start.15) | collective-permute-done | bytes 65568 | tf_op jit(solution)/shard_map/ppermute | solution.py:20
  36.5 0.2 collective-permute-done.14.refs_5_
  36.7 0.5 %shard_map.88 = (bf16[128,256]{1,0:T(8,128)(2,1)S(1)}, bf16[128,256]{1,0:T(8,128)(2,1)S(1)}, bf16[128,256]{1,0:T(8,128)(2,1)S(1)}, bf16[128,256]{1,0:T(8,128)(2,1)S(1)}) custom-call(bf16[128,256]{1,0:T(8,128)(2,1)S(1)} %get-tuple-element.40.refs_0_, bf16[128,256]{1,0:T(8,128)(2,1)S(1)} %collective-permute-done.11.refs_1_, ...), custom_call_target="tpu_custom_call" | custom-call | flops 268435456 | tf_op jit(solution)/shard_map/pallas_call | solution.py:128
  37.2 0.1 collective-permute-start.17
  37.3 1.4 %collective-permute-start.18 = (bf16[128,256]{1,0:T(8,128)(2,1)S(1)}, bf16[128,256]{1,0:T(8,128)(2,1)S(1)}, u32[]{:S(2)}, u32[]{:S(2)}) collective-permute-start(bf16[128,256]{1,0:T(8,128)(2,1)S(1)} %get-tuple-element.38), channel_id=1, source_target_pairs={{0,16},{1,17},{2,18},{3,19},{4,20},{5,21},{6,22},{7,23},{8,24},{9,... | collective-permute-start | bytes 196616 | tf_op jit(solution)/shard_map/ppermute | solution.py:20
  38.7 0.4 collective-permute-start.19
  39.1 0.7 %fusion.1 = bf16[1,1,128,256]{3,2,1,0:T(8,128)(2,1)} fusion(f32[128,256]{1,0:T(8,128)S(1)} %get-tuple-element.33), kind=kLoop, calls=%fused_computation.7 | loop fusion | flops 163840 | bytes 196608 | tf_op jit(solution)/shard_map/broadcast_in_dim | solution.py:167
  39.8 1.9 %collective-permute-done.17 = bf16[128,256]{1,0:T(8,128)(2,1)S(1)} collective-permute-done((bf16[128,256]{1,0:T(8,128)(2,1)S(1)}, bf16[128,256]{1,0:T(8,128)(2,1)S(1)}, u32[]{:S(2)}, u32[]{:S(2)}) %collective-permute-start.17) | collective-permute-done | bytes 65568 | tf_op jit(solution)/shard_map/ppermute | solution.py:20
  41.6 1.3 %collective-permute-done.18 = bf16[128,256]{1,0:T(8,128)(2,1)S(1)} collective-permute-done((bf16[128,256]{1,0:T(8,128)(2,1)S(1)}, bf16[128,256]{1,0:T(8,128)(2,1)S(1)}, u32[]{:S(2)}, u32[]{:S(2)}) %collective-permute-start.18) | collective-permute-done | bytes 65568 | tf_op jit(solution)/shard_map/ppermute | solution.py:20
  42.9 0.0 collective-permute-done.19
  42.9 0.8 %fusion = bf16[1,1,128,256]{3,2,1,0:T(8,128)(2,1)} fusion(bf16[256,256]{1,0:T(8,128)(2,1)S(1)} %copy-done.1, bf16[128,256]{1,0:T(8,128)(2,1)S(1)} %collective-permute-done.19, bf16[128,256]{1,0:T(8,128)(2,1)S(1)} %collective-permute-done.18, bf16[128,256]{1,0:T(8,128)(2,1)S(1)} %collective-permute-done.17, bf16[128,256]{1,0:T(8,128)(2,1)S(1)} %get-tuple-element.36), kind=kOutput, calls=%fused_computation.1 | convolution fusion | flops 17072128 | bytes 458752 | tf_op jit(solution)/shard_map/dot_general | solution.py:166
  (1 shorter events, 0.0 us)
Async XLA Ops:
  0.6 3.1 %copy-start.6 = (s32[1,1,8,3]{2,1,3,0:T(1,128)S(1)}, s32[1,1,8,3]{2,1,3,0:T(1,128)}, u32[]{:S(2)}) copy-start(s32[1,1,8,3]{2,1,3,0:T(1,128)} %param.11) | copy-start | bytes 292
  0.6 9.0 %collective-permute-start.2 = (bf16[128,256]{1,0:T(8,128)(2,1)}, bf16[128,256]{1,0:T(8,128)(2,1)S(1)}, u32[]{:S(2)}, u32[]{:S(2)}) collective-permute-start(bf16[128,256]{1,0:T(8,128)(2,1)} %bitcast.8), channel_id=1, source_target_pairs={{0,24},{1,25},{2,26},{3,27},{4,28},{5,29},{6,30},{7,31},{8,16},{9,... | collective-permute-start | bytes 196616 | tf_op jit(solution)/shard_map/ppermute | solution.py:20
  3.1 6.5 %collective-permute-start.1 = (bf16[128,256]{1,0:T(8,128)(2,1)}, bf16[128,256]{1,0:T(8,128)(2,1)S(1)}, u32[]{:S(2)}, u32[]{:S(2)}) collective-permute-start(bf16[128,256]{1,0:T(8,128)(2,1)} %bitcast.9), channel_id=1, source_target_pairs={{0,16},{1,17},{2,18},{3,19},{4,20},{5,21},{6,22},{7,23},{8,24},{9,... | collective-permute-start | bytes 196616 | tf_op jit(solution)/shard_map/ppermute | solution.py:20
  3.7 5.9 %collective-permute-start = (bf16[128,256]{1,0:T(8,128)(2,1)}, bf16[128,256]{1,0:T(8,128)(2,1)S(1)}, u32[]{:S(2)}, u32[]{:S(2)}) collective-permute-start(bf16[128,256]{1,0:T(8,128)(2,1)} %bitcast.10), channel_id=1, source_target_pairs={{0,8},{1,9},{2,10},{3,11},{4,12},{5,13},{6,14},{7,15},{8,0},{9,1},... | collective-permute-start | bytes 196616 | tf_op jit(solution)/shard_map/ppermute | solution.py:20
  3.8 0.7 %copy-start.4 = (f32[256]{0:T(256)S(1)}, f32[256]{0:T(256)}, u32[]{:S(2)}) copy-start(f32[256]{0:T(256)} %param.9) | copy-start | bytes 3076
  3.8 0.7 %copy-start.5 = (s32[1,1,8]{2,1,0:T(1,128)S(1)}, s32[1,1,8]{2,1,0:T(1,128)}, u32[]{:S(2)}) copy-start(s32[1,1,8]{2,1,0:T(1,128)} %counts_hbm.1) | copy-start | bytes 100
  4.5 1.1 %copy-start = (bf16[1,1,8,3,128,128]{5,4,3,2,1,0:T(8,128)(2,1)S(1)}, bf16[1,1,8,3,128,128]{5,4,3,2,1,0:T(8,128)(2,1)}, u32[]{:S(2)}) copy-start(bf16[1,1,8,3,128,128]{5,4,3,2,1,0:T(8,128)(2,1)} %tiles_hbm.1) | copy-start | bytes 2359300
  5.7 0.8 %copy-start.2 = (bf16[1,1,128,256]{3,2,1,0:T(8,128)(2,1)S(1)}, bf16[1,1,128,256]{3,2,1,0:T(8,128)(2,1)}, u32[]{:S(2)}) copy-start(bf16[1,1,128,256]{3,2,1,0:T(8,128)(2,1)} %cot_hbm.1) | copy-start | bytes 196612
  6.5 0.8 %copy-start.3 = (bf16[1,1,128,256]{3,2,1,0:T(8,128)(2,1)S(1)}, bf16[1,1,128,256]{3,2,1,0:T(8,128)(2,1)}, u32[]{:S(2)}) copy-start(bf16[1,1,128,256]{3,2,1,0:T(8,128)(2,1)} %feat_hbm.1) | copy-start | bytes 196612
  7.3 2.3 %copy-start.1 = (bf16[256,256]{1,0:T(8,128)(2,1)S(1)}, bf16[256,256]{1,0:T(8,128)(2,1)}, u32[]{:S(2)}) copy-start(bf16[256,256]{1,0:T(8,128)(2,1)} %refs_4_.1) | copy-start | bytes 393220
  10.3 7.0 %collective-permute-start.6 = (bf16[128,256]{1,0:T(8,128)(2,1)S(1)}, bf16[128,256]{1,0:T(8,128)(2,1)S(1)}, u32[]{:S(2)}, u32[]{:S(2)}) collective-permute-start(bf16[128,256]{1,0:T(8,128)(2,1)S(1)} %get-tuple-element.28), channel_id=1, source_target_pairs={{0,3},{1,2},{2,1},{3,0},{4,7},{5,6},{6,5},{7,4},{8,11},{9,10},{10,... | collective-permute-start | bytes 196616 | tf_op jit(solution)/shard_map/ppermute | solution.py:20
  13.0 4.7 %collective-permute-start.7 = (bf16[128,256]{1,0:T(8,128)(2,1)S(1)}, bf16[128,256]{1,0:T(8,128)(2,1)S(1)}, u32[]{:S(2)}, u32[]{:S(2)}) collective-permute-start(bf16[128,256]{1,0:T(8,128)(2,1)S(1)} %get-tuple-element.29), channel_id=1, source_target_pairs={{0,1},{1,0},{2,3},{3,2},{4,5},{5,4},{6,7},{7,6},{8,9},{9,8},{10,11... | collective-permute-start | bytes 196616 | tf_op jit(solution)/shard_map/ppermute | solution.py:20
  13.8 4.6 %collective-permute-start.8 = (bf16[128,256]{1,0:T(8,128)(2,1)S(1)}, bf16[128,256]{1,0:T(8,128)(2,1)S(1)}, u32[]{:S(2)}, u32[]{:S(2)}) collective-permute-start(bf16[128,256]{1,0:T(8,128)(2,1)S(1)} %get-tuple-element.30), channel_id=1, source_target_pairs={{0,2},{1,3},{2,0},{3,1},{4,6},{5,7},{6,4},{7,5},{8,10},{9,11},{10,... | collective-permute-start | bytes 196616 | tf_op jit(solution)/shard_map/ppermute | solution.py:20
  13.8 7.2 %collective-permute-start.3 = (bf16[128,256]{1,0:T(8,128)(2,1)S(1)}, bf16[128,256]{1,0:T(8,128)(2,1)S(1)}, u32[]{:S(2)}, u32[]{:S(2)}) collective-permute-start(bf16[128,256]{1,0:T(8,128)(2,1)S(1)} %get-tuple-element.24), channel_id=1, source_target_pairs={{0,3},{1,2},{2,1},{3,0},{4,7},{5,6},{6,5},{7,4},{8,11},{9,10},{10,... | collective-permute-start | bytes 196616 | tf_op jit(solution)/shard_map/ppermute | solution.py:20
  16.5 4.5 %collective-permute-start.4 = (bf16[128,256]{1,0:T(8,128)(2,1)S(1)}, bf16[128,256]{1,0:T(8,128)(2,1)S(1)}, u32[]{:S(2)}, u32[]{:S(2)}) collective-permute-start(bf16[128,256]{1,0:T(8,128)(2,1)S(1)} %get-tuple-element.25), channel_id=1, source_target_pairs={{0,1},{1,0},{2,3},{3,2},{4,5},{5,4},{6,7},{7,6},{8,9},{9,8},{10,11... | collective-permute-start | bytes 196616 | tf_op jit(solution)/shard_map/ppermute | solution.py:20
  17.3 4.5 %collective-permute-start.5 = (bf16[128,256]{1,0:T(8,128)(2,1)S(1)}, bf16[128,256]{1,0:T(8,128)(2,1)S(1)}, u32[]{:S(2)}, u32[]{:S(2)}) collective-permute-start(bf16[128,256]{1,0:T(8,128)(2,1)S(1)} %get-tuple-element.26), channel_id=1, source_target_pairs={{0,2},{1,3},{2,0},{3,1},{4,6},{5,7},{6,4},{7,5},{8,10},{9,11},{10,... | collective-permute-start | bytes 196616 | tf_op jit(solution)/shard_map/ppermute | solution.py:20
  18.4 5.9 %collective-permute-start.9 = (bf16[128,256]{1,0:T(8,128)(2,1)S(1)}, bf16[128,256]{1,0:T(8,128)(2,1)S(1)}, u32[]{:S(2)}, u32[]{:S(2)}) collective-permute-start(bf16[128,256]{1,0:T(8,128)(2,1)S(1)} %add_convert_fusion.1), channel_id=1, source_target_pairs={{0,4},{1,5},{2,6},{3,7},{4,0},{5,1},{6,2},{7,3},{8,12},{9,13},{10,... | collective-permute-start | bytes 196616 | tf_op jit(solution)/shard_map/ppermute | solution.py:20
  24.5 5.8 %collective-permute-start.10 = (bf16[128,256]{1,0:T(8,128)(2,1)S(1)}, bf16[128,256]{1,0:T(8,128)(2,1)S(1)}, u32[]{:S(2)}, u32[]{:S(2)}) collective-permute-start(bf16[128,256]{1,0:T(8,128)(2,1)S(1)} %get-tuple-element.40.refs_0_), channel_id=1, source_target_pairs={{0,4},{1,5},{2,6},{3,7},{4,0},{5,1},{6,2},{7,3},{8,12},{9,13},{10,... | collective-permute-start | bytes 196616 | tf_op jit(solution)/shard_map/ppermute | solution.py:20
  26.3 6.1 %collective-permute-start.13 = (bf16[128,256]{1,0:T(8,128)(2,1)S(1)}, bf16[128,256]{1,0:T(8,128)(2,1)S(1)}, u32[]{:S(2)}, u32[]{:S(2)}) collective-permute-start(bf16[128,256]{1,0:T(8,128)(2,1)S(1)} %get-tuple-element.40.refs_0_), channel_id=1, source_target_pairs={{0,3},{1,2},{2,1},{3,0},{4,7},{5,6},{6,5},{7,4},{8,11},{9,10},{10,... | collective-permute-start | bytes 196616 | tf_op jit(solution)/shard_map/ppermute | solution.py:20
  28.7 5.0 %collective-permute-start.12 = (bf16[128,256]{1,0:T(8,128)(2,1)S(1)}, bf16[128,256]{1,0:T(8,128)(2,1)S(1)}, u32[]{:S(2)}, u32[]{:S(2)}) collective-permute-start(bf16[128,256]{1,0:T(8,128)(2,1)S(1)} %get-tuple-element.40.refs_0_), channel_id=1, source_target_pairs={{0,2},{1,3},{2,0},{3,1},{4,6},{5,7},{6,4},{7,5},{8,10},{9,11},{10,... | collective-permute-start | bytes 196616 | tf_op jit(solution)/shard_map/ppermute | solution.py:20
  29.0 4.8 %collective-permute-start.11 = (bf16[128,256]{1,0:T(8,128)(2,1)S(1)}, bf16[128,256]{1,0:T(8,128)(2,1)S(1)}, u32[]{:S(2)}, u32[]{:S(2)}) collective-permute-start(bf16[128,256]{1,0:T(8,128)(2,1)S(1)} %get-tuple-element.40.refs_0_), channel_id=1, source_target_pairs={{0,1},{1,0},{2,3},{3,2},{4,5},{5,4},{6,7},{7,6},{8,9},{9,8},{10,11... | collective-permute-start | bytes 196616 | tf_op jit(solution)/shard_map/ppermute | solution.py:20
  30.3 5.2 %collective-permute-start.16 = (bf16[128,256]{1,0:T(8,128)(2,1)S(1)}, bf16[128,256]{1,0:T(8,128)(2,1)S(1)}, u32[]{:S(2)}, u32[]{:S(2)}) collective-permute-start(bf16[128,256]{1,0:T(8,128)(2,1)S(1)} %collective-permute-done.10.refs_4_), channel_id=1, source_target_pairs={{0,3},{1,2},{2,1},{3,0},{4,7},{5,6},{6,5},{7,4},{8,11},{9,10},{10,... | collective-permute-start | bytes 196616 | tf_op jit(solution)/shard_map/ppermute | solution.py:20
  32.2 4.3 %collective-permute-start.15 = (bf16[128,256]{1,0:T(8,128)(2,1)S(1)}, bf16[128,256]{1,0:T(8,128)(2,1)S(1)}, u32[]{:S(2)}, u32[]{:S(2)}) collective-permute-start(bf16[128,256]{1,0:T(8,128)(2,1)S(1)} %collective-permute-done.10.refs_4_), channel_id=1, source_target_pairs={{0,2},{1,3},{2,0},{3,1},{4,6},{5,7},{6,4},{7,5},{8,10},{9,11},{10,... | collective-permute-start | bytes 196616 | tf_op jit(solution)/shard_map/ppermute | solution.py:20
  32.5 4.3 %collective-permute-start.14 = (bf16[128,256]{1,0:T(8,128)(2,1)S(1)}, bf16[128,256]{1,0:T(8,128)(2,1)S(1)}, u32[]{:S(2)}, u32[]{:S(2)}) collective-permute-start(bf16[128,256]{1,0:T(8,128)(2,1)S(1)} %collective-permute-done.10.refs_4_), channel_id=1, source_target_pairs={{0,1},{1,0},{2,3},{3,2},{4,5},{5,4},{6,7},{7,6},{8,9},{9,8},{10,11... | collective-permute-start | bytes 196616 | tf_op jit(solution)/shard_map/ppermute | solution.py:20
  37.2 4.5 %collective-permute-start.17 = (bf16[128,256]{1,0:T(8,128)(2,1)S(1)}, bf16[128,256]{1,0:T(8,128)(2,1)S(1)}, u32[]{:S(2)}, u32[]{:S(2)}) collective-permute-start(bf16[128,256]{1,0:T(8,128)(2,1)S(1)} %get-tuple-element.37), channel_id=1, source_target_pairs={{0,24},{1,25},{2,26},{3,27},{4,28},{5,29},{6,30},{7,31},{8,16},{9,... | collective-permute-start | bytes 196616 | tf_op jit(solution)/shard_map/ppermute | solution.py:20
  37.3 5.6 %collective-permute-start.18 = (bf16[128,256]{1,0:T(8,128)(2,1)S(1)}, bf16[128,256]{1,0:T(8,128)(2,1)S(1)}, u32[]{:S(2)}, u32[]{:S(2)}) collective-permute-start(bf16[128,256]{1,0:T(8,128)(2,1)S(1)} %get-tuple-element.38), channel_id=1, source_target_pairs={{0,16},{1,17},{2,18},{3,19},{4,20},{5,21},{6,22},{7,23},{8,24},{9,... | collective-permute-start | bytes 196616 | tf_op jit(solution)/shard_map/ppermute | solution.py:20
  38.7 4.2 %collective-permute-start.19 = (bf16[128,256]{1,0:T(8,128)(2,1)S(1)}, bf16[128,256]{1,0:T(8,128)(2,1)S(1)}, u32[]{:S(2)}, u32[]{:S(2)}) collective-permute-start(bf16[128,256]{1,0:T(8,128)(2,1)S(1)} %get-tuple-element.39), channel_id=1, source_target_pairs={{0,8},{1,9},{2,10},{3,11},{4,12},{5,13},{6,14},{7,15},{8,0},{9,1},... | collective-permute-start | bytes 196616 | tf_op jit(solution)/shard_map/ppermute | solution.py:20

commit v3 on v2

v3 whole, which is shorter than its diff:
```python
import jax
import jax.numpy as jnp
from jax import lax
from jax.experimental import pallas as pl
from jax.experimental.pallas import tpu as pltpu
from jax.sharding import PartitionSpec as P

BOTH = ("row", "col")
HBM = pl.BlockSpec(memory_space=pltpu.HBM)


def silu_slope(preact):
    sigmoid_z = jax.nn.sigmoid(preact)
    return (preact * sigmoid_z, sigmoid_z * (1.0 + preact * (1.0 - sigmoid_z)))


def swap(value, row=0, col=0):
    rows, cols = lax.axis_size("row"), lax.axis_size("col")
    pairs = [(r * cols + c, (r ^ row) * cols + (c ^ col)) for r in range(rows) for c in range(cols)]
    return lax.ppermute(value, BOTH, pairs)


def limit(count):
    return 56 * 1024 * 1024 if count * 2 > 6 * 1024 * 1024 else 8 * 1024 * 1024


def dense_kernel(cols_hbm, counts_hbm, tiles_hbm, dense, cols, counts, tiles, sems):
    row_tiles, slots, tile, _ = tiles.shape
    me_row, me_col = lax.axis_index("row"), lax.axis_index("col")
    copies = [
        pltpu.make_async_copy(cols_hbm.at[0, 0], cols, sems.at[0]),
        pltpu.make_async_copy(counts_hbm.at[0], counts, sems.at[1]),
        pltpu.make_async_copy(tiles_hbm.at[0, 0], tiles, sems.at[2]),
    ]
    for copy in copies:
        copy.start()
    dense[...] = jnp.zeros(dense.shape, dense.dtype)
    for copy in copies:
        copy.wait()

    def place(position):
        row_tile = position ^ me_col
        start = pl.multiple_of(position * tile, tile)
        for slot in range(slots):

            @pl.when(slot < counts[0, row_tile])
            def _():
                column = pl.multiple_of((cols[row_tile, slot] ^ me_row) * tile, tile)
                dense[pl.ds(start, tile), pl.ds(column, tile)] = tiles[row_tile, slot]

    if row_tiles <= 8:
        for position in range(row_tiles):
            place(position)
    else:
        pl.loop(0, row_tiles)(place)


def dense_block(tile_cols, tile_counts, tile_values):
    row_tiles, slots, tile, _ = tile_values.shape[2:]
    height, width = row_tiles * tile, lax.axis_size("row") * tile
    kind = tile_values.dtype
    return pl.pallas_call(
        dense_kernel,
        in_specs=[HBM] * 3,
        out_shape=jax.ShapeDtypeStruct((height, width), kind),
        scratch_shapes=[
            pltpu.SMEM((row_tiles, slots), jnp.int32),
            pltpu.SMEM((1, row_tiles), jnp.int32),
            pltpu.VMEM((row_tiles, slots, tile, tile), kind),
            pltpu.SemaphoreType.DMA((3,)),
        ],
        compiler_params=pltpu.CompilerParams(vmem_limit_bytes=limit(height * width)),
        cost_estimate=pl.CostEstimate(flops=0, bytes_accessed=tile_values.size * 2, transcendentals=0),
    )(tile_cols, tile_counts, tile_values)


def forward_kernel(count, *refs):
    pieces, (weight, dense), outs, projected = refs[:count], refs[count : count + 2], refs[count + 2 : -1], refs[-1]
    tile = pieces[0].shape[0]
    for j, piece in enumerate(pieces):
        value = jnp.dot(piece[...], weight[...], preferred_element_type=jnp.float32)
        projected[j * tile : (j + 1) * tile] = value.astype(projected.dtype)
    for p, out in enumerate(outs):
        value = jnp.dot(dense[p * tile : (p + 1) * tile], projected[...], preferred_element_type=jnp.float32)
        out[...] = value.astype(out.dtype)


def forward(pieces, weight, dense):
    tile, width = pieces[0].shape
    return pl.pallas_call(
        lambda *refs: forward_kernel(len(pieces), *refs),
        out_shape=[jax.ShapeDtypeStruct((tile, width), jnp.bfloat16)] * (dense.shape[0] // tile),
        scratch_shapes=[pltpu.VMEM((len(pieces) * tile, width), jnp.bfloat16)],
        compiler_params=pltpu.CompilerParams(vmem_limit_bytes=limit(dense.size)),
        cost_estimate=pl.CostEstimate(flops=2 * dense.size * width, bytes_accessed=0, transcendentals=0),
    )(*pieces, weight, dense)


def backward_kernel(count, *refs):
    pieces, dense, outs, grads = refs[:count], refs[count], refs[count + 1 : -1], refs[-1]
    tile = pieces[0].shape[0]
    for p, piece in enumerate(pieces):
        grads[p * tile : (p + 1) * tile] = piece[...]
    for j, out in enumerate(outs):
        value = lax.dot_general(
            dense[:, j * tile : (j + 1) * tile], grads[...], (((0,), (0,)), ((), ())), preferred_element_type=jnp.float32
        )
        out[...] = value.astype(out.dtype)


def backward(pieces, dense):
    tile, width = pieces[0].shape
    return pl.pallas_call(
        lambda *refs: backward_kernel(len(pieces), *refs),
        out_shape=[jax.ShapeDtypeStruct((tile, width), jnp.bfloat16)] * (dense.shape[1] // tile),
        scratch_shapes=[pltpu.VMEM((len(pieces) * tile, width), jnp.bfloat16)],
        compiler_params=pltpu.CompilerParams(vmem_limit_bytes=limit(dense.size)),
        cost_estimate=pl.CostEstimate(flops=2 * dense.size * width, bytes_accessed=0, transcendentals=0),
    )(*pieces, dense)


def shards(features, weight, out_bias, tile_values, tile_cols, tile_counts, cotangent):
    far = lax.axis_size("col") // 2
    near = {k: v if far == 4 else range(1, far) for k, v in {'far': (3, 1, 2), 'own': (3, 1, 2), 'far grad': (2, 1, 3), 'own grad': (3, 1, 2)}.items()}
    rows = range(1, lax.axis_size("row"))
    own = features[0, 0]
    even = [s for s in rows if s % 2 == 0]
    pieces = {s: swap(own, row=s) for s in even}
    pieces[0] = own
    pieces[1] = swap(own, row=1)
    dense = dense_block(tile_cols, tile_counts, tile_values)
    dense, *got = lax.optimization_barrier((dense, *(pieces[s] for s in even)))
    for s, piece in zip(even, got):
        pieces[s] = piece
        pieces[s + 1] = swap(piece, row=1)
    product = forward([pieces[s] for s in range(len(pieces))], weight, dense)
    half = {}
    for p in (far, 0):
        total = product[p].astype(jnp.float32)
        for s in near["far" if p else "own"]:
            total = total + swap(product[p ^ s], col=s).astype(jnp.float32)
        half[p] = total
    other = swap(half[far].astype(jnp.bfloat16), col=far)
    preact = half[0] + other.astype(jnp.float32) + out_bias
    grads = {0: (cotangent[0, 0].astype(jnp.float32) * silu_slope(preact)[1]).astype(jnp.bfloat16)}
    grads[far] = swap(grads[0], col=far)
    preact, grads[far] = lax.optimization_barrier((preact, grads[far]))
    activated = silu_slope(preact)[0].astype(jnp.bfloat16)
    for p in (0, far):
        for s in near["far grad" if p else "own grad"]:
            grads[p ^ s] = swap(grads[p], col=s)
    back = backward([grads[p] for p in range(2 * far)], dense)
    spread = back[0].astype(jnp.float32)
    for s in (2, 1, 3):
        spread = spread + swap(back[s], row=s).astype(jnp.float32)
    feature_grad = jnp.dot(spread.astype(jnp.bfloat16), weight.T, preferred_element_type=jnp.float32)
    return activated[None, None], feature_grad.astype(jnp.bfloat16)[None, None]


def solution(mesh):
    in_specs = (
        P("col", "row", None, None),
        P(),
        P(),
        P("row", "col", None, None, None, None),
        P("row", "col", None, None),
        P("row", "col", None),
        P("row", "col", None, None),
    )
    out_specs = (P("row", "col", None, None), P("col", "row", None, None))
    return jax.shard_map(shards, mesh=mesh, in_specs=in_specs, out_specs=out_specs, check_vma=False)
```

time: 44.2 us -> 41.7 us (0.943)
  local copies, waits for them, and re-layouts: 3.58 us -> 1.24 us
  Pallas kernels: 3.33 us -> 2.1 us
  starting transfers between devices: 23.9 us -> 24.7 us
  waiting for transfers between devices: 10.6 us -> 11.1 us
    unnamed x15, local copies, waits for them, and re-layouts: 3.58 us -> 1.24 us
    pallas_call x1, Pallas kernels: 2.25 us -> 0.99 us  [dense_block(): pl.pallas_call(dense_kernel, in_specs=[HBM] * 3, out_shape=jax.ShapeDtype...]
    ppermute x20, starting transfers between devices: 23.9 us -> 24.7 us  [swap(): return lax.ppermute(value, BOTH, pairs)]
    ppermute x20, waiting for transfers between devices: 10.6 us -> 11.1 us  [swap(): return lax.ppermute(value, BOTH, pairs)]
  transfers between devices with their start and end apart: 20 -> 20, of which waited for: 9 -> 11; matrix products, arithmetic and copies ran while one was open for 2% -> 2% of each run, Pallas kernels for 5% -> 2%
where the time goes in v3:
time: 41.7 us; the launch traced here: 41.5 us
  starting transfers between devices  24.7 us (59%)
  waiting for transfers between devices  11.1 us (27%)
  Pallas kernels  2.1 us (5%)
  local copies, waits for them, and re-layouts  1.24 us (3%)
  matrix products  0.83 us (2%)
  other arithmetic  0.81 us (2%)
  between operations  0.71 us (2%)
    ppermute x20, starting transfers between devices, swap(): return lax.ppermute(value, BOTH, pairs)  24.7 us
    ppermute x20, waiting for transfers between devices, swap(): return lax.ppermute(value, BOTH, pairs)  11.1 us
    unnamed x15, local copies, waits for them, and re-layouts  1.24 us
    pallas_call x1, Pallas kernels, dense_block(): pl.pallas_call(dense_kernel, in_specs=[HBM] * 3, out_shape=jax.ShapeDtype...  0.99 us
  transfers between devices with their start and end apart: 20, of which 11 were waited for; matrix products, arithmetic and copies ran while one was open for 2% of the time, Pallas kernels for 2%

profile of v3, /device:TPU:0, one launch (start us, length us, event | category | flops | bytes accessed | tf_op | source)
XLA Modules:
  0.0 41.5 jit_solution(10501688895058694690)
XLA Ops:
  0.6 0.0 copy-start.5
  0.6 0.0 copy-start.3
  0.6 3.0 %collective-permute-start.1 = (bf16[128,256]{1,0:T(8,128)(2,1)}, bf16[128,256]{1,0:T(8,128)(2,1)S(1)}, u32[]{:S(2)}, u32[]{:S(2)}) collective-permute-start(bf16[128,256]{1,0:T(8,128)(2,1)} %bitcast.9), channel_id=1, source_target_pairs={{0,16},{1,17},{2,18},{3,19},{4,20},{5,21},{6,22},{7,23},{8,24},{9,... | collective-permute-start | bytes 196616 | tf_op jit(solution)/shard_map/ppermute | solution.py:20
  3.7 0.0 collective-permute-start
  3.7 0.0 copy-done.5
  3.7 0.1 copy.9.cols_hbm
  3.7 0.0 copy-done.3
  3.7 0.0 copy-start
  3.7 1.1 %copy-done = bf16[1,1,8,3,128,128]{5,4,3,2,1,0:T(8,128)(2,1)S(1)} copy-done((bf16[1,1,8,3,128,128]{5,4,3,2,1,0:T(8,128)(2,1)S(1)}, bf16[1,1,8,3,128,128]{5,4,3,2,1,0:T(8,128)(2,1)}, u32[]{:S(2)}) %copy-start) | copy-done | bytes 786456
  4.9 0.0 copy-start.1
  4.9 0.0 copy-start.2
  4.9 1.0 %shard_map.86.refs_5_.refs_8_ = bf16[1024,512]{1,0:T(8,128)(2,1)S(1)} custom-call(s32[1,1,8,3]{3,2,1,0:T(8,128)S(1)} %copy.9.cols_hbm, s32[1,1,8]{2,1,0:T(1,128)S(1)} %copy-done.3, bf16[1,1,8,3,128,128]{5,4,3,2,1,0:T(8,128)(2,1)S(1)} %copy-done), custom_call_target="tpu_custom_call" | custom-call | bytes 786432 | tf_op jit(solution)/shard_map/pallas_call | solution.py:62
  5.9 0.2 collective-permute-done.1.refs_2_
  6.1 0.3 collective-permute-start.2
  6.4 0.0 collective-permute-done.refs_1_
  6.4 0.9 %collective-permute-done.2.refs_3_ = bf16[128,256]{1,0:T(8,128)(2,1)S(1)} collective-permute-done((bf16[128,256]{1,0:T(8,128)(2,1)S(1)}, bf16[128,256]{1,0:T(8,128)(2,1)S(1)}, u32[]{:S(2)}, u32[]{:S(2)}) %collective-permute-start.2) | collective-permute-done | bytes 65568 | tf_op jit(solution)/shard_map/ppermute | solution.py:20
  7.4 0.0 copy-done.1
  7.4 0.0 copy-done.2
  7.4 0.6 %shard_map.87 = (bf16[128,256]{1,0:T(8,128)(2,1)S(1)}, bf16[128,256]{1,0:T(8,128)(2,1)S(1)}, bf16[128,256]{1,0:T(8,128)(2,1)S(1)}, bf16[128,256]{1,0:T(8,128)(2,...) custom-call(bf16[128,256]{1,0:T(8,128)(2,1)S(1)} %bitcast.11, ...), custom_call_target="tpu_custom_call" | custom-call | flops 268435456 | tf_op jit(solution)/shard_map/pallas_call | solution.py:90
  8.0 3.1 %collective-permute-start.6 = (bf16[128,256]{1,0:T(8,128)(2,1)S(1)}, bf16[128,256]{1,0:T(8,128)(2,1)S(1)}, u32[]{:S(2)}, u32[]{:S(2)}) collective-permute-start(bf16[128,256]{1,0:T(8,128)(2,1)S(1)} %get-tuple-element.25), channel_id=1, source_target_pairs={{0,3},{1,2},{2,1},{3,0},{4,7},{5,6},{6,5},{7,4},{8,11},{9,10},{10,... | collective-permute-start | bytes 196616 | tf_op jit(solution)/shard_map/ppermute | solution.py:20
  11.1 0.5 %collective-permute-start.7 = (bf16[128,256]{1,0:T(8,128)(2,1)S(1)}, bf16[128,256]{1,0:T(8,128)(2,1)S(1)}, u32[]{:S(2)}, u32[]{:S(2)}) collective-permute-start(bf16[128,256]{1,0:T(8,128)(2,1)S(1)} %get-tuple-element.26), channel_id=1, source_target_pairs={{0,1},{1,0},{2,3},{3,2},{4,5},{5,4},{6,7},{7,6},{8,9},{9,8},{10,11... | collective-permute-start | bytes 196616 | tf_op jit(solution)/shard_map/ppermute | solution.py:20
  11.7 0.1 collective-permute-start.8
  11.8 2.8 %collective-permute-start.3 = (bf16[128,256]{1,0:T(8,128)(2,1)S(1)}, bf16[128,256]{1,0:T(8,128)(2,1)S(1)}, u32[]{:S(2)}, u32[]{:S(2)}) collective-permute-start(bf16[128,256]{1,0:T(8,128)(2,1)S(1)} %get-tuple-element.21), channel_id=1, source_target_pairs={{0,3},{1,2},{2,1},{3,0},{4,7},{5,6},{6,5},{7,4},{8,11},{9,10},{10,... | collective-permute-start | bytes 196616 | tf_op jit(solution)/shard_map/ppermute | solution.py:20
  14.6 0.5 %collective-permute-start.4 = (bf16[128,256]{1,0:T(8,128)(2,1)S(1)}, bf16[128,256]{1,0:T(8,128)(2,1)S(1)}, u32[]{:S(2)}, u32[]{:S(2)}) collective-permute-start(bf16[128,256]{1,0:T(8,128)(2,1)S(1)} %get-tuple-element.22), channel_id=1, source_target_pairs={{0,1},{1,0},{2,3},{3,2},{4,5},{5,4},{6,7},{7,6},{8,9},{9,8},{10,11... | collective-permute-start | bytes 196616 | tf_op jit(solution)/shard_map/ppermute | solution.py:20
  15.1 0.0 collective-permute-done.6
  15.1 0.4 collective-permute-start.5
  15.5 0.0 collective-permute-done.7
  15.5 0.8 %collective-permute-done.8 = bf16[128,256]{1,0:T(8,128)(2,1)S(1)} collective-permute-done((bf16[128,256]{1,0:T(8,128)(2,1)S(1)}, bf16[128,256]{1,0:T(8,128)(2,1)S(1)}, u32[]{:S(2)}, u32[]{:S(2)}) %collective-permute-start.8) | collective-permute-done | bytes 65568 | tf_op jit(solution)/shard_map/ppermute | solution.py:20
  16.4 0.0 copy-start.4
  16.4 0.0 copy-start.6
  16.4 2.7 %collective-permute-start.9 = (bf16[128,256]{1,0:T(8,128)(2,1)S(1)}, bf16[128,256]{1,0:T(8,128)(2,1)S(1)}, u32[]{:S(2)}, u32[]{:S(2)}) collective-permute-start(bf16[128,256]{1,0:T(8,128)(2,1)S(1)} %add_convert_fusion.1), channel_id=1, source_target_pairs={{0,4},{1,5},{2,6},{3,7},{4,0},{5,1},{6,2},{7,3},{8,12},{9,13},{10,... | collective-permute-start | bytes 196616 | tf_op jit(solution)/shard_map/ppermute | solution.py:20
  19.1 0.0 collective-permute-done.3
  19.1 0.0 collective-permute-done.4
  19.1 0.3 collective-permute-done.5
  19.4 3.0 %collective-permute-done.9 = bf16[128,256]{1,0:T(8,128)(2,1)S(1)} collective-permute-done((bf16[128,256]{1,0:T(8,128)(2,1)S(1)}, bf16[128,256]{1,0:T(8,128)(2,1)S(1)}, u32[]{:S(2)}, u32[]{:S(2)}) %collective-permute-start.9) | collective-permute-done | bytes 65568 | tf_op jit(solution)/shard_map/ppermute | solution.py:20
  22.4 0.0 copy-done.4
  22.4 0.0 copy-done.6
  22.4 0.1 fusion.1
  22.5 2.0 %collective-permute-start.10 = (bf16[128,256]{1,0:T(8,128)(2,1)S(1)}, bf16[128,256]{1,0:T(8,128)(2,1)S(1)}, u32[]{:S(2)}, u32[]{:S(2)}) collective-permute-start(bf16[128,256]{1,0:T(8,128)(2,1)S(1)} %get-tuple-element.34.refs_0_), channel_id=1, source_target_pairs={{0,4},{1,5},{2,6},{3,7},{4,0},{5,1},{6,2},{7,3},{8,12},{9,13},{10,... | collective-permute-start | bytes 196616 | tf_op jit(solution)/shard_map/ppermute | solution.py:20
  24.5 2.4 %collective-permute-start.13 = (bf16[128,256]{1,0:T(8,128)(2,1)S(1)}, bf16[128,256]{1,0:T(8,128)(2,1)S(1)}, u32[]{:S(2)}, u32[]{:S(2)}) collective-permute-start(bf16[128,256]{1,0:T(8,128)(2,1)S(1)} %get-tuple-element.34.refs_0_), channel_id=1, source_target_pairs={{0,3},{1,2},{2,1},{3,0},{4,7},{5,6},{6,5},{7,4},{8,11},{9,10},{10,... | collective-permute-start | bytes 196616 | tf_op jit(solution)/shard_map/ppermute | solution.py:20
  26.9 0.2 collective-permute-start.12
  27.1 0.9 %collective-permute-start.11 = (bf16[128,256]{1,0:T(8,128)(2,1)S(1)}, bf16[128,256]{1,0:T(8,128)(2,1)S(1)}, u32[]{:S(2)}, u32[]{:S(2)}) collective-permute-start(bf16[128,256]{1,0:T(8,128)(2,1)S(1)} %get-tuple-element.34.refs_0_), channel_id=1, source_target_pairs={{0,1},{1,0},{2,3},{3,2},{4,5},{5,4},{6,7},{7,6},{8,9},{9,8},{10,11... | collective-permute-start | bytes 196616 | tf_op jit(solution)/shard_map/ppermute | solution.py:20
  28.0 0.4 collective-permute-done.10.refs_4_
  28.3 2.1 %collective-permute-start.16 = (bf16[128,256]{1,0:T(8,128)(2,1)S(1)}, bf16[128,256]{1,0:T(8,128)(2,1)S(1)}, u32[]{:S(2)}, u32[]{:S(2)}) collective-permute-start(bf16[128,256]{1,0:T(8,128)(2,1)S(1)} %collective-permute-done.10.refs_4_), channel_id=1, source_target_pairs={{0,3},{1,2},{2,1},{3,0},{4,7},{5,6},{6,5},{7,4},{8,11},{9,10},{10,... | collective-permute-start | bytes 196616 | tf_op jit(solution)/shard_map/ppermute | solution.py:20
  30.4 0.2 collective-permute-start.15
  30.6 0.0 collective-permute-done.13.refs_3_
  30.6 1.2 %collective-permute-start.14 = (bf16[128,256]{1,0:T(8,128)(2,1)S(1)}, bf16[128,256]{1,0:T(8,128)(2,1)S(1)}, u32[]{:S(2)}, u32[]{:S(2)}) collective-permute-start(bf16[128,256]{1,0:T(8,128)(2,1)S(1)} %collective-permute-done.10.refs_4_), channel_id=1, source_target_pairs={{0,1},{1,0},{2,3},{3,2},{4,5},{5,4},{6,7},{7,6},{8,9},{9,8},{10,11... | collective-permute-start | bytes 196616 | tf_op jit(solution)/shard_map/ppermute | solution.py:20
  31.8 0.0 collective-permute-done.12.refs_2_
  31.8 0.0 collective-permute-done.11.refs_1_
  31.8 1.7 %collective-permute-done.16.refs_7_ = bf16[128,256]{1,0:T(8,128)(2,1)S(1)} collective-permute-done((bf16[128,256]{1,0:T(8,128)(2,1)S(1)}, bf16[128,256]{1,0:T(8,128)(2,1)S(1)}, u32[]{:S(2)}, u32[]{:S(2)}) %collective-permute-start.16) | collective-permute-done | bytes 65568 | tf_op jit(solution)/shard_map/ppermute | solution.py:20
  33.5 1.2 %collective-permute-done.15.refs_6_ = bf16[128,256]{1,0:T(8,128)(2,1)S(1)} collective-permute-done((bf16[128,256]{1,0:T(8,128)(2,1)S(1)}, bf16[128,256]{1,0:T(8,128)(2,1)S(1)}, u32[]{:S(2)}, u32[]{:S(2)}) %collective-permute-start.15) | collective-permute-done | bytes 65568 | tf_op jit(solution)/shard_map/ppermute | solution.py:20
  34.6 0.2 collective-permute-done.14.refs_5_
  34.9 0.5 %shard_map.88 = (bf16[128,256]{1,0:T(8,128)(2,1)S(1)}, bf16[128,256]{1,0:T(8,128)(2,1)S(1)}, bf16[128,256]{1,0:T(8,128)(2,1)S(1)}, bf16[128,256]{1,0:T(8,128)(2,1)S(1)}) custom-call(bf16[128,256]{1,0:T(8,128)(2,1)S(1)} %get-tuple-element.34.refs_0_, bf16[128,256]{1,0:T(8,128)(2,1)S(1)} %collective-permute-done.11.refs_1_, ...), custom_call_target="tpu_custom_call" | custom-call | flops 268435456 | tf_op jit(solution)/shard_map/pallas_call | solution.py:113
  35.4 1.5 %collective-permute-start.17 = (bf16[128,256]{1,0:T(8,128)(2,1)S(1)}, bf16[128,256]{1,0:T(8,128)(2,1)S(1)}, u32[]{:S(2)}, u32[]{:S(2)}) collective-permute-start(bf16[128,256]{1,0:T(8,128)(2,1)S(1)} %get-tuple-element.31), channel_id=1, source_target_pairs={{0,16},{1,17},{2,18},{3,19},{4,20},{5,21},{6,22},{7,23},{8,24},{9,... | collective-permute-start | bytes 196616 | tf_op jit(solution)/shard_map/ppermute | solution.py:20
  36.9 0.0 collective-permute-start.18
  36.9 0.7 %collective-permute-start.19 = (bf16[128,256]{1,0:T(8,128)(2,1)S(1)}, bf16[128,256]{1,0:T(8,128)(2,1)S(1)}, u32[]{:S(2)}, u32[]{:S(2)}) collective-permute-start(bf16[128,256]{1,0:T(8,128)(2,1)S(1)} %get-tuple-element.33), channel_id=1, source_target_pairs={{0,24},{1,25},{2,26},{3,27},{4,28},{5,29},{6,30},{7,31},{8,16},{9,... | collective-permute-start | bytes 196616 | tf_op jit(solution)/shard_map/ppermute | solution.py:20
  37.6 0.7 %fusion.2 = bf16[1,1,128,256]{3,2,1,0:T(8,128)(2,1)} fusion(f32[128,256]{1,0:T(8,128)S(1)} %get-tuple-element.28), kind=kLoop, calls=%fused_computation.8 | loop fusion | flops 163840 | bytes 196608 | tf_op jit(solution)/shard_map/broadcast_in_dim | solution.py:157
  38.2 1.4 %collective-permute-done.17 = bf16[128,256]{1,0:T(8,128)(2,1)S(1)} collective-permute-done((bf16[128,256]{1,0:T(8,128)(2,1)S(1)}, bf16[128,256]{1,0:T(8,128)(2,1)S(1)}, u32[]{:S(2)}, u32[]{:S(2)}) %collective-permute-start.17) | collective-permute-done | bytes 65568 | tf_op jit(solution)/shard_map/ppermute | solution.py:20
  39.7 0.0 collective-permute-done.18
  39.7 1.0 %collective-permute-done.19 = bf16[128,256]{1,0:T(8,128)(2,1)S(1)} collective-permute-done((bf16[128,256]{1,0:T(8,128)(2,1)S(1)}, bf16[128,256]{1,0:T(8,128)(2,1)S(1)}, u32[]{:S(2)}, u32[]{:S(2)}) %collective-permute-start.19) | collective-permute-done | bytes 65568 | tf_op jit(solution)/shard_map/ppermute | solution.py:20
  40.7 0.8 %fusion = bf16[1,1,128,256]{3,2,1,0:T(8,128)(2,1)} fusion(bf16[256,256]{1,0:T(8,128)(2,1)S(1)} %copy-done.1, bf16[128,256]{1,0:T(8,128)(2,1)S(1)} %collective-permute-done.19, bf16[128,256]{1,0:T(8,128)(2,1)S(1)} %collective-permute-done.18, bf16[128,256]{1,0:T(8,128)(2,1)S(1)} %collective-permute-done.17, bf16[128,256]{1,0:T(8,128)(2,1)S(1)} %get-tuple-element.30), kind=kOutput, calls=%fused_computation.1 | convolution fusion | flops 17072128 | bytes 458752 | tf_op jit(solution)/shard_map/dot_general | solution.py:156
  (1 shorter events, 0.0 us)
Async XLA Ops:
  0.6 3.0 %copy-start.5 = (s32[1,1,8,3]{2,1,3,0:T(1,128)S(1)}, s32[1,1,8,3]{2,1,3,0:T(1,128)}, u32[]{:S(2)}) copy-start(s32[1,1,8,3]{2,1,3,0:T(1,128)} %param.11) | copy-start | bytes 292
  0.6 3.1 %copy-start.3 = (s32[1,1,8]{2,1,0:T(1,128)S(1)}, s32[1,1,8]{2,1,0:T(1,128)}, u32[]{:S(2)}) copy-start(s32[1,1,8]{2,1,0:T(1,128)} %counts_hbm.1) | copy-start | bytes 100
  0.6 5.5 %collective-permute-start.1 = (bf16[128,256]{1,0:T(8,128)(2,1)}, bf16[128,256]{1,0:T(8,128)(2,1)S(1)}, u32[]{:S(2)}, u32[]{:S(2)}) collective-permute-start(bf16[128,256]{1,0:T(8,128)(2,1)} %bitcast.9), channel_id=1, source_target_pairs={{0,16},{1,17},{2,18},{3,19},{4,20},{5,21},{6,22},{7,23},{8,24},{9,... | collective-permute-start | bytes 196616 | tf_op jit(solution)/shard_map/ppermute | solution.py:20
  3.7 2.8 %collective-permute-start = (bf16[128,256]{1,0:T(8,128)(2,1)}, bf16[128,256]{1,0:T(8,128)(2,1)S(1)}, u32[]{:S(2)}, u32[]{:S(2)}) collective-permute-start(bf16[128,256]{1,0:T(8,128)(2,1)} %bitcast.10), channel_id=1, source_target_pairs={{0,8},{1,9},{2,10},{3,11},{4,12},{5,13},{6,14},{7,15},{8,0},{9,1},... | collective-permute-start | bytes 196616 | tf_op jit(solution)/shard_map/ppermute | solution.py:20
  3.7 1.1 %copy-start = (bf16[1,1,8,3,128,128]{5,4,3,2,1,0:T(8,128)(2,1)S(1)}, bf16[1,1,8,3,128,128]{5,4,3,2,1,0:T(8,128)(2,1)}, u32[]{:S(2)}) copy-start(bf16[1,1,8,3,128,128]{5,4,3,2,1,0:T(8,128)(2,1)} %tiles_hbm.1) | copy-start | bytes 2359300
  4.9 2.5 %copy-start.1 = (bf16[256,256]{1,0:T(8,128)(2,1)S(1)}, bf16[256,256]{1,0:T(8,128)(2,1)}, u32[]{:S(2)}) copy-start(bf16[256,256]{1,0:T(8,128)(2,1)} %refs_4_.1) | copy-start | bytes 393220
  4.9 2.5 %copy-start.2 = (bf16[1,1,128,256]{3,2,1,0:T(8,128)(2,1)S(1)}, bf16[1,1,128,256]{3,2,1,0:T(8,128)(2,1)}, u32[]{:S(2)}) copy-start(bf16[1,1,128,256]{3,2,1,0:T(8,128)(2,1)} %param.7) | copy-start | bytes 196612
  6.1 1.3 %collective-permute-start.2 = (bf16[128,256]{1,0:T(8,128)(2,1)S(1)}, bf16[128,256]{1,0:T(8,128)(2,1)S(1)}, u32[]{:S(2)}, u32[]{:S(2)}) collective-permute-start(bf16[128,256]{1,0:T(8,128)(2,1)S(1)} %collective-permute-done.1.refs_2_), channel_id=1, source_target_pairs={{0,8},{1,9},{2,10},{3,11},{4,12},{5,13},{6,14},{7,15},{8,0},{9,1},... | collective-permute-start | bytes 196616 | tf_op jit(solution)/shard_map/ppermute | solution.py:20
  8.0 7.1 %collective-permute-start.6 = (bf16[128,256]{1,0:T(8,128)(2,1)S(1)}, bf16[128,256]{1,0:T(8,128)(2,1)S(1)}, u32[]{:S(2)}, u32[]{:S(2)}) collective-permute-start(bf16[128,256]{1,0:T(8,128)(2,1)S(1)} %get-tuple-element.25), channel_id=1, source_target_pairs={{0,3},{1,2},{2,1},{3,0},{4,7},{5,6},{6,5},{7,4},{8,11},{9,10},{10,... | collective-permute-start | bytes 196616 | tf_op jit(solution)/shard_map/ppermute | solution.py:20
  11.1 4.4 %collective-permute-start.7 = (bf16[128,256]{1,0:T(8,128)(2,1)S(1)}, bf16[128,256]{1,0:T(8,128)(2,1)S(1)}, u32[]{:S(2)}, u32[]{:S(2)}) collective-permute-start(bf16[128,256]{1,0:T(8,128)(2,1)S(1)} %get-tuple-element.26), channel_id=1, source_target_pairs={{0,1},{1,0},{2,3},{3,2},{4,5},{5,4},{6,7},{7,6},{8,9},{9,8},{10,11... | collective-permute-start | bytes 196616 | tf_op jit(solution)/shard_map/ppermute | solution.py:20
  11.7 4.7 %collective-permute-start.8 = (bf16[128,256]{1,0:T(8,128)(2,1)S(1)}, bf16[128,256]{1,0:T(8,128)(2,1)S(1)}, u32[]{:S(2)}, u32[]{:S(2)}) collective-permute-start(bf16[128,256]{1,0:T(8,128)(2,1)S(1)} %get-tuple-element.27), channel_id=1, source_target_pairs={{0,2},{1,3},{2,0},{3,1},{4,6},{5,7},{6,4},{7,5},{8,10},{9,11},{10,... | collective-permute-start | bytes 196616 | tf_op jit(solution)/shard_map/ppermute | solution.py:20
  11.8 7.3 %collective-permute-start.3 = (bf16[128,256]{1,0:T(8,128)(2,1)S(1)}, bf16[128,256]{1,0:T(8,128)(2,1)S(1)}, u32[]{:S(2)}, u32[]{:S(2)}) collective-permute-start(bf16[128,256]{1,0:T(8,128)(2,1)S(1)} %get-tuple-element.21), channel_id=1, source_target_pairs={{0,3},{1,2},{2,1},{3,0},{4,7},{5,6},{6,5},{7,4},{8,11},{9,10},{10,... | collective-permute-start | bytes 196616 | tf_op jit(solution)/shard_map/ppermute | solution.py:20
  14.6 4.5 %collective-permute-start.4 = (bf16[128,256]{1,0:T(8,128)(2,1)S(1)}, bf16[128,256]{1,0:T(8,128)(2,1)S(1)}, u32[]{:S(2)}, u32[]{:S(2)}) collective-permute-start(bf16[128,256]{1,0:T(8,128)(2,1)S(1)} %get-tuple-element.22), channel_id=1, source_target_pairs={{0,1},{1,0},{2,3},{3,2},{4,5},{5,4},{6,7},{7,6},{8,9},{9,8},{10,11... | collective-permute-start | bytes 196616 | tf_op jit(solution)/shard_map/ppermute | solution.py:20
  15.1 4.3 %collective-permute-start.5 = (bf16[128,256]{1,0:T(8,128)(2,1)S(1)}, bf16[128,256]{1,0:T(8,128)(2,1)S(1)}, u32[]{:S(2)}, u32[]{:S(2)}) collective-permute-start(bf16[128,256]{1,0:T(8,128)(2,1)S(1)} %get-tuple-element.23), channel_id=1, source_target_pairs={{0,2},{1,3},{2,0},{3,1},{4,6},{5,7},{6,4},{7,5},{8,10},{9,11},{10,... | collective-permute-start | bytes 196616 | tf_op jit(solution)/shard_map/ppermute | solution.py:20
  16.4 6.0 %copy-start.4 = (bf16[1,1,128,256]{3,2,1,0:T(8,128)(2,1)S(1)}, bf16[1,1,128,256]{3,2,1,0:T(8,128)(2,1)}, u32[]{:S(2)}) copy-start(bf16[1,1,128,256]{3,2,1,0:T(8,128)(2,1)} %param.13) | copy-start | bytes 196612
  16.4 6.0 %copy-start.6 = (f32[256]{0:T(256)S(1)}, f32[256]{0:T(256)}, u32[]{:S(2)}) copy-start(f32[256]{0:T(256)} %param.9) | copy-start | bytes 3076
  16.4 6.0 %collective-permute-start.9 = (bf16[128,256]{1,0:T(8,128)(2,1)S(1)}, bf16[128,256]{1,0:T(8,128)(2,1)S(1)}, u32[]{:S(2)}, u32[]{:S(2)}) collective-permute-start(bf16[128,256]{1,0:T(8,128)(2,1)S(1)} %add_convert_fusion.1), channel_id=1, source_target_pairs={{0,4},{1,5},{2,6},{3,7},{4,0},{5,1},{6,2},{7,3},{8,12},{9,13},{10,... | collective-permute-start | bytes 196616 | tf_op jit(solution)/shard_map/ppermute | solution.py:20
  22.5 5.8 %collective-permute-start.10 = (bf16[128,256]{1,0:T(8,128)(2,1)S(1)}, bf16[128,256]{1,0:T(8,128)(2,1)S(1)}, u32[]{:S(2)}, u32[]{:S(2)}) collective-permute-start(bf16[128,256]{1,0:T(8,128)(2,1)S(1)} %get-tuple-element.34.refs_0_), channel_id=1, source_target_pairs={{0,4},{1,5},{2,6},{3,7},{4,0},{5,1},{6,2},{7,3},{8,12},{9,13},{10,... | collective-permute-start | bytes 196616 | tf_op jit(solution)/shard_map/ppermute | solution.py:20
  24.5 6.1 %collective-permute-start.13 = (bf16[128,256]{1,0:T(8,128)(2,1)S(1)}, bf16[128,256]{1,0:T(8,128)(2,1)S(1)}, u32[]{:S(2)}, u32[]{:S(2)}) collective-permute-start(bf16[128,256]{1,0:T(8,128)(2,1)S(1)} %get-tuple-element.34.refs_0_), channel_id=1, source_target_pairs={{0,3},{1,2},{2,1},{3,0},{4,7},{5,6},{6,5},{7,4},{8,11},{9,10},{10,... | collective-permute-start | bytes 196616 | tf_op jit(solution)/shard_map/ppermute | solution.py:20
  26.9 4.9 %collective-permute-start.12 = (bf16[128,256]{1,0:T(8,128)(2,1)S(1)}, bf16[128,256]{1,0:T(8,128)(2,1)S(1)}, u32[]{:S(2)}, u32[]{:S(2)}) collective-permute-start(bf16[128,256]{1,0:T(8,128)(2,1)S(1)} %get-tuple-element.34.refs_0_), channel_id=1, source_target_pairs={{0,2},{1,3},{2,0},{3,1},{4,6},{5,7},{6,4},{7,5},{8,10},{9,11},{10,... | collective-permute-start | bytes 196616 | tf_op jit(solution)/shard_map/ppermute | solution.py:20
  27.1 4.7 %collective-permute-start.11 = (bf16[128,256]{1,0:T(8,128)(2,1)S(1)}, bf16[128,256]{1,0:T(8,128)(2,1)S(1)}, u32[]{:S(2)}, u32[]{:S(2)}) collective-permute-start(bf16[128,256]{1,0:T(8,128)(2,1)S(1)} %get-tuple-element.34.refs_0_), channel_id=1, source_target_pairs={{0,1},{1,0},{2,3},{3,2},{4,5},{5,4},{6,7},{7,6},{8,9},{9,8},{10,11... | collective-permute-start | bytes 196616 | tf_op jit(solution)/shard_map/ppermute | solution.py:20
  28.3 5.2 %collective-permute-start.16 = (bf16[128,256]{1,0:T(8,128)(2,1)S(1)}, bf16[128,256]{1,0:T(8,128)(2,1)S(1)}, u32[]{:S(2)}, u32[]{:S(2)}) collective-permute-start(bf16[128,256]{1,0:T(8,128)(2,1)S(1)} %collective-permute-done.10.refs_4_), channel_id=1, source_target_pairs={{0,3},{1,2},{2,1},{3,0},{4,7},{5,6},{6,5},{7,4},{8,11},{9,10},{10,... | collective-permute-start | bytes 196616 | tf_op jit(solution)/shard_map/ppermute | solution.py:20
  30.4 4.3 %collective-permute-start.15 = (bf16[128,256]{1,0:T(8,128)(2,1)S(1)}, bf16[128,256]{1,0:T(8,128)(2,1)S(1)}, u32[]{:S(2)}, u32[]{:S(2)}) collective-permute-start(bf16[128,256]{1,0:T(8,128)(2,1)S(1)} %collective-permute-done.10.refs_4_), channel_id=1, source_target_pairs={{0,2},{1,3},{2,0},{3,1},{4,6},{5,7},{6,4},{7,5},{8,10},{9,11},{10,... | collective-permute-start | bytes 196616 | tf_op jit(solution)/shard_map/ppermute | solution.py:20
  30.6 4.3 %collective-permute-start.14 = (bf16[128,256]{1,0:T(8,128)(2,1)S(1)}, bf16[128,256]{1,0:T(8,128)(2,1)S(1)}, u32[]{:S(2)}, u32[]{:S(2)}) collective-permute-start(bf16[128,256]{1,0:T(8,128)(2,1)S(1)} %collective-permute-done.10.refs_4_), channel_id=1, source_target_pairs={{0,1},{1,0},{2,3},{3,2},{4,5},{5,4},{6,7},{7,6},{8,9},{9,8},{10,11... | collective-permute-start | bytes 196616 | tf_op jit(solution)/shard_map/ppermute | solution.py:20
  35.4 4.3 %collective-permute-start.17 = (bf16[128,256]{1,0:T(8,128)(2,1)S(1)}, bf16[128,256]{1,0:T(8,128)(2,1)S(1)}, u32[]{:S(2)}, u32[]{:S(2)}) collective-permute-start(bf16[128,256]{1,0:T(8,128)(2,1)S(1)} %get-tuple-element.31), channel_id=1, source_target_pairs={{0,16},{1,17},{2,18},{3,19},{4,20},{5,21},{6,22},{7,23},{8,24},{9,... | collective-permute-start | bytes 196616 | tf_op jit(solution)/shard_map/ppermute | solution.py:20
  36.9 2.8 %collective-permute-start.18 = (bf16[128,256]{1,0:T(8,128)(2,1)S(1)}, bf16[128,256]{1,0:T(8,128)(2,1)S(1)}, u32[]{:S(2)}, u32[]{:S(2)}) collective-permute-start(bf16[128,256]{1,0:T(8,128)(2,1)S(1)} %get-tuple-element.32), channel_id=1, source_target_pairs={{0,8},{1,9},{2,10},{3,11},{4,12},{5,13},{6,14},{7,15},{8,0},{9,1},... | collective-permute-start | bytes 196616 | tf_op jit(solution)/shard_map/ppermute | solution.py:20
  36.9 3.7 %collective-permute-start.19 = (bf16[128,256]{1,0:T(8,128)(2,1)S(1)}, bf16[128,256]{1,0:T(8,128)(2,1)S(1)}, u32[]{:S(2)}, u32[]{:S(2)}) collective-permute-start(bf16[128,256]{1,0:T(8,128)(2,1)S(1)} %get-tuple-element.33), channel_id=1, source_target_pairs={{0,24},{1,25},{2,26},{3,27},{4,28},{5,29},{6,30},{7,31},{8,16},{9,... | collective-permute-start | bytes 196616 | tf_op jit(solution)/shard_map/ppermute | solution.py:20

commit v4 on v3

--- a/solution.py
+++ b/solution.py
@@ -74,33 +74,49 @@
     )(tile_cols, tile_counts, tile_values)
 
 
-def forward_kernel(count, *refs):
-    pieces, (weight, dense), outs, projected = refs[:count], refs[count : count + 2], refs[count + 2 : -1], refs[-1]
+def project_kernel(places, count, *refs):
+    pieces, (weight, dense), (projected, *outs) = refs[:count], refs[count : count + 2], refs[count + 2 :]
     tile = pieces[0].shape[0]
     for j, piece in enumerate(pieces):
         value = jnp.dot(piece[...], weight[...], preferred_element_type=jnp.float32)
         projected[j * tile : (j + 1) * tile] = value.astype(projected.dtype)
-    for p, out in enumerate(outs):
+    product_kernel(places, projected, dense, *outs)
+
+
+def product_kernel(places, projected, dense, *outs):
+    tile = outs[0].shape[0]
+    for p, out in zip(places, outs):
         value = jnp.dot(dense[p * tile : (p + 1) * tile], projected[...], preferred_element_type=jnp.float32)
         out[...] = value.astype(out.dtype)
 
 
-def forward(pieces, weight, dense):
+def forward(pieces, weight, dense, far):
     tile, width = pieces[0].shape
-    return pl.pallas_call(
-        lambda *refs: forward_kernel(len(pieces), *refs),
-        out_shape=[jax.ShapeDtypeStruct((tile, width), jnp.bfloat16)] * (dense.shape[0] // tile),
-        scratch_shapes=[pltpu.VMEM((len(pieces) * tile, width), jnp.bfloat16)],
-        compiler_params=pltpu.CompilerParams(vmem_limit_bytes=limit(dense.size)),
-        cost_estimate=pl.CostEstimate(flops=2 * dense.size * width, bytes_accessed=0, transcendentals=0),
+    params = pltpu.CompilerParams(vmem_limit_bytes=limit(dense.size))
+    cost = pl.CostEstimate(flops=dense.size * width, bytes_accessed=0, transcendentals=0)
+    out = [jax.ShapeDtypeStruct((tile, width), jnp.bfloat16)] * far
+    last, first = range(far), range(far, 2 * far)
+    projected, *outs = pl.pallas_call(
+        lambda *refs: project_kernel(first, len(pieces), *refs),
+        out_shape=[jax.ShapeDtypeStruct((len(pieces) * tile, width), jnp.bfloat16), *out],
+        compiler_params=params,
+        cost_estimate=cost,
     )(*pieces, weight, dense)
+    product = dict(zip(first, outs))
+    outs = pl.pallas_call(
+        lambda *refs: product_kernel(last, *refs), out_shape=out, compiler_params=params, cost_estimate=cost
+    )(projected, dense)
+    return {**product, **dict(zip(last, outs))}
 
 
-def backward_kernel(count, *refs):
+def backward_kernel(places, *refs):
+    count = len(places)
     pieces, dense, outs, grads = refs[:count], refs[count], refs[count + 1 : -1], refs[-1]
-    tile = pieces[0].shape[0]
-    for p, piece in enumerate(pieces):
-        grads[p * tile : (p + 1) * tile] = piece[...]
+    tile = pieces[0].shape[1]
+    half = grads.shape[0] // 2
+    for p, piece in zip(places, pieces):
+        grads[p * tile : (p + 1) * tile] = piece[0]
+        grads[half + p * tile : half + (p + 1) * tile] = piece[1]
     for j, out in enumerate(outs):
         value = lax.dot_general(
             dense[:, j * tile : (j + 1) * tile], grads[...], (((0,), (0,)), ((), ())), preferred_element_type=jnp.float32
@@ -108,12 +124,12 @@
         out[...] = value.astype(out.dtype)
 
 
-def backward(pieces, dense):
-    tile, width = pieces[0].shape
+def backward(places, pieces, dense):
+    _, tile, width = pieces[0].shape
     return pl.pallas_call(
-        lambda *refs: backward_kernel(len(pieces), *refs),
+        lambda *refs: backward_kernel(places, *refs),
         out_shape=[jax.ShapeDtypeStruct((tile, width), jnp.bfloat16)] * (dense.shape[1] // tile),
-        scratch_shapes=[pltpu.VMEM((len(pieces) * tile, width), jnp.bfloat16)],
+        scratch_shapes=[pltpu.VMEM((2 * len(pieces) * tile, width), jnp.bfloat16)],
         compiler_params=pltpu.CompilerParams(vmem_limit_bytes=limit(dense.size)),
         cost_estimate=pl.CostEstimate(flops=2 * dense.size * width, bytes_accessed=0, transcendentals=0),
     )(*pieces, dense)
@@ -121,7 +137,7 @@
 
 def shards(features, weight, out_bias, tile_values, tile_cols, tile_counts, cotangent):
     far = lax.axis_size("col") // 2
-    near = {k: v if far == 4 else range(1, far) for k, v in {'far': (3, 1, 2), 'own': (3, 1, 2), 'far grad': (2, 1, 3), 'own grad': (3, 1, 2)}.items()}
+    near = {k: v if far == 4 else range(1, far) for k, v in {'far': (3, 2, 1), 'own': (3, 1, 2)}.items()}
     rows = range(1, lax.axis_size("row"))
     own = features[0, 0]
     even = [s for s in rows if s % 2 == 0]
@@ -133,7 +149,7 @@
     for s, piece in zip(even, got):
         pieces[s] = piece
         pieces[s + 1] = swap(piece, row=1)
-    product = forward([pieces[s] for s in range(len(pieces))], weight, dense)
+    product = forward([pieces[s] for s in range(len(pieces))], weight, dense, far)
     half = {}
     for p in (far, 0):
         total = product[p].astype(jnp.float32)
@@ -146,12 +162,11 @@
     grads[far] = swap(grads[0], col=far)
     preact, grads[far] = lax.optimization_barrier((preact, grads[far]))
     activated = silu_slope(preact)[0].astype(jnp.bfloat16)
-    for p in (0, far):
-        for s in near["far grad" if p else "own grad"]:
-            grads[p ^ s] = swap(grads[p], col=s)
-    back = backward([grads[p] for p in range(2 * far)], dense)
+    pair = jnp.stack([grads[0], grads[far]])
+    places = [1, 2, 3, 0] if far == 4 else list(range(far))
+    back = backward(places, [swap(pair, col=p) if p else pair for p in places], dense)
     spread = back[0].astype(jnp.float32)
-    for s in (2, 1, 3):
+    for s in ((2, 1, 3) if len(rows) == 3 else rows):
         spread = spread + swap(back[s], row=s).astype(jnp.float32)
     feature_grad = jnp.dot(spread.astype(jnp.bfloat16), weight.T, preferred_element_type=jnp.float32)
     return activated[None, None], feature_grad.astype(jnp.bfloat16)[None, None]

time: 41.7 us -> 41.3 us (level)
  starting transfers between devices: 24.7 us -> 22.3 us
  waiting for transfers between devices: 11.1 us -> 13 us
    ppermute x20 -> x17, starting transfers between devices: 24.7 us -> 22.3 us  [swap(): return lax.ppermute(value, BOTH, pairs)]
    ppermute x20 -> x17, waiting for transfers between devices: 11.1 us -> 13 us  [swap(): return lax.ppermute(value, BOTH, pairs)]
    pallas_call x2 -> x3, Pallas kernels: 1.11 us -> 1.29 us  [the longest x1 0.5 us: forward(): pl.pallas_call(lambda *refs: project_kernel(first, len(pieces), *refs), o...]
  transfers between devices with their start and end apart: 20 -> 17, of which waited for: 11 -> 11; matrix products, arithmetic and copies ran while one was open for 2% -> 2% of each run, Pallas kernels for 2% -> 3%
where the time goes in v4:
time: 41.3 us; the launch traced here: 41.1 us
  starting transfers between devices  22.3 us (54%)
  waiting for transfers between devices  13 us (31%)
  Pallas kernels  2.26 us (5%)
  local copies, waits for them, and re-layouts  1.24 us (3%)
  other arithmetic  0.83 us (2%)
  matrix products  0.83 us (2%)
  between operations  0.72 us (2%)
    ppermute x17, starting transfers between devices, swap(): return lax.ppermute(value, BOTH, pairs)  22.3 us
    ppermute x17, waiting for transfers between devices, swap(): return lax.ppermute(value, BOTH, pairs)  13 us
    unnamed x15, local copies, waits for them, and re-layouts  1.24 us
    pallas_call x1, Pallas kernels, dense_block(): pl.pallas_call(dense_kernel, in_specs=[HBM] * 3, out_shape=jax.ShapeDtype...  0.97 us
    dot_general x1, matrix products, shards(): jnp.dot(spread.astype(jnp.bfloat16), weight.T, preferred_element_type=jnp...  0.83 us
  transfers between devices with their start and end apart: 17, of which 11 were waited for; matrix products, arithmetic and copies ran while one was open for 2% of the time, Pallas kernels for 3%

profile of v4, /device:TPU:0, one launch (start us, length us, event | category | flops | bytes accessed | tf_op | source)
XLA Modules:
  0.0 41.1 jit_solution(6266473530522097581)
XLA Ops:
  0.6 0.0 copy-start.5
  0.6 0.0 copy-start.3
  0.6 3.0 %collective-permute-start.1 = (bf16[128,256]{1,0:T(8,128)(2,1)}, bf16[128,256]{1,0:T(8,128)(2,1)S(1)}, u32[]{:S(2)}, u32[]{:S(2)}) collective-permute-start(bf16[128,256]{1,0:T(8,128)(2,1)} %bitcast.11), channel_id=1, source_target_pairs={{0,16},{1,17},{2,18},{3,19},{4,20},{5,21},{6,22},{7,23},{8,24},{9,... | collective-permute-start | bytes 196616 | tf_op jit(solution)/shard_map/ppermute | solution.py:20
  3.7 0.0 collective-permute-start
  3.7 0.0 copy-done.5
  3.7 0.1 copy.9.cols_hbm
  3.7 0.0 copy-done.3
  3.7 0.0 copy-start
  3.7 1.1 %copy-done = bf16[1,1,8,3,128,128]{5,4,3,2,1,0:T(8,128)(2,1)S(1)} copy-done((bf16[1,1,8,3,128,128]{5,4,3,2,1,0:T(8,128)(2,1)S(1)}, bf16[1,1,8,3,128,128]{5,4,3,2,1,0:T(8,128)(2,1)}, u32[]{:S(2)}) %copy-start) | copy-done | bytes 786456
  4.9 0.0 copy-start.1
  4.9 0.0 copy-start.2
  4.9 1.0 %shard_map.86.refs_5_.refs_1_.refs_4_ = bf16[1024,512]{1,0:T(8,128)(2,1)S(1)} custom-call(s32[1,1,8,3]{3,2,1,0:T(8,128)S(1)} %copy.9.cols_hbm, s32[1,1,8]{2,1,0:T(1,128)S(1)} %copy-done.3, bf16[1,1,8,3,128,128]{5,4,3,2,1,0:T(8,128)(2,1)S(1)} %copy-done), custom_call_target="tpu_custom_call" | custom-call | bytes 786432 | tf_op jit(solution)/shard_map/pallas_call | solution.py:62
  5.9 0.2 collective-permute-done.1.refs_2_
  6.1 0.4 collective-permute-start.2
  6.5 0.0 collective-permute-done.refs_1_
  6.5 0.9 %collective-permute-done.2.refs_3_ = bf16[128,256]{1,0:T(8,128)(2,1)S(1)} collective-permute-done((bf16[128,256]{1,0:T(8,128)(2,1)S(1)}, bf16[128,256]{1,0:T(8,128)(2,1)S(1)}, u32[]{:S(2)}, u32[]{:S(2)}) %collective-permute-start.2) | collective-permute-done | bytes 65568 | tf_op jit(solution)/shard_map/ppermute | solution.py:20
  7.4 0.0 copy-done.1
  7.4 0.0 copy-done.2
  7.4 0.5 %shard_map.87 = (bf16[512,256]{1,0:T(8,128)(2,1)S(1)}, bf16[128,256]{1,0:T(8,128)(2,1)S(1)}, bf16[128,256]{1,0:T(8,128)(2,1)S(1)}, bf16[128,256]{1,0:T(8,128)(2,1)S(1)}, bf16[128,256]{1,0:T(8,128)(2,1)S(1)}) custom-call(bf16[128,256]{1,0:T(8,128)(2,1)S(1)} %bitcast.13, bf16[128,256]{1,0:T(8,128)(2,1)S(1)} %collective-permute-done.refs_1_, ...), custom_call_target="tpu_custom_call" | custom-call | flops 134217728 | tf_op jit(solution)/shard_map/pallas_call | solution.py:99
  7.9 3.1 %collective-permute-start.6 = (bf16[128,256]{1,0:T(8,128)(2,1)S(1)}, bf16[128,256]{1,0:T(8,128)(2,1)S(1)}, u32[]{:S(2)}, u32[]{:S(2)}) collective-permute-start(bf16[128,256]{1,0:T(8,128)(2,1)S(1)} %get-tuple-element.27), channel_id=1, source_target_pairs={{0,3},{1,2},{2,1},{3,0},{4,7},{5,6},{6,5},{7,4},{8,11},{9,10},{10,... | collective-permute-start | bytes 196616 | tf_op jit(solution)/shard_map/ppermute | solution.py:20
  11.0 0.5 %collective-permute-start.7 = (bf16[128,256]{1,0:T(8,128)(2,1)S(1)}, bf16[128,256]{1,0:T(8,128)(2,1)S(1)}, u32[]{:S(2)}, u32[]{:S(2)}) collective-permute-start(bf16[128,256]{1,0:T(8,128)(2,1)S(1)} %get-tuple-element.28), channel_id=1, source_target_pairs={{0,2},{1,3},{2,0},{3,1},{4,6},{5,7},{6,4},{7,5},{8,10},{9,11},{10,... | collective-permute-start | bytes 196616 | tf_op jit(solution)/shard_map/ppermute | solution.py:20
  11.4 0.2 collective-permute-start.8
  11.6 0.3 shard_map.88
  12.0 2.9 %collective-permute-start.3 = (bf16[128,256]{1,0:T(8,128)(2,1)S(1)}, bf16[128,256]{1,0:T(8,128)(2,1)S(1)}, u32[]{:S(2)}, u32[]{:S(2)}) collective-permute-start(bf16[128,256]{1,0:T(8,128)(2,1)S(1)} %get-tuple-element.23), channel_id=1, source_target_pairs={{0,3},{1,2},{2,1},{3,0},{4,7},{5,6},{6,5},{7,4},{8,11},{9,10},{10,... | collective-permute-start | bytes 196616 | tf_op jit(solution)/shard_map/ppermute | solution.py:20
  14.9 0.5 %collective-permute-start.4 = (bf16[128,256]{1,0:T(8,128)(2,1)S(1)}, bf16[128,256]{1,0:T(8,128)(2,1)S(1)}, u32[]{:S(2)}, u32[]{:S(2)}) collective-permute-start(bf16[128,256]{1,0:T(8,128)(2,1)S(1)} %get-tuple-element.24), channel_id=1, source_target_pairs={{0,1},{1,0},{2,3},{3,2},{4,5},{5,4},{6,7},{7,6},{8,9},{9,8},{10,11... | collective-permute-start | bytes 196616 | tf_op jit(solution)/shard_map/ppermute | solution.py:20
  15.4 0.0 collective-permute-done.6
  15.4 0.5 %collective-permute-start.5 = (bf16[128,256]{1,0:T(8,128)(2,1)S(1)}, bf16[128,256]{1,0:T(8,128)(2,1)S(1)}, u32[]{:S(2)}, u32[]{:S(2)}) collective-permute-start(bf16[128,256]{1,0:T(8,128)(2,1)S(1)} %get-tuple-element.25), channel_id=1, source_target_pairs={{0,2},{1,3},{2,0},{3,1},{4,6},{5,7},{6,4},{7,5},{8,10},{9,11},{10,... | collective-permute-start | bytes 196616 | tf_op jit(solution)/shard_map/ppermute | solution.py:20
  15.9 0.0 collective-permute-done.7
  15.9 0.5 %collective-permute-done.8 = bf16[128,256]{1,0:T(8,128)(2,1)S(1)} collective-permute-done((bf16[128,256]{1,0:T(8,128)(2,1)S(1)}, bf16[128,256]{1,0:T(8,128)(2,1)S(1)}, u32[]{:S(2)}, u32[]{:S(2)}) %collective-permute-start.8) | collective-permute-done | bytes 65568 | tf_op jit(solution)/shard_map/ppermute | solution.py:20
  16.4 0.0 copy-start.4
  16.5 0.0 copy-start.6
  16.5 2.7 %collective-permute-start.9 = (bf16[128,256]{1,0:T(8,128)(2,1)S(1)}, bf16[128,256]{1,0:T(8,128)(2,1)S(1)}, u32[]{:S(2)}, u32[]{:S(2)}) collective-permute-start(bf16[128,256]{1,0:T(8,128)(2,1)S(1)} %add_convert_fusion.1), channel_id=1, source_target_pairs={{0,4},{1,5},{2,6},{3,7},{4,0},{5,1},{6,2},{7,3},{8,12},{9,13},{10,... | collective-permute-start | bytes 196616 | tf_op jit(solution)/shard_map/ppermute | solution.py:20
  19.1 0.0 collective-permute-done.3
  19.1 0.0 collective-permute-done.4
  19.1 0.5 %collective-permute-done.5 = bf16[128,256]{1,0:T(8,128)(2,1)S(1)} collective-permute-done((bf16[128,256]{1,0:T(8,128)(2,1)S(1)}, bf16[128,256]{1,0:T(8,128)(2,1)S(1)}, u32[]{:S(2)}, u32[]{:S(2)}) %collective-permute-start.5) | collective-permute-done | bytes 65568 | tf_op jit(solution)/shard_map/ppermute | solution.py:20
  19.6 2.1 %collective-permute-done.9 = bf16[128,256]{1,0:T(8,128)(2,1)S(1)} collective-permute-done((bf16[128,256]{1,0:T(8,128)(2,1)S(1)}, bf16[128,256]{1,0:T(8,128)(2,1)S(1)}, u32[]{:S(2)}, u32[]{:S(2)}) %collective-permute-start.9) | collective-permute-done | bytes 65568 | tf_op jit(solution)/shard_map/ppermute | solution.py:20
  21.7 0.0 copy-done.4
  21.7 0.0 copy-done.6
  21.7 0.1 fusion.1
  21.8 2.7 %collective-permute-start.10 = (bf16[128,256]{1,0:T(8,128)(2,1)S(1)}, bf16[128,256]{1,0:T(8,128)(2,1)S(1)}, u32[]{:S(2)}, u32[]{:S(2)}) collective-permute-start(bf16[128,256]{1,0:T(8,128)(2,1)S(1)} %get-tuple-element.36), channel_id=1, source_target_pairs={{0,4},{1,5},{2,6},{3,7},{4,0},{5,1},{6,2},{7,3},{8,12},{9,13},{10,... | collective-permute-start | bytes 196616 | tf_op jit(solution)/shard_map/ppermute | solution.py:20
  24.5 2.6 %collective-permute-done.10 = bf16[128,256]{1,0:T(8,128)(2,1)S(1)} collective-permute-done((bf16[128,256]{1,0:T(8,128)(2,1)S(1)}, bf16[128,256]{1,0:T(8,128)(2,1)S(1)}, u32[]{:S(2)}, u32[]{:S(2)}) %collective-permute-start.10) | collective-permute-done | bytes 65568 | tf_op jit(solution)/shard_map/ppermute | solution.py:20
  27.1 2.4 %collective-permute-start.13 = (bf16[2,128,256]{2,1,0:T(8,128)(2,1)S(1)}, bf16[2,128,256]{2,1,0:T(8,128)(2,1)S(1)}, u32[]{:S(2)}, u32[]{:S(2)}) collective-permute-start(bf16[2,128,256]{2,1,0:T(8,128)(2,1)S(1)} %pad_maximum_fusion.refs_3_), channel_id=1, source_target_pairs={{0,3},{1,2},{2,1},{3,0},{4,7},{5,6},{6,5},{7,4},{8,11},{9,10},{10,... | collective-permute-start | bytes 393224 | tf_op jit(solution)/shard_map/ppermute | solution.py:20
  29.5 0.1 collective-permute-start.12
  29.5 1.2 %collective-permute-start.11 = (bf16[2,128,256]{2,1,0:T(8,128)(2,1)S(1)}, bf16[2,128,256]{2,1,0:T(8,128)(2,1)S(1)}, u32[]{:S(2)}, u32[]{:S(2)}) collective-permute-start(bf16[2,128,256]{2,1,0:T(8,128)(2,1)S(1)} %pad_maximum_fusion.refs_3_), channel_id=1, source_target_pairs={{0,1},{1,0},{2,3},{3,2},{4,5},{5,4},{6,7},{7,6},{8,9},{9,8},{10,11... | collective-permute-start | bytes 393224 | tf_op jit(solution)/shard_map/ppermute | solution.py:20
  30.8 2.2 %collective-permute-done.13.refs_2_ = bf16[2,128,256]{2,1,0:T(8,128)(2,1)S(1)} collective-permute-done((bf16[2,128,256]{2,1,0:T(8,128)(2,1)S(1)}, bf16[2,128,256]{2,1,0:T(8,128)(2,1)S(1)}, u32[]{:S(2)}, u32[]{:S(2)}) %collective-permute-start.13) | collective-permute-done | bytes 131104 | tf_op jit(solution)/shard_map/ppermute | solution.py:20
  33.0 1.4 %collective-permute-done.12.refs_1_ = bf16[2,128,256]{2,1,0:T(8,128)(2,1)S(1)} collective-permute-done((bf16[2,128,256]{2,1,0:T(8,128)(2,1)S(1)}, bf16[2,128,256]{2,1,0:T(8,128)(2,1)S(1)}, u32[]{:S(2)}, u32[]{:S(2)}) %collective-permute-start.12) | collective-permute-done | bytes 131104 | tf_op jit(solution)/shard_map/ppermute | solution.py:20
  34.4 0.1 collective-permute-done.11.refs_0_
  34.5 0.5 %shard_map.89 = (bf16[128,256]{1,0:T(8,128)(2,1)S(1)}, bf16[128,256]{1,0:T(8,128)(2,1)S(1)}, bf16[128,256]{1,0:T(8,128)(2,1)S(1)}, bf16[128,256]{1,0:T(8,128)(2,1)S(1)}) custom-call(bf16[2,128,256]{2,1,0:T(8,128)(2,1)S(1)} %collective-permute-done.11.refs_0_, bf16[2,128,256]{2,1,0:T(8,128)(2,1)S(1)} %collective-permute-done.12.refs_1_, ...), custom_call_target="tpu_custom_call" | custom-call | flops 268435456 | tf_op jit(solution)/shard_map/pallas_call | solution.py:129
  35.0 1.6 %collective-permute-start.14 = (bf16[128,256]{1,0:T(8,128)(2,1)S(1)}, bf16[128,256]{1,0:T(8,128)(2,1)S(1)}, u32[]{:S(2)}, u32[]{:S(2)}) collective-permute-start(bf16[128,256]{1,0:T(8,128)(2,1)S(1)} %get-tuple-element.33), channel_id=1, source_target_pairs={{0,16},{1,17},{2,18},{3,19},{4,20},{5,21},{6,22},{7,23},{8,24},{9,... | collective-permute-start | bytes 196616 | tf_op jit(solution)/shard_map/ppermute | solution.py:20
  36.6 0.0 collective-permute-start.15
  36.6 0.6 %collective-permute-start.16 = (bf16[128,256]{1,0:T(8,128)(2,1)S(1)}, bf16[128,256]{1,0:T(8,128)(2,1)S(1)}, u32[]{:S(2)}, u32[]{:S(2)}) collective-permute-start(bf16[128,256]{1,0:T(8,128)(2,1)S(1)} %get-tuple-element.35), channel_id=1, source_target_pairs={{0,24},{1,25},{2,26},{3,27},{4,28},{5,29},{6,30},{7,31},{8,16},{9,... | collective-permute-start | bytes 196616 | tf_op jit(solution)/shard_map/ppermute | solution.py:20
  37.2 0.7 %fusion.2 = bf16[1,1,128,256]{3,2,1,0:T(8,128)(2,1)} fusion(f32[128,256]{1,0:T(8,128)S(1)} %get-tuple-element.30), kind=kLoop, calls=%fused_computation.9 | loop fusion | flops 163840 | bytes 196608 | tf_op jit(solution)/shard_map/broadcast_in_dim | solution.py:172
  37.9 1.4 %collective-permute-done.14 = bf16[128,256]{1,0:T(8,128)(2,1)S(1)} collective-permute-done((bf16[128,256]{1,0:T(8,128)(2,1)S(1)}, bf16[128,256]{1,0:T(8,128)(2,1)S(1)}, u32[]{:S(2)}, u32[]{:S(2)}) %collective-permute-start.14) | collective-permute-done | bytes 65568 | tf_op jit(solution)/shard_map/ppermute | solution.py:20
  39.3 0.0 collective-permute-done.15
  39.3 1.0 %collective-permute-done.16 = bf16[128,256]{1,0:T(8,128)(2,1)S(1)} collective-permute-done((bf16[128,256]{1,0:T(8,128)(2,1)S(1)}, bf16[128,256]{1,0:T(8,128)(2,1)S(1)}, u32[]{:S(2)}, u32[]{:S(2)}) %collective-permute-start.16) | collective-permute-done | bytes 65568 | tf_op jit(solution)/shard_map/ppermute | solution.py:20
  40.3 0.8 %fusion = bf16[1,1,128,256]{3,2,1,0:T(8,128)(2,1)} fusion(bf16[256,256]{1,0:T(8,128)(2,1)S(1)} %copy-done.1, bf16[128,256]{1,0:T(8,128)(2,1)S(1)} %collective-permute-done.16, bf16[128,256]{1,0:T(8,128)(2,1)S(1)} %collective-permute-done.15, bf16[128,256]{1,0:T(8,128)(2,1)S(1)} %collective-permute-done.14, bf16[128,256]{1,0:T(8,128)(2,1)S(1)} %get-tuple-element.32), kind=kOutput, calls=%fused_computation.1 | convolution fusion | flops 17072128 | bytes 458752 | tf_op jit(solution)/shard_map/dot_general | solution.py:171
  (2 shorter events, 0.1 us)
Async XLA Ops:
  0.6 3.0 %copy-start.5 = (s32[1,1,8,3]{2,1,3,0:T(1,128)S(1)}, s32[1,1,8,3]{2,1,3,0:T(1,128)}, u32[]{:S(2)}) copy-start(s32[1,1,8,3]{2,1,3,0:T(1,128)} %param.11) | copy-start | bytes 292
  0.6 3.1 %copy-start.3 = (s32[1,1,8]{2,1,0:T(1,128)S(1)}, s32[1,1,8]{2,1,0:T(1,128)}, u32[]{:S(2)}) copy-start(s32[1,1,8]{2,1,0:T(1,128)} %counts_hbm.1) | copy-start | bytes 100
  0.6 5.5 %collective-permute-start.1 = (bf16[128,256]{1,0:T(8,128)(2,1)}, bf16[128,256]{1,0:T(8,128)(2,1)S(1)}, u32[]{:S(2)}, u32[]{:S(2)}) collective-permute-start(bf16[128,256]{1,0:T(8,128)(2,1)} %bitcast.11), channel_id=1, source_target_pairs={{0,16},{1,17},{2,18},{3,19},{4,20},{5,21},{6,22},{7,23},{8,24},{9,... | collective-permute-start | bytes 196616 | tf_op jit(solution)/shard_map/ppermute | solution.py:20
  3.7 2.8 %collective-permute-start = (bf16[128,256]{1,0:T(8,128)(2,1)}, bf16[128,256]{1,0:T(8,128)(2,1)S(1)}, u32[]{:S(2)}, u32[]{:S(2)}) collective-permute-start(bf16[128,256]{1,0:T(8,128)(2,1)} %bitcast.12), channel_id=1, source_target_pairs={{0,8},{1,9},{2,10},{3,11},{4,12},{5,13},{6,14},{7,15},{8,0},{9,1},... | collective-permute-start | bytes 196616 | tf_op jit(solution)/shard_map/ppermute | solution.py:20
  3.7 1.1 %copy-start = (bf16[1,1,8,3,128,128]{5,4,3,2,1,0:T(8,128)(2,1)S(1)}, bf16[1,1,8,3,128,128]{5,4,3,2,1,0:T(8,128)(2,1)}, u32[]{:S(2)}) copy-start(bf16[1,1,8,3,128,128]{5,4,3,2,1,0:T(8,128)(2,1)} %tiles_hbm.1) | copy-start | bytes 2359300
  4.9 2.5 %copy-start.1 = (bf16[256,256]{1,0:T(8,128)(2,1)S(1)}, bf16[256,256]{1,0:T(8,128)(2,1)}, u32[]{:S(2)}) copy-start(bf16[256,256]{1,0:T(8,128)(2,1)} %refs_4_.1) | copy-start | bytes 393220
  4.9 2.5 %copy-start.2 = (bf16[1,1,128,256]{3,2,1,0:T(8,128)(2,1)S(1)}, bf16[1,1,128,256]{3,2,1,0:T(8,128)(2,1)}, u32[]{:S(2)}) copy-start(bf16[1,1,128,256]{3,2,1,0:T(8,128)(2,1)} %param.7) | copy-start | bytes 196612
  6.1 1.3 %collective-permute-start.2 = (bf16[128,256]{1,0:T(8,128)(2,1)S(1)}, bf16[128,256]{1,0:T(8,128)(2,1)S(1)}, u32[]{:S(2)}, u32[]{:S(2)}) collective-permute-start(bf16[128,256]{1,0:T(8,128)(2,1)S(1)} %collective-permute-done.1.refs_2_), channel_id=1, source_target_pairs={{0,8},{1,9},{2,10},{3,11},{4,12},{5,13},{6,14},{7,15},{8,0},{9,1},... | collective-permute-start | bytes 196616 | tf_op jit(solution)/shard_map/ppermute | solution.py:20
  7.9 7.5 %collective-permute-start.6 = (bf16[128,256]{1,0:T(8,128)(2,1)S(1)}, bf16[128,256]{1,0:T(8,128)(2,1)S(1)}, u32[]{:S(2)}, u32[]{:S(2)}) collective-permute-start(bf16[128,256]{1,0:T(8,128)(2,1)S(1)} %get-tuple-element.27), channel_id=1, source_target_pairs={{0,3},{1,2},{2,1},{3,0},{4,7},{5,6},{6,5},{7,4},{8,11},{9,10},{10,... | collective-permute-start | bytes 196616 | tf_op jit(solution)/shard_map/ppermute | solution.py:20
  11.0 4.9 %collective-permute-start.7 = (bf16[128,256]{1,0:T(8,128)(2,1)S(1)}, bf16[128,256]{1,0:T(8,128)(2,1)S(1)}, u32[]{:S(2)}, u32[]{:S(2)}) collective-permute-start(bf16[128,256]{1,0:T(8,128)(2,1)S(1)} %get-tuple-element.28), channel_id=1, source_target_pairs={{0,2},{1,3},{2,0},{3,1},{4,6},{5,7},{6,4},{7,5},{8,10},{9,11},{10,... | collective-permute-start | bytes 196616 | tf_op jit(solution)/shard_map/ppermute | solution.py:20
  11.4 5.0 %collective-permute-start.8 = (bf16[128,256]{1,0:T(8,128)(2,1)S(1)}, bf16[128,256]{1,0:T(8,128)(2,1)S(1)}, u32[]{:S(2)}, u32[]{:S(2)}) collective-permute-start(bf16[128,256]{1,0:T(8,128)(2,1)S(1)} %get-tuple-element.29), channel_id=1, source_target_pairs={{0,1},{1,0},{2,3},{3,2},{4,5},{5,4},{6,7},{7,6},{8,9},{9,8},{10,11... | collective-permute-start | bytes 196616 | tf_op jit(solution)/shard_map/ppermute | solution.py:20
  12.0 7.2 %collective-permute-start.3 = (bf16[128,256]{1,0:T(8,128)(2,1)S(1)}, bf16[128,256]{1,0:T(8,128)(2,1)S(1)}, u32[]{:S(2)}, u32[]{:S(2)}) collective-permute-start(bf16[128,256]{1,0:T(8,128)(2,1)S(1)} %get-tuple-element.23), channel_id=1, source_target_pairs={{0,3},{1,2},{2,1},{3,0},{4,7},{5,6},{6,5},{7,4},{8,11},{9,10},{10,... | collective-permute-start | bytes 196616 | tf_op jit(solution)/shard_map/ppermute | solution.py:20
  14.9 4.3 %collective-permute-start.4 = (bf16[128,256]{1,0:T(8,128)(2,1)S(1)}, bf16[128,256]{1,0:T(8,128)(2,1)S(1)}, u32[]{:S(2)}, u32[]{:S(2)}) collective-permute-start(bf16[128,256]{1,0:T(8,128)(2,1)S(1)} %get-tuple-element.24), channel_id=1, source_target_pairs={{0,1},{1,0},{2,3},{3,2},{4,5},{5,4},{6,7},{7,6},{8,9},{9,8},{10,11... | collective-permute-start | bytes 196616 | tf_op jit(solution)/shard_map/ppermute | solution.py:20
  15.4 4.3 %collective-permute-start.5 = (bf16[128,256]{1,0:T(8,128)(2,1)S(1)}, bf16[128,256]{1,0:T(8,128)(2,1)S(1)}, u32[]{:S(2)}, u32[]{:S(2)}) collective-permute-start(bf16[128,256]{1,0:T(8,128)(2,1)S(1)} %get-tuple-element.25), channel_id=1, source_target_pairs={{0,2},{1,3},{2,0},{3,1},{4,6},{5,7},{6,4},{7,5},{8,10},{9,11},{10,... | collective-permute-start | bytes 196616 | tf_op jit(solution)/shard_map/ppermute | solution.py:20
  16.4 5.3 %copy-start.4 = (bf16[1,1,128,256]{3,2,1,0:T(8,128)(2,1)S(1)}, bf16[1,1,128,256]{3,2,1,0:T(8,128)(2,1)}, u32[]{:S(2)}) copy-start(bf16[1,1,128,256]{3,2,1,0:T(8,128)(2,1)} %param.13) | copy-start | bytes 196612
  16.5 5.2 %copy-start.6 = (f32[256]{0:T(256)S(1)}, f32[256]{0:T(256)}, u32[]{:S(2)}) copy-start(f32[256]{0:T(256)} %param.9) | copy-start | bytes 3076
  16.5 5.2 %collective-permute-start.9 = (bf16[128,256]{1,0:T(8,128)(2,1)S(1)}, bf16[128,256]{1,0:T(8,128)(2,1)S(1)}, u32[]{:S(2)}, u32[]{:S(2)}) collective-permute-start(bf16[128,256]{1,0:T(8,128)(2,1)S(1)} %add_convert_fusion.1), channel_id=1, source_target_pairs={{0,4},{1,5},{2,6},{3,7},{4,0},{5,1},{6,2},{7,3},{8,12},{9,13},{10,... | collective-permute-start | bytes 196616 | tf_op jit(solution)/shard_map/ppermute | solution.py:20
  21.8 5.3 %collective-permute-start.10 = (bf16[128,256]{1,0:T(8,128)(2,1)S(1)}, bf16[128,256]{1,0:T(8,128)(2,1)S(1)}, u32[]{:S(2)}, u32[]{:S(2)}) collective-permute-start(bf16[128,256]{1,0:T(8,128)(2,1)S(1)} %get-tuple-element.36), channel_id=1, source_target_pairs={{0,4},{1,5},{2,6},{3,7},{4,0},{5,1},{6,2},{7,3},{8,12},{9,13},{10,... | collective-permute-start | bytes 196616 | tf_op jit(solution)/shard_map/ppermute | solution.py:20
  27.1 5.9 %collective-permute-start.13 = (bf16[2,128,256]{2,1,0:T(8,128)(2,1)S(1)}, bf16[2,128,256]{2,1,0:T(8,128)(2,1)S(1)}, u32[]{:S(2)}, u32[]{:S(2)}) collective-permute-start(bf16[2,128,256]{2,1,0:T(8,128)(2,1)S(1)} %pad_maximum_fusion.refs_3_), channel_id=1, source_target_pairs={{0,3},{1,2},{2,1},{3,0},{4,7},{5,6},{6,5},{7,4},{8,11},{9,10},{10,... | collective-permute-start | bytes 393224 | tf_op jit(solution)/shard_map/ppermute | solution.py:20
  29.5 5.0 %collective-permute-start.12 = (bf16[2,128,256]{2,1,0:T(8,128)(2,1)S(1)}, bf16[2,128,256]{2,1,0:T(8,128)(2,1)S(1)}, u32[]{:S(2)}, u32[]{:S(2)}) collective-permute-start(bf16[2,128,256]{2,1,0:T(8,128)(2,1)S(1)} %pad_maximum_fusion.refs_3_), channel_id=1, source_target_pairs={{0,2},{1,3},{2,0},{3,1},{4,6},{5,7},{6,4},{7,5},{8,10},{9,11},{10,... | collective-permute-start | bytes 393224 | tf_op jit(solution)/shard_map/ppermute | solution.py:20
  29.5 5.0 %collective-permute-start.11 = (bf16[2,128,256]{2,1,0:T(8,128)(2,1)S(1)}, bf16[2,128,256]{2,1,0:T(8,128)(2,1)S(1)}, u32[]{:S(2)}, u32[]{:S(2)}) collective-permute-start(bf16[2,128,256]{2,1,0:T(8,128)(2,1)S(1)} %pad_maximum_fusion.refs_3_), channel_id=1, source_target_pairs={{0,1},{1,0},{2,3},{3,2},{4,5},{5,4},{6,7},{7,6},{8,9},{9,8},{10,11... | collective-permute-start | bytes 393224 | tf_op jit(solution)/shard_map/ppermute | solution.py:20
  35.0 4.3 %collective-permute-start.14 = (bf16[128,256]{1,0:T(8,128)(2,1)S(1)}, bf16[128,256]{1,0:T(8,128)(2,1)S(1)}, u32[]{:S(2)}, u32[]{:S(2)}) collective-permute-start(bf16[128,256]{1,0:T(8,128)(2,1)S(1)} %get-tuple-element.33), channel_id=1, source_target_pairs={{0,16},{1,17},{2,18},{3,19},{4,20},{5,21},{6,22},{7,23},{8,24},{9,... | collective-permute-start | bytes 196616 | tf_op jit(solution)/shard_map/ppermute | solution.py:20
  36.6 2.8 %collective-permute-start.15 = (bf16[128,256]{1,0:T(8,128)(2,1)S(1)}, bf16[128,256]{1,0:T(8,128)(2,1)S(1)}, u32[]{:S(2)}, u32[]{:S(2)}) collective-permute-start(bf16[128,256]{1,0:T(8,128)(2,1)S(1)} %get-tuple-element.34), channel_id=1, source_target_pairs={{0,8},{1,9},{2,10},{3,11},{4,12},{5,13},{6,14},{7,15},{8,0},{9,1},... | collective-permute-start | bytes 196616 | tf_op jit(solution)/shard_map/ppermute | solution.py:20
  36.6 3.7 %collective-permute-start.16 = (bf16[128,256]{1,0:T(8,128)(2,1)S(1)}, bf16[128,256]{1,0:T(8,128)(2,1)S(1)}, u32[]{:S(2)}, u32[]{:S(2)}) collective-permute-start(bf16[128,256]{1,0:T(8,128)(2,1)S(1)} %get-tuple-element.35), channel_id=1, source_target_pairs={{0,24},{1,25},{2,26},{3,27},{4,28},{5,29},{6,30},{7,31},{8,16},{9,... | collective-permute-start | bytes 196616 | tf_op jit(solution)/shard_map/ppermute | solution.py:20

commit v5 on v4

--- a/solution.py
+++ b/solution.py
@@ -26,6 +26,7 @@
 
 def dense_kernel(cols_hbm, counts_hbm, tiles_hbm, dense, cols, counts, tiles, sems):
     row_tiles, slots, tile, _ = tiles.shape
+    width = dense.shape[1]
     me_row, me_col = lax.axis_index("row"), lax.axis_index("col")
     copies = [
         pltpu.make_async_copy(cols_hbm.at[0, 0], cols, sems.at[0]),
@@ -45,7 +46,8 @@
 
             @pl.when(slot < counts[0, row_tile])
             def _():
-                column = pl.multiple_of((cols[row_tile, slot] ^ me_row) * tile, tile)
+                peer = cols[row_tile, slot] ^ me_row
+                column = pl.multiple_of((peer // 2 + peer % 2 * (width // tile // 2)) * tile, tile)
                 dense[pl.ds(start, tile), pl.ds(column, tile)] = tiles[row_tile, slot]
 
     if row_tiles <= 8:
@@ -74,39 +76,76 @@
     )(tile_cols, tile_counts, tile_values)
 
 
-def project_kernel(places, count, *refs):
-    pieces, (weight, dense), (projected, *outs) = refs[:count], refs[count : count + 2], refs[count + 2 :]
-    tile = pieces[0].shape[0]
+def start_kernel(count, *refs):
+    pieces, (weight, dense), (projected, begun) = refs[:count], refs[count : count + 2], refs[count + 2 :]
+    tile, far = pieces[0].shape[0], begun.shape[0]
     for j, piece in enumerate(pieces):
         value = jnp.dot(piece[...], weight[...], preferred_element_type=jnp.float32)
         projected[j * tile : (j + 1) * tile] = value.astype(projected.dtype)
-    product_kernel(places, projected, dense, *outs)
-
-
-def product_kernel(places, projected, dense, *outs):
-    tile = outs[0].shape[0]
-    for p, out in zip(places, outs):
-        value = jnp.dot(dense[p * tile : (p + 1) * tile], projected[...], preferred_element_type=jnp.float32)
+    for k in range(far):
+        begun[k] = jnp.dot(
+            dense[(far + k) * tile : (far + k + 1) * tile, : count * tile],
+            projected[...],
+            preferred_element_type=jnp.float32,
+        )
+
+
+def finish_kernel(count, *refs):
+    pieces, (weight, dense, begun), (projected, *outs) = refs[:count], refs[count : count + 3], refs[count + 3 :]
+    tile, far = pieces[0].shape[0], begun.shape[0]
+    for j, piece in enumerate(pieces):
+        value = jnp.dot(piece[...], weight[...], preferred_element_type=jnp.float32)
+        projected[j * tile : (j + 1) * tile] = value.astype(projected.dtype)
+    for k, out in enumerate(outs):
+        value = jnp.dot(
+            dense[(far + k) * tile : (far + k + 1) * tile, count * tile :],
+            projected[...],
+            preferred_element_type=jnp.float32,
+        )
+        out[...] = (begun[k] + value).astype(out.dtype)
+
+
+def product_kernel(first, second, dense, *outs):
+    tile, width = outs[0].shape[0], first.shape[0]
+    for p, out in enumerate(outs):
+        rows = dense[p * tile : (p + 1) * tile]
+        value = jnp.dot(rows[:, :width], first[...], preferred_element_type=jnp.float32)
+        value = value + jnp.dot(rows[:, width:], second[...], preferred_element_type=jnp.float32)
         out[...] = value.astype(out.dtype)
 
 
-def forward(pieces, weight, dense, far):
+def start(pieces, weight, dense, far):
+    tile, width = pieces[0].shape
+    return pl.pallas_call(
+        lambda *refs: start_kernel(len(pieces), *refs),
+        out_shape=(
+            jax.ShapeDtypeStruct((len(pieces) * tile, width), jnp.bfloat16),
+            jax.ShapeDtypeStruct((far, tile, width), jnp.float32),
+        ),
+        compiler_params=pltpu.CompilerParams(vmem_limit_bytes=limit(dense.size)),
+        cost_estimate=pl.CostEstimate(flops=dense.size * width // 2, bytes_accessed=0, transcendentals=0),
+    )(*pieces, weight, dense)
+
+
+def forward(begun, pieces, weight, dense, far):
+    first, begun = begun
     tile, width = pieces[0].shape
     params = pltpu.CompilerParams(vmem_limit_bytes=limit(dense.size))
-    cost = pl.CostEstimate(flops=dense.size * width, bytes_accessed=0, transcendentals=0)
     out = [jax.ShapeDtypeStruct((tile, width), jnp.bfloat16)] * far
-    last, first = range(far), range(far, 2 * far)
-    projected, *outs = pl.pallas_call(
-        lambda *refs: project_kernel(first, len(pieces), *refs),
+    second, *outs = pl.pallas_call(
+        lambda *refs: finish_kernel(len(pieces), *refs),
         out_shape=[jax.ShapeDtypeStruct((len(pieces) * tile, width), jnp.bfloat16), *out],
         compiler_params=params,
-        cost_estimate=cost,
-    )(*pieces, weight, dense)
-    product = dict(zip(first, outs))
+        cost_estimate=pl.CostEstimate(flops=dense.size * width // 2, bytes_accessed=0, transcendentals=0),
+    )(*pieces, weight, dense, begun)
+    product = {far + k: value for k, value in enumerate(outs)}
     outs = pl.pallas_call(
-        lambda *refs: product_kernel(last, *refs), out_shape=out, compiler_params=params, cost_estimate=cost
-    )(projected, dense)
-    return {**product, **dict(zip(last, outs))}
+        product_kernel,
+        out_shape=out,
+        compiler_params=params,
+        cost_estimate=pl.CostEstimate(flops=dense.size * width, bytes_accessed=0, transcendentals=0),
+    )(first, second, dense)
+    return {**product, **dict(enumerate(outs))}
 
 
 def backward_kernel(places, *refs):
@@ -137,7 +176,7 @@
 
 def shards(features, weight, out_bias, tile_values, tile_cols, tile_counts, cotangent):
     far = lax.axis_size("col") // 2
-    near = {k: v if far == 4 else range(1, far) for k, v in {'far': (3, 2, 1), 'own': (3, 1, 2)}.items()}
+    near = {"far": (3, 2, 1), "own": (3, 1, 2)} if far == 4 else {"far": range(1, far), "own": range(1, far)}
     rows = range(1, lax.axis_size("row"))
     own = features[0, 0]
     even = [s for s in rows if s % 2 == 0]
@@ -146,10 +185,9 @@
     pieces[1] = swap(own, row=1)
     dense = dense_block(tile_cols, tile_counts, tile_values)
     dense, *got = lax.optimization_barrier((dense, *(pieces[s] for s in even)))
-    for s, piece in zip(even, got):
-        pieces[s] = piece
-        pieces[s + 1] = swap(piece, row=1)
-    product = forward([pieces[s] for s in range(len(pieces))], weight, dense, far)
+    twins = [swap(piece, row=1) for piece in got]
+    begun = start([own, *got], weight, dense, far)
+    product = forward(begun, [pieces[1], *twins], weight, dense, far)
     half = {}
     for p in (far, 0):
         total = product[p].astype(jnp.float32)
@@ -165,6 +203,7 @@
     pair = jnp.stack([grads[0], grads[far]])
     places = [1, 2, 3, 0] if far == 4 else list(range(far))
     back = backward(places, [swap(pair, col=p) if p else pair for p in places], dense)
+    back = dict(zip([0, *even, *(s for s in rows if s % 2)], back))
     spread = back[0].astype(jnp.float32)
     for s in ((2, 1, 3) if len(rows) == 3 else rows):
         spread = spread + swap(back[s], row=s).astype(jnp.float32)

time: 41.3 us -> 41.2 us (level)
  waiting for transfers between devices: 13 us -> 12.5 us
  Pallas kernels: 2.26 us -> 2.68 us
    ppermute x17, waiting for transfers between devices: 13 us -> 12.5 us  [swap(): return lax.ppermute(value, BOTH, pairs)]
    pallas_call x2 -> x3, Pallas kernels: 0.8 us -> 1.11 us  [the longest x1 0.41 us: forward(): pl.pallas_call(lambda *refs: finish_kernel(len(pieces), *refs), out_shape...]
  transfers between devices with their start and end apart: 17 -> 17, of which waited for: 11 -> 11; matrix products, arithmetic and copies ran while one was open for 2% -> 2% of each run, Pallas kernels for 3% -> 4%
where the time goes in v5:
time: 41.2 us; the launch traced here: 41 us
  starting transfers between devices  22.3 us (54%)
  waiting for transfers between devices  12.5 us (30%)
  Pallas kernels  2.68 us (7%)
  local copies, waits for them, and re-layouts  1.24 us (3%)
  other arithmetic  0.83 us (2%)
  matrix products  0.83 us (2%)
  between operations  0.73 us (2%)
    ppermute x17, starting transfers between devices, swap(): return lax.ppermute(value, BOTH, pairs)  22.3 us
    ppermute x17, waiting for transfers between devices, swap(): return lax.ppermute(value, BOTH, pairs)  12.5 us
    unnamed x15, local copies, waits for them, and re-layouts  1.24 us
    pallas_call x1, Pallas kernels, dense_block(): pl.pallas_call(dense_kernel, in_specs=[HBM] * 3, out_shape=jax.ShapeDtype...  1.08 us
    dot_general x1, matrix products, shards(): jnp.dot(spread.astype(jnp.bfloat16), weight.T, preferred_element_type=jnp...  0.83 us
  transfers between devices with their start and end apart: 17, of which 11 were waited for; matrix products, arithmetic and copies ran while one was open for 2% of the time, Pallas kernels for 4%

profile of v5, /device:TPU:0, one launch (start us, length us, event | category | flops | bytes accessed | tf_op | source)
XLA Modules:
  0.0 41.0 jit_solution(17371275965634963540)
XLA Ops:
  0.6 0.0 copy-start.5
  0.6 0.0 copy-start.3
  0.6 3.0 %collective-permute-start = (bf16[128,256]{1,0:T(8,128)(2,1)}, bf16[128,256]{1,0:T(8,128)(2,1)S(1)}, u32[]{:S(2)}, u32[]{:S(2)}) collective-permute-start(bf16[128,256]{1,0:T(8,128)(2,1)} %bitcast.11), channel_id=1, source_target_pairs={{0,16},{1,17},{2,18},{3,19},{4,20},{5,21},{6,22},{7,23},{8,24},{9,... | collective-permute-start | bytes 196616 | tf_op jit(solution)/shard_map/ppermute | solution.py:20
  3.7 0.0 collective-permute-start.1
  3.7 0.0 copy-done.5
  3.7 0.1 copy.9.cols_hbm
  3.7 0.0 copy-done.3
  3.7 0.0 copy-start.1
  3.7 1.1 %copy-done.1 = bf16[1,1,8,3,128,128]{5,4,3,2,1,0:T(8,128)(2,1)S(1)} copy-done((bf16[1,1,8,3,128,128]{5,4,3,2,1,0:T(8,128)(2,1)S(1)}, bf16[1,1,8,3,128,128]{5,4,3,2,1,0:T(8,128)(2,1)}, u32[]{:S(2)}) %copy-start.1) | copy-done | bytes 786456
  4.9 0.0 copy-start
  4.9 0.0 copy-start.2
  4.9 1.1 %shard_map.86.refs_3_.dense.refs_4_ = bf16[1024,512]{1,0:T(8,128)(2,1)S(1)} custom-call(s32[1,1,8,3]{3,2,1,0:T(8,128)S(1)} %copy.9.cols_hbm, s32[1,1,8]{2,1,0:T(1,128)S(1)} %copy-done.3, bf16[1,1,8,3,128,128]{5,4,3,2,1,0:T(8,128)(2,1)S(1)} %copy-done.1), custom_call_target="tpu_custom_call" | custom-call | bytes 786432 | tf_op jit(solution)/shard_map/pallas_call | solution.py:64
  6.0 0.1 collective-permute-done.refs_1_
  6.1 0.4 collective-permute-start.2
  6.5 0.0 copy-done
  6.5 0.0 copy-done.2
  6.5 0.4 shard_map.87
  6.9 0.0 collective-permute-done.1.refs_0_
  6.9 0.5 %collective-permute-done.2.refs_1_ = bf16[128,256]{1,0:T(8,128)(2,1)S(1)} collective-permute-done((bf16[128,256]{1,0:T(8,128)(2,1)S(1)}, bf16[128,256]{1,0:T(8,128)(2,1)S(1)}, u32[]{:S(2)}, u32[]{:S(2)}) %collective-permute-start.2) | collective-permute-done | bytes 65568 | tf_op jit(solution)/shard_map/ppermute | solution.py:20
  7.4 0.4 shard_map.88
  7.8 3.1 %collective-permute-start.6 = (bf16[128,256]{1,0:T(8,128)(2,1)S(1)}, bf16[128,256]{1,0:T(8,128)(2,1)S(1)}, u32[]{:S(2)}, u32[]{:S(2)}) collective-permute-start(bf16[128,256]{1,0:T(8,128)(2,1)S(1)} %get-tuple-element.31), channel_id=1, source_target_pairs={{0,3},{1,2},{2,1},{3,0},{4,7},{5,6},{6,5},{7,4},{8,11},{9,10},{10,... | collective-permute-start | bytes 196616 | tf_op jit(solution)/shard_map/ppermute | solution.py:20
  10.9 0.4 %collective-permute-start.7 = (bf16[128,256]{1,0:T(8,128)(2,1)S(1)}, bf16[128,256]{1,0:T(8,128)(2,1)S(1)}, u32[]{:S(2)}, u32[]{:S(2)}) collective-permute-start(bf16[128,256]{1,0:T(8,128)(2,1)S(1)} %get-tuple-element.32), channel_id=1, source_target_pairs={{0,2},{1,3},{2,0},{3,1},{4,6},{5,7},{6,4},{7,5},{8,10},{9,11},{10,... | collective-permute-start | bytes 196616 | tf_op jit(solution)/shard_map/ppermute | solution.py:20
  11.4 0.2 collective-permute-start.8
  11.5 0.3 shard_map.89
  11.9 2.9 %collective-permute-start.3 = (bf16[128,256]{1,0:T(8,128)(2,1)S(1)}, bf16[128,256]{1,0:T(8,128)(2,1)S(1)}, u32[]{:S(2)}, u32[]{:S(2)}) collective-permute-start(bf16[128,256]{1,0:T(8,128)(2,1)S(1)} %get-tuple-element.27), channel_id=1, source_target_pairs={{0,3},{1,2},{2,1},{3,0},{4,7},{5,6},{6,5},{7,4},{8,11},{9,10},{10,... | collective-permute-start | bytes 196616 | tf_op jit(solution)/shard_map/ppermute | solution.py:20
  14.8 0.5 %collective-permute-start.4 = (bf16[128,256]{1,0:T(8,128)(2,1)S(1)}, bf16[128,256]{1,0:T(8,128)(2,1)S(1)}, u32[]{:S(2)}, u32[]{:S(2)}) collective-permute-start(bf16[128,256]{1,0:T(8,128)(2,1)S(1)} %get-tuple-element.28), channel_id=1, source_target_pairs={{0,1},{1,0},{2,3},{3,2},{4,5},{5,4},{6,7},{7,6},{8,9},{9,8},{10,11... | collective-permute-start | bytes 196616 | tf_op jit(solution)/shard_map/ppermute | solution.py:20
  15.3 0.0 collective-permute-done.6
  15.3 0.5 %collective-permute-start.5 = (bf16[128,256]{1,0:T(8,128)(2,1)S(1)}, bf16[128,256]{1,0:T(8,128)(2,1)S(1)}, u32[]{:S(2)}, u32[]{:S(2)}) collective-permute-start(bf16[128,256]{1,0:T(8,128)(2,1)S(1)} %get-tuple-element.29), channel_id=1, source_target_pairs={{0,2},{1,3},{2,0},{3,1},{4,6},{5,7},{6,4},{7,5},{8,10},{9,11},{10,... | collective-permute-start | bytes 196616 | tf_op jit(solution)/shard_map/ppermute | solution.py:20
  15.8 0.0 collective-permute-done.7
  15.8 0.5 %collective-permute-done.8 = bf16[128,256]{1,0:T(8,128)(2,1)S(1)} collective-permute-done((bf16[128,256]{1,0:T(8,128)(2,1)S(1)}, bf16[128,256]{1,0:T(8,128)(2,1)S(1)}, u32[]{:S(2)}, u32[]{:S(2)}) %collective-permute-start.8) | collective-permute-done | bytes 65568 | tf_op jit(solution)/shard_map/ppermute | solution.py:20
  16.3 0.0 copy-start.4
  16.4 0.0 copy-start.6
  16.4 2.7 %collective-permute-start.9 = (bf16[128,256]{1,0:T(8,128)(2,1)S(1)}, bf16[128,256]{1,0:T(8,128)(2,1)S(1)}, u32[]{:S(2)}, u32[]{:S(2)}) collective-permute-start(bf16[128,256]{1,0:T(8,128)(2,1)S(1)} %add_convert_fusion.1), channel_id=1, source_target_pairs={{0,4},{1,5},{2,6},{3,7},{4,0},{5,1},{6,2},{7,3},{8,12},{9,13},{10,... | collective-permute-start | bytes 196616 | tf_op jit(solution)/shard_map/ppermute | solution.py:20
  19.0 0.0 collective-permute-done.3
  19.0 0.0 collective-permute-done.4
  19.0 0.5 %collective-permute-done.5 = bf16[128,256]{1,0:T(8,128)(2,1)S(1)} collective-permute-done((bf16[128,256]{1,0:T(8,128)(2,1)S(1)}, bf16[128,256]{1,0:T(8,128)(2,1)S(1)}, u32[]{:S(2)}, u32[]{:S(2)}) %collective-permute-start.5) | collective-permute-done | bytes 65568 | tf_op jit(solution)/shard_map/ppermute | solution.py:20
  19.5 2.1 %collective-permute-done.9 = bf16[128,256]{1,0:T(8,128)(2,1)S(1)} collective-permute-done((bf16[128,256]{1,0:T(8,128)(2,1)S(1)}, bf16[128,256]{1,0:T(8,128)(2,1)S(1)}, u32[]{:S(2)}, u32[]{:S(2)}) %collective-permute-start.9) | collective-permute-done | bytes 65568 | tf_op jit(solution)/shard_map/ppermute | solution.py:20
  21.6 0.0 copy-done.4
  21.6 0.0 copy-done.6
  21.6 0.1 fusion.1
  21.7 2.7 %collective-permute-start.10 = (bf16[128,256]{1,0:T(8,128)(2,1)S(1)}, bf16[128,256]{1,0:T(8,128)(2,1)S(1)}, u32[]{:S(2)}, u32[]{:S(2)}) collective-permute-start(bf16[128,256]{1,0:T(8,128)(2,1)S(1)} %get-tuple-element.40), channel_id=1, source_target_pairs={{0,4},{1,5},{2,6},{3,7},{4,0},{5,1},{6,2},{7,3},{8,12},{9,13},{10,... | collective-permute-start | bytes 196616 | tf_op jit(solution)/shard_map/ppermute | solution.py:20
  24.4 2.6 %collective-permute-done.10 = bf16[128,256]{1,0:T(8,128)(2,1)S(1)} collective-permute-done((bf16[128,256]{1,0:T(8,128)(2,1)S(1)}, bf16[128,256]{1,0:T(8,128)(2,1)S(1)}, u32[]{:S(2)}, u32[]{:S(2)}) %collective-permute-start.10) | collective-permute-done | bytes 65568 | tf_op jit(solution)/shard_map/ppermute | solution.py:20
  27.0 2.4 %collective-permute-start.13 = (bf16[2,128,256]{2,1,0:T(8,128)(2,1)S(1)}, bf16[2,128,256]{2,1,0:T(8,128)(2,1)S(1)}, u32[]{:S(2)}, u32[]{:S(2)}) collective-permute-start(bf16[2,128,256]{2,1,0:T(8,128)(2,1)S(1)} %pad_maximum_fusion.refs_3_), channel_id=1, source_target_pairs={{0,3},{1,2},{2,1},{3,0},{4,7},{5,6},{6,5},{7,4},{8,11},{9,10},{10,... | collective-permute-start | bytes 393224 | tf_op jit(solution)/shard_map/ppermute | solution.py:20
  29.4 0.1 collective-permute-start.12
  29.4 1.2 %collective-permute-start.11 = (bf16[2,128,256]{2,1,0:T(8,128)(2,1)S(1)}, bf16[2,128,256]{2,1,0:T(8,128)(2,1)S(1)}, u32[]{:S(2)}, u32[]{:S(2)}) collective-permute-start(bf16[2,128,256]{2,1,0:T(8,128)(2,1)S(1)} %pad_maximum_fusion.refs_3_), channel_id=1, source_target_pairs={{0,1},{1,0},{2,3},{3,2},{4,5},{5,4},{6,7},{7,6},{8,9},{9,8},{10,11... | collective-permute-start | bytes 393224 | tf_op jit(solution)/shard_map/ppermute | solution.py:20
  30.7 2.2 %collective-permute-done.13.refs_2_ = bf16[2,128,256]{2,1,0:T(8,128)(2,1)S(1)} collective-permute-done((bf16[2,128,256]{2,1,0:T(8,128)(2,1)S(1)}, bf16[2,128,256]{2,1,0:T(8,128)(2,1)S(1)}, u32[]{:S(2)}, u32[]{:S(2)}) %collective-permute-start.13) | collective-permute-done | bytes 131104 | tf_op jit(solution)/shard_map/ppermute | solution.py:20
  32.9 1.4 %collective-permute-done.12.refs_1_ = bf16[2,128,256]{2,1,0:T(8,128)(2,1)S(1)} collective-permute-done((bf16[2,128,256]{2,1,0:T(8,128)(2,1)S(1)}, bf16[2,128,256]{2,1,0:T(8,128)(2,1)S(1)}, u32[]{:S(2)}, u32[]{:S(2)}) %collective-permute-start.12) | collective-permute-done | bytes 131104 | tf_op jit(solution)/shard_map/ppermute | solution.py:20
  34.3 0.1 collective-permute-done.11.refs_0_
  34.4 0.5 %shard_map.90 = (bf16[128,256]{1,0:T(8,128)(2,1)S(1)}, bf16[128,256]{1,0:T(8,128)(2,1)S(1)}, bf16[128,256]{1,0:T(8,128)(2,1)S(1)}, bf16[128,256]{1,0:T(8,128)(2,1)S(1)}) custom-call(bf16[2,128,256]{2,1,0:T(8,128)(2,1)S(1)} %collective-permute-done.11.refs_0_, bf16[2,128,256]{2,1,0:T(8,128)(2,1)S(1)} %collective-permute-done.12.refs_1_, ...), custom_call_target="tpu_custom_call" | custom-call | flops 268435456 | tf_op jit(solution)/shard_map/pallas_call | solution.py:168
  34.9 1.6 %collective-permute-start.14 = (bf16[128,256]{1,0:T(8,128)(2,1)S(1)}, bf16[128,256]{1,0:T(8,128)(2,1)S(1)}, u32[]{:S(2)}, u32[]{:S(2)}) collective-permute-start(bf16[128,256]{1,0:T(8,128)(2,1)S(1)} %get-tuple-element.37), channel_id=1, source_target_pairs={{0,16},{1,17},{2,18},{3,19},{4,20},{5,21},{6,22},{7,23},{8,24},{9,... | collective-permute-start | bytes 196616 | tf_op jit(solution)/shard_map/ppermute | solution.py:20
  36.5 0.0 collective-permute-start.15
  36.5 0.6 %collective-permute-start.16 = (bf16[128,256]{1,0:T(8,128)(2,1)S(1)}, bf16[128,256]{1,0:T(8,128)(2,1)S(1)}, u32[]{:S(2)}, u32[]{:S(2)}) collective-permute-start(bf16[128,256]{1,0:T(8,128)(2,1)S(1)} %get-tuple-element.39), channel_id=1, source_target_pairs={{0,24},{1,25},{2,26},{3,27},{4,28},{5,29},{6,30},{7,31},{8,16},{9,... | collective-permute-start | bytes 196616 | tf_op jit(solution)/shard_map/ppermute | solution.py:20
  37.1 0.7 %fusion.2 = bf16[1,1,128,256]{3,2,1,0:T(8,128)(2,1)} fusion(f32[128,256]{1,0:T(8,128)S(1)} %get-tuple-element.34), kind=kLoop, calls=%fused_computation.9 | loop fusion | flops 163840 | bytes 196608 | tf_op jit(solution)/shard_map/broadcast_in_dim | solution.py:211
  37.8 1.4 %collective-permute-done.14 = bf16[128,256]{1,0:T(8,128)(2,1)S(1)} collective-permute-done((bf16[128,256]{1,0:T(8,128)(2,1)S(1)}, bf16[128,256]{1,0:T(8,128)(2,1)S(1)}, u32[]{:S(2)}, u32[]{:S(2)}) %collective-permute-start.14) | collective-permute-done | bytes 65568 | tf_op jit(solution)/shard_map/ppermute | solution.py:20
  39.2 0.0 collective-permute-done.15
  39.2 1.0 %collective-permute-done.16 = bf16[128,256]{1,0:T(8,128)(2,1)S(1)} collective-permute-done((bf16[128,256]{1,0:T(8,128)(2,1)S(1)}, bf16[128,256]{1,0:T(8,128)(2,1)S(1)}, u32[]{:S(2)}, u32[]{:S(2)}) %collective-permute-start.16) | collective-permute-done | bytes 65568 | tf_op jit(solution)/shard_map/ppermute | solution.py:20
  40.2 0.8 %fusion = bf16[1,1,128,256]{3,2,1,0:T(8,128)(2,1)} fusion(bf16[256,256]{1,0:T(8,128)(2,1)S(1)} %copy-done, bf16[128,256]{1,0:T(8,128)(2,1)S(1)} %collective-permute-done.16, bf16[128,256]{1,0:T(8,128)(2,1)S(1)} %collective-permute-done.15, bf16[128,256]{1,0:T(8,128)(2,1)S(1)} %collective-permute-done.14, bf16[128,256]{1,0:T(8,128)(2,1)S(1)} %get-tuple-element.36), kind=kOutput, calls=%fused_computation.1 | convolution fusion | flops 17072128 | bytes 458752 | tf_op jit(solution)/shard_map/dot_general | solution.py:210
  (2 shorter events, 0.1 us)
Async XLA Ops:
  0.6 3.0 %copy-start.5 = (s32[1,1,8,3]{2,1,3,0:T(1,128)S(1)}, s32[1,1,8,3]{2,1,3,0:T(1,128)}, u32[]{:S(2)}) copy-start(s32[1,1,8,3]{2,1,3,0:T(1,128)} %param.11) | copy-start | bytes 292
  0.6 3.1 %copy-start.3 = (s32[1,1,8]{2,1,0:T(1,128)S(1)}, s32[1,1,8]{2,1,0:T(1,128)}, u32[]{:S(2)}) copy-start(s32[1,1,8]{2,1,0:T(1,128)} %counts_hbm.1) | copy-start | bytes 100
  0.6 5.5 %collective-permute-start = (bf16[128,256]{1,0:T(8,128)(2,1)}, bf16[128,256]{1,0:T(8,128)(2,1)S(1)}, u32[]{:S(2)}, u32[]{:S(2)}) collective-permute-start(bf16[128,256]{1,0:T(8,128)(2,1)} %bitcast.11), channel_id=1, source_target_pairs={{0,16},{1,17},{2,18},{3,19},{4,20},{5,21},{6,22},{7,23},{8,24},{9,... | collective-permute-start | bytes 196616 | tf_op jit(solution)/shard_map/ppermute | solution.py:20
  3.7 3.3 %collective-permute-start.1 = (bf16[128,256]{1,0:T(8,128)(2,1)}, bf16[128,256]{1,0:T(8,128)(2,1)S(1)}, u32[]{:S(2)}, u32[]{:S(2)}) collective-permute-start(bf16[128,256]{1,0:T(8,128)(2,1)} %bitcast.12), channel_id=1, source_target_pairs={{0,8},{1,9},{2,10},{3,11},{4,12},{5,13},{6,14},{7,15},{8,0},{9,1},... | collective-permute-start | bytes 196616 | tf_op jit(solution)/shard_map/ppermute | solution.py:20
  3.7 1.1 %copy-start.1 = (bf16[1,1,8,3,128,128]{5,4,3,2,1,0:T(8,128)(2,1)S(1)}, bf16[1,1,8,3,128,128]{5,4,3,2,1,0:T(8,128)(2,1)}, u32[]{:S(2)}) copy-start(bf16[1,1,8,3,128,128]{5,4,3,2,1,0:T(8,128)(2,1)} %tiles_hbm.1) | copy-start | bytes 2359300
  4.9 1.6 %copy-start = (bf16[256,256]{1,0:T(8,128)(2,1)S(1)}, bf16[256,256]{1,0:T(8,128)(2,1)}, u32[]{:S(2)}) copy-start(bf16[256,256]{1,0:T(8,128)(2,1)} %refs_2_.3) | copy-start | bytes 393220
  4.9 1.6 %copy-start.2 = (bf16[1,1,128,256]{3,2,1,0:T(8,128)(2,1)S(1)}, bf16[1,1,128,256]{3,2,1,0:T(8,128)(2,1)}, u32[]{:S(2)}) copy-start(bf16[1,1,128,256]{3,2,1,0:T(8,128)(2,1)} %param.7) | copy-start | bytes 196612
  6.1 1.3 %collective-permute-start.2 = (bf16[128,256]{1,0:T(8,128)(2,1)S(1)}, bf16[128,256]{1,0:T(8,128)(2,1)S(1)}, u32[]{:S(2)}, u32[]{:S(2)}) collective-permute-start(bf16[128,256]{1,0:T(8,128)(2,1)S(1)} %collective-permute-done.refs_1_), channel_id=1, source_target_pairs={{0,8},{1,9},{2,10},{3,11},{4,12},{5,13},{6,14},{7,15},{8,0},{9,1},... | collective-permute-start | bytes 196616 | tf_op jit(solution)/shard_map/ppermute | solution.py:20
  7.8 7.5 %collective-permute-start.6 = (bf16[128,256]{1,0:T(8,128)(2,1)S(1)}, bf16[128,256]{1,0:T(8,128)(2,1)S(1)}, u32[]{:S(2)}, u32[]{:S(2)}) collective-permute-start(bf16[128,256]{1,0:T(8,128)(2,1)S(1)} %get-tuple-element.31), channel_id=1, source_target_pairs={{0,3},{1,2},{2,1},{3,0},{4,7},{5,6},{6,5},{7,4},{8,11},{9,10},{10,... | collective-permute-start | bytes 196616 | tf_op jit(solution)/shard_map/ppermute | solution.py:20
  10.9 4.9 %collective-permute-start.7 = (bf16[128,256]{1,0:T(8,128)(2,1)S(1)}, bf16[128,256]{1,0:T(8,128)(2,1)S(1)}, u32[]{:S(2)}, u32[]{:S(2)}) collective-permute-start(bf16[128,256]{1,0:T(8,128)(2,1)S(1)} %get-tuple-element.32), channel_id=1, source_target_pairs={{0,2},{1,3},{2,0},{3,1},{4,6},{5,7},{6,4},{7,5},{8,10},{9,11},{10,... | collective-permute-start | bytes 196616 | tf_op jit(solution)/shard_map/ppermute | solution.py:20
  11.4 5.0 %collective-permute-start.8 = (bf16[128,256]{1,0:T(8,128)(2,1)S(1)}, bf16[128,256]{1,0:T(8,128)(2,1)S(1)}, u32[]{:S(2)}, u32[]{:S(2)}) collective-permute-start(bf16[128,256]{1,0:T(8,128)(2,1)S(1)} %get-tuple-element.33), channel_id=1, source_target_pairs={{0,1},{1,0},{2,3},{3,2},{4,5},{5,4},{6,7},{7,6},{8,9},{9,8},{10,11... | collective-permute-start | bytes 196616 | tf_op jit(solution)/shard_map/ppermute | solution.py:20
  11.9 7.2 %collective-permute-start.3 = (bf16[128,256]{1,0:T(8,128)(2,1)S(1)}, bf16[128,256]{1,0:T(8,128)(2,1)S(1)}, u32[]{:S(2)}, u32[]{:S(2)}) collective-permute-start(bf16[128,256]{1,0:T(8,128)(2,1)S(1)} %get-tuple-element.27), channel_id=1, source_target_pairs={{0,3},{1,2},{2,1},{3,0},{4,7},{5,6},{6,5},{7,4},{8,11},{9,10},{10,... | collective-permute-start | bytes 196616 | tf_op jit(solution)/shard_map/ppermute | solution.py:20
  14.8 4.3 %collective-permute-start.4 = (bf16[128,256]{1,0:T(8,128)(2,1)S(1)}, bf16[128,256]{1,0:T(8,128)(2,1)S(1)}, u32[]{:S(2)}, u32[]{:S(2)}) collective-permute-start(bf16[128,256]{1,0:T(8,128)(2,1)S(1)} %get-tuple-element.28), channel_id=1, source_target_pairs={{0,1},{1,0},{2,3},{3,2},{4,5},{5,4},{6,7},{7,6},{8,9},{9,8},{10,11... | collective-permute-start | bytes 196616 | tf_op jit(solution)/shard_map/ppermute | solution.py:20
  15.3 4.3 %collective-permute-start.5 = (bf16[128,256]{1,0:T(8,128)(2,1)S(1)}, bf16[128,256]{1,0:T(8,128)(2,1)S(1)}, u32[]{:S(2)}, u32[]{:S(2)}) collective-permute-start(bf16[128,256]{1,0:T(8,128)(2,1)S(1)} %get-tuple-element.29), channel_id=1, source_target_pairs={{0,2},{1,3},{2,0},{3,1},{4,6},{5,7},{6,4},{7,5},{8,10},{9,11},{10,... | collective-permute-start | bytes 196616 | tf_op jit(solution)/shard_map/ppermute | solution.py:20
  16.3 5.3 %copy-start.4 = (bf16[1,1,128,256]{3,2,1,0:T(8,128)(2,1)S(1)}, bf16[1,1,128,256]{3,2,1,0:T(8,128)(2,1)}, u32[]{:S(2)}) copy-start(bf16[1,1,128,256]{3,2,1,0:T(8,128)(2,1)} %param.13) | copy-start | bytes 196612
  16.4 5.2 %copy-start.6 = (f32[256]{0:T(256)S(1)}, f32[256]{0:T(256)}, u32[]{:S(2)}) copy-start(f32[256]{0:T(256)} %param.9) | copy-start | bytes 3076
  16.4 5.2 %collective-permute-start.9 = (bf16[128,256]{1,0:T(8,128)(2,1)S(1)}, bf16[128,256]{1,0:T(8,128)(2,1)S(1)}, u32[]{:S(2)}, u32[]{:S(2)}) collective-permute-start(bf16[128,256]{1,0:T(8,128)(2,1)S(1)} %add_convert_fusion.1), channel_id=1, source_target_pairs={{0,4},{1,5},{2,6},{3,7},{4,0},{5,1},{6,2},{7,3},{8,12},{9,13},{10,... | collective-permute-start | bytes 196616 | tf_op jit(solution)/shard_map/ppermute | solution.py:20
  21.7 5.3 %collective-permute-start.10 = (bf16[128,256]{1,0:T(8,128)(2,1)S(1)}, bf16[128,256]{1,0:T(8,128)(2,1)S(1)}, u32[]{:S(2)}, u32[]{:S(2)}) collective-permute-start(bf16[128,256]{1,0:T(8,128)(2,1)S(1)} %get-tuple-element.40), channel_id=1, source_target_pairs={{0,4},{1,5},{2,6},{3,7},{4,0},{5,1},{6,2},{7,3},{8,12},{9,13},{10,... | collective-permute-start | bytes 196616 | tf_op jit(solution)/shard_map/ppermute | solution.py:20
  27.0 5.9 %collective-permute-start.13 = (bf16[2,128,256]{2,1,0:T(8,128)(2,1)S(1)}, bf16[2,128,256]{2,1,0:T(8,128)(2,1)S(1)}, u32[]{:S(2)}, u32[]{:S(2)}) collective-permute-start(bf16[2,128,256]{2,1,0:T(8,128)(2,1)S(1)} %pad_maximum_fusion.refs_3_), channel_id=1, source_target_pairs={{0,3},{1,2},{2,1},{3,0},{4,7},{5,6},{6,5},{7,4},{8,11},{9,10},{10,... | collective-permute-start | bytes 393224 | tf_op jit(solution)/shard_map/ppermute | solution.py:20
  29.4 5.0 %collective-permute-start.12 = (bf16[2,128,256]{2,1,0:T(8,128)(2,1)S(1)}, bf16[2,128,256]{2,1,0:T(8,128)(2,1)S(1)}, u32[]{:S(2)}, u32[]{:S(2)}) collective-permute-start(bf16[2,128,256]{2,1,0:T(8,128)(2,1)S(1)} %pad_maximum_fusion.refs_3_), channel_id=1, source_target_pairs={{0,2},{1,3},{2,0},{3,1},{4,6},{5,7},{6,4},{7,5},{8,10},{9,11},{10,... | collective-permute-start | bytes 393224 | tf_op jit(solution)/shard_map/ppermute | solution.py:20
  29.4 5.0 %collective-permute-start.11 = (bf16[2,128,256]{2,1,0:T(8,128)(2,1)S(1)}, bf16[2,128,256]{2,1,0:T(8,128)(2,1)S(1)}, u32[]{:S(2)}, u32[]{:S(2)}) collective-permute-start(bf16[2,128,256]{2,1,0:T(8,128)(2,1)S(1)} %pad_maximum_fusion.refs_3_), channel_id=1, source_target_pairs={{0,1},{1,0},{2,3},{3,2},{4,5},{5,4},{6,7},{7,6},{8,9},{9,8},{10,11... | collective-permute-start | bytes 393224 | tf_op jit(solution)/shard_map/ppermute | solution.py:20
  34.9 4.3 %collective-permute-start.14 = (bf16[128,256]{1,0:T(8,128)(2,1)S(1)}, bf16[128,256]{1,0:T(8,128)(2,1)S(1)}, u32[]{:S(2)}, u32[]{:S(2)}) collective-permute-start(bf16[128,256]{1,0:T(8,128)(2,1)S(1)} %get-tuple-element.37), channel_id=1, source_target_pairs={{0,16},{1,17},{2,18},{3,19},{4,20},{5,21},{6,22},{7,23},{8,24},{9,... | collective-permute-start | bytes 196616 | tf_op jit(solution)/shard_map/ppermute | solution.py:20
  36.5 2.8 %collective-permute-start.15 = (bf16[128,256]{1,0:T(8,128)(2,1)S(1)}, bf16[128,256]{1,0:T(8,128)(2,1)S(1)}, u32[]{:S(2)}, u32[]{:S(2)}) collective-permute-start(bf16[128,256]{1,0:T(8,128)(2,1)S(1)} %get-tuple-element.38), channel_id=1, source_target_pairs={{0,8},{1,9},{2,10},{3,11},{4,12},{5,13},{6,14},{7,15},{8,0},{9,1},... | collective-permute-start | bytes 196616 | tf_op jit(solution)/shard_map/ppermute | solution.py:20
  36.5 3.7 %collective-permute-start.16 = (bf16[128,256]{1,0:T(8,128)(2,1)S(1)}, bf16[128,256]{1,0:T(8,128)(2,1)S(1)}, u32[]{:S(2)}, u32[]{:S(2)}) collective-permute-start(bf16[128,256]{1,0:T(8,128)(2,1)S(1)} %get-tuple-element.39), channel_id=1, source_target_pairs={{0,24},{1,25},{2,26},{3,27},{4,28},{5,29},{6,30},{7,31},{8,16},{9,... | collective-permute-start | bytes 196616 | tf_op jit(solution)/shard_map/ppermute | solution.py:20

commit v6 on v5

--- a/solution.py
+++ b/solution.py
@@ -150,7 +150,7 @@
 
 def backward_kernel(places, *refs):
     count = len(places)
-    pieces, dense, outs, grads = refs[:count], refs[count], refs[count + 1 : -1], refs[-1]
+    pieces, (dense, weight), outs, grads = refs[:count], refs[count : count + 2], refs[count + 2 : -1], refs[-1]
     tile = pieces[0].shape[1]
     half = grads.shape[0] // 2
     for p, piece in zip(places, pieces):
@@ -160,10 +160,14 @@
         value = lax.dot_general(
             dense[:, j * tile : (j + 1) * tile], grads[...], (((0,), (0,)), ((), ())), preferred_element_type=jnp.float32
         )
+        if j > len(outs) // 2:
+            value = lax.dot_general(
+                value.astype(out.dtype), weight[...], (((1,), (1,)), ((), ())), preferred_element_type=jnp.float32
+            )
         out[...] = value.astype(out.dtype)
 
 
-def backward(places, pieces, dense):
+def backward(places, pieces, dense, weight):
     _, tile, width = pieces[0].shape
     return pl.pallas_call(
         lambda *refs: backward_kernel(places, *refs),
@@ -171,7 +175,7 @@
         scratch_shapes=[pltpu.VMEM((2 * len(pieces) * tile, width), jnp.bfloat16)],
         compiler_params=pltpu.CompilerParams(vmem_limit_bytes=limit(dense.size)),
         cost_estimate=pl.CostEstimate(flops=2 * dense.size * width, bytes_accessed=0, transcendentals=0),
-    )(*pieces, dense)
+    )(*pieces, dense, weight)
 
 
 def shards(features, weight, out_bias, tile_values, tile_cols, tile_counts, cotangent):
@@ -202,13 +206,18 @@
     activated = silu_slope(preact)[0].astype(jnp.bfloat16)
     pair = jnp.stack([grads[0], grads[far]])
     places = [1, 2, 3, 0] if far == 4 else list(range(far))
-    back = backward(places, [swap(pair, col=p) if p else pair for p in places], dense)
+    messages = [swap(pair, col=p) if p else pair for p in places]
+    messages[0], activated = lax.optimization_barrier((messages[0], activated))
+    back = backward(places, messages, dense, weight)
     back = dict(zip([0, *even, *(s for s in rows if s % 2)], back))
     spread = back[0].astype(jnp.float32)
-    for s in ((2, 1, 3) if len(rows) == 3 else rows):
+    for s in (*even, 1):
         spread = spread + swap(back[s], row=s).astype(jnp.float32)
-    feature_grad = jnp.dot(spread.astype(jnp.bfloat16), weight.T, preferred_element_type=jnp.float32)
-    return activated[None, None], feature_grad.astype(jnp.bfloat16)[None, None]
+    ready = jnp.dot(spread.astype(jnp.bfloat16), weight.T, preferred_element_type=jnp.float32)
+    ready = lax.optimization_barrier(ready)
+    for s in even:
+        ready = ready + swap(back[s + 1], row=s + 1).astype(jnp.float32)
+    return activated[None, None], ready.astype(jnp.bfloat16)[None, None]
 
 
 def solution(mesh):

time: 41.2 us -> 41.1 us (level)
  other arithmetic: 0.83 us -> 1.47 us
  matrix products: 0.83 us -> 0.19 us
    convert_element_type x0 -> x1, other arithmetic: none -> 0.67 us  [shards(): activated = silu_slope(preact)[0].astype(jnp.bfloat16)]
    dot_general x1, matrix products: 0.83 us -> 0.19 us  [shards(): jnp.dot(spread.astype(jnp.bfloat16), weight.T, preferred_element_type=jnp...]
  transfers between devices with their start and end apart: 17 -> 17, of which waited for: 11 -> 9; matrix products, arithmetic and copies ran while one was open for 2% -> 2% of each run, Pallas kernels for 4% -> 5%
where the time goes in v6:
time: 41.1 us; the launch traced here: 41 us
  starting transfers between devices  22.3 us (54%)
  waiting for transfers between devices  12.2 us (30%)
  Pallas kernels  2.88 us (7%)
  other arithmetic  1.47 us (4%)
  local copies, waits for them, and re-layouts  1.24 us (3%)
  between operations  0.73 us (2%)
    ppermute x17, starting transfers between devices, swap(): return lax.ppermute(value, BOTH, pairs)  22.3 us
    ppermute x17, waiting for transfers between devices, swap(): return lax.ppermute(value, BOTH, pairs)  12.2 us
    unnamed x15, local copies, waits for them, and re-layouts  1.24 us
    pallas_call x1, Pallas kernels, dense_block(): pl.pallas_call(dense_kernel, in_specs=[HBM] * 3, out_shape=jax.ShapeDtype...  1.16 us
  transfers between devices with their start and end apart: 17, of which 9 were waited for; matrix products, arithmetic and copies ran while one was open for 2% of the time, Pallas kernels for 5%

profile of v6, /device:TPU:0, one launch (start us, length us, event | category | flops | bytes accessed | tf_op | source)
XLA Modules:
  0.0 41.0 jit_solution(16706697905790467077)
XLA Ops:
  0.6 0.0 copy-start.5
  0.6 0.0 copy-start.3
  0.6 3.0 %collective-permute-start = (bf16[128,256]{1,0:T(8,128)(2,1)}, bf16[128,256]{1,0:T(8,128)(2,1)S(1)}, u32[]{:S(2)}, u32[]{:S(2)}) collective-permute-start(bf16[128,256]{1,0:T(8,128)(2,1)} %bitcast.10), channel_id=1, source_target_pairs={{0,16},{1,17},{2,18},{3,19},{4,20},{5,21},{6,22},{7,23},{8,24},{9,... | collective-permute-start | bytes 196616 | tf_op jit(solution)/shard_map/ppermute | solution.py:20
  3.7 0.0 collective-permute-start.1
  3.7 0.0 copy-done.5
  3.7 0.1 copy.9.cols_hbm
  3.7 0.0 copy-done.3
  3.7 0.0 copy-start.1
  3.7 1.1 %copy-done.1 = bf16[1,1,8,3,128,128]{5,4,3,2,1,0:T(8,128)(2,1)S(1)} copy-done((bf16[1,1,8,3,128,128]{5,4,3,2,1,0:T(8,128)(2,1)S(1)}, bf16[1,1,8,3,128,128]{5,4,3,2,1,0:T(8,128)(2,1)}, u32[]{:S(2)}) %copy-start.1) | copy-done | bytes 786456
  4.9 0.0 copy-start
  4.9 0.0 copy-start.2
  4.9 1.2 %shard_map.86.refs_3_.dense.refs_4_ = bf16[1024,512]{1,0:T(8,128)(2,1)S(1)} custom-call(s32[1,1,8,3]{3,2,1,0:T(8,128)S(1)} %copy.9.cols_hbm, s32[1,1,8]{2,1,0:T(1,128)S(1)} %copy-done.3, bf16[1,1,8,3,128,128]{5,4,3,2,1,0:T(8,128)(2,1)S(1)} %copy-done.1), custom_call_target="tpu_custom_call" | custom-call | bytes 786432 | tf_op jit(solution)/shard_map/pallas_call | solution.py:64
  6.1 0.1 collective-permute-done.refs_1_
  6.1 0.5 %collective-permute-start.2 = (bf16[128,256]{1,0:T(8,128)(2,1)S(1)}, bf16[128,256]{1,0:T(8,128)(2,1)S(1)}, u32[]{:S(2)}, u32[]{:S(2)}) collective-permute-start(bf16[128,256]{1,0:T(8,128)(2,1)S(1)} %collective-permute-done.refs_1_), channel_id=1, source_target_pairs={{0,8},{1,9},{2,10},{3,11},{4,12},{5,13},{6,14},{7,15},{8,0},{9,1},... | collective-permute-start | bytes 196616 | tf_op jit(solution)/shard_map/ppermute | solution.py:20
  6.6 0.0 copy-done
  6.6 0.0 copy-done.2
  6.6 0.4 shard_map.87
  7.0 0.0 collective-permute-done.1.refs_0_
  7.0 0.5 %collective-permute-done.2.refs_1_ = bf16[128,256]{1,0:T(8,128)(2,1)S(1)} collective-permute-done((bf16[128,256]{1,0:T(8,128)(2,1)S(1)}, bf16[128,256]{1,0:T(8,128)(2,1)S(1)}, u32[]{:S(2)}, u32[]{:S(2)}) %collective-permute-start.2) | collective-permute-done | bytes 65568 | tf_op jit(solution)/shard_map/ppermute | solution.py:20
  7.5 0.4 shard_map.88
  7.9 3.0 %collective-permute-start.6 = (bf16[128,256]{1,0:T(8,128)(2,1)S(1)}, bf16[128,256]{1,0:T(8,128)(2,1)S(1)}, u32[]{:S(2)}, u32[]{:S(2)}) collective-permute-start(bf16[128,256]{1,0:T(8,128)(2,1)S(1)} %get-tuple-element.33), channel_id=1, source_target_pairs={{0,3},{1,2},{2,1},{3,0},{4,7},{5,6},{6,5},{7,4},{8,11},{9,10},{10,... | collective-permute-start | bytes 196616 | tf_op jit(solution)/shard_map/ppermute | solution.py:20
  10.9 0.4 %collective-permute-start.7 = (bf16[128,256]{1,0:T(8,128)(2,1)S(1)}, bf16[128,256]{1,0:T(8,128)(2,1)S(1)}, u32[]{:S(2)}, u32[]{:S(2)}) collective-permute-start(bf16[128,256]{1,0:T(8,128)(2,1)S(1)} %get-tuple-element.34), channel_id=1, source_target_pairs={{0,2},{1,3},{2,0},{3,1},{4,6},{5,7},{6,4},{7,5},{8,10},{9,11},{10,... | collective-permute-start | bytes 196616 | tf_op jit(solution)/shard_map/ppermute | solution.py:20
  11.4 0.2 collective-permute-start.8
  11.5 0.3 shard_map.89
  11.9 2.9 %collective-permute-start.3 = (bf16[128,256]{1,0:T(8,128)(2,1)S(1)}, bf16[128,256]{1,0:T(8,128)(2,1)S(1)}, u32[]{:S(2)}, u32[]{:S(2)}) collective-permute-start(bf16[128,256]{1,0:T(8,128)(2,1)S(1)} %get-tuple-element.29), channel_id=1, source_target_pairs={{0,3},{1,2},{2,1},{3,0},{4,7},{5,6},{6,5},{7,4},{8,11},{9,10},{10,... | collective-permute-start | bytes 196616 | tf_op jit(solution)/shard_map/ppermute | solution.py:20
  14.8 0.5 %collective-permute-start.4 = (bf16[128,256]{1,0:T(8,128)(2,1)S(1)}, bf16[128,256]{1,0:T(8,128)(2,1)S(1)}, u32[]{:S(2)}, u32[]{:S(2)}) collective-permute-start(bf16[128,256]{1,0:T(8,128)(2,1)S(1)} %get-tuple-element.30), channel_id=1, source_target_pairs={{0,1},{1,0},{2,3},{3,2},{4,5},{5,4},{6,7},{7,6},{8,9},{9,8},{10,11... | collective-permute-start | bytes 196616 | tf_op jit(solution)/shard_map/ppermute | solution.py:20
  15.3 0.0 collective-permute-done.6
  15.3 0.5 %collective-permute-start.5 = (bf16[128,256]{1,0:T(8,128)(2,1)S(1)}, bf16[128,256]{1,0:T(8,128)(2,1)S(1)}, u32[]{:S(2)}, u32[]{:S(2)}) collective-permute-start(bf16[128,256]{1,0:T(8,128)(2,1)S(1)} %get-tuple-element.31), channel_id=1, source_target_pairs={{0,2},{1,3},{2,0},{3,1},{4,6},{5,7},{6,4},{7,5},{8,10},{9,11},{10,... | collective-permute-start | bytes 196616 | tf_op jit(solution)/shard_map/ppermute | solution.py:20
  15.8 0.0 collective-permute-done.7
  15.8 0.5 %collective-permute-done.8 = bf16[128,256]{1,0:T(8,128)(2,1)S(1)} collective-permute-done((bf16[128,256]{1,0:T(8,128)(2,1)S(1)}, bf16[128,256]{1,0:T(8,128)(2,1)S(1)}, u32[]{:S(2)}, u32[]{:S(2)}) %collective-permute-start.8) | collective-permute-done | bytes 65568 | tf_op jit(solution)/shard_map/ppermute | solution.py:20
  16.3 0.0 copy-start.4
  16.4 0.0 copy-start.6
  16.4 2.7 %collective-permute-start.9 = (bf16[128,256]{1,0:T(8,128)(2,1)S(1)}, bf16[128,256]{1,0:T(8,128)(2,1)S(1)}, u32[]{:S(2)}, u32[]{:S(2)}) collective-permute-start(bf16[128,256]{1,0:T(8,128)(2,1)S(1)} %add_convert_fusion.2), channel_id=1, source_target_pairs={{0,4},{1,5},{2,6},{3,7},{4,0},{5,1},{6,2},{7,3},{8,12},{9,13},{10,... | collective-permute-start | bytes 196616 | tf_op jit(solution)/shard_map/ppermute | solution.py:20
  19.0 0.0 collective-permute-done.3
  19.0 0.0 collective-permute-done.4
  19.0 0.5 %collective-permute-done.5 = bf16[128,256]{1,0:T(8,128)(2,1)S(1)} collective-permute-done((bf16[128,256]{1,0:T(8,128)(2,1)S(1)}, bf16[128,256]{1,0:T(8,128)(2,1)S(1)}, u32[]{:S(2)}, u32[]{:S(2)}) %collective-permute-start.5) | collective-permute-done | bytes 65568 | tf_op jit(solution)/shard_map/ppermute | solution.py:20
  19.5 2.1 %collective-permute-done.9 = bf16[128,256]{1,0:T(8,128)(2,1)S(1)} collective-permute-done((bf16[128,256]{1,0:T(8,128)(2,1)S(1)}, bf16[128,256]{1,0:T(8,128)(2,1)S(1)}, u32[]{:S(2)}, u32[]{:S(2)}) %collective-permute-start.9) | collective-permute-done | bytes 65568 | tf_op jit(solution)/shard_map/ppermute | solution.py:20
  21.6 0.0 copy-done.4
  21.6 0.0 copy-done.6
  21.6 0.1 fusion
  21.7 2.7 %collective-permute-start.10 = (bf16[128,256]{1,0:T(8,128)(2,1)S(1)}, bf16[128,256]{1,0:T(8,128)(2,1)S(1)}, u32[]{:S(2)}, u32[]{:S(2)}) collective-permute-start(bf16[128,256]{1,0:T(8,128)(2,1)S(1)} %get-tuple-element.44), channel_id=1, source_target_pairs={{0,4},{1,5},{2,6},{3,7},{4,0},{5,1},{6,2},{7,3},{8,12},{9,13},{10,... | collective-permute-start | bytes 196616 | tf_op jit(solution)/shard_map/ppermute | solution.py:20
  24.4 2.6 %collective-permute-done.10 = bf16[128,256]{1,0:T(8,128)(2,1)S(1)} collective-permute-done((bf16[128,256]{1,0:T(8,128)(2,1)S(1)}, bf16[128,256]{1,0:T(8,128)(2,1)S(1)}, u32[]{:S(2)}, u32[]{:S(2)}) %collective-permute-start.10) | collective-permute-done | bytes 65568 | tf_op jit(solution)/shard_map/ppermute | solution.py:20
  27.0 2.4 %collective-permute-start.13 = (bf16[2,128,256]{2,1,0:T(8,128)(2,1)S(1)}, bf16[2,128,256]{2,1,0:T(8,128)(2,1)S(1)}, u32[]{:S(2)}, u32[]{:S(2)}) collective-permute-start(bf16[2,128,256]{2,1,0:T(8,128)(2,1)S(1)} %pad_maximum_fusion.refs_3_), channel_id=1, source_target_pairs={{0,3},{1,2},{2,1},{3,0},{4,7},{5,6},{6,5},{7,4},{8,11},{9,10},{10,... | collective-permute-start | bytes 393224 | tf_op jit(solution)/shard_map/ppermute | solution.py:20
  29.4 0.1 collective-permute-start.12
  29.4 1.2 %collective-permute-start.11 = (bf16[2,128,256]{2,1,0:T(8,128)(2,1)S(1)}, bf16[2,128,256]{2,1,0:T(8,128)(2,1)S(1)}, u32[]{:S(2)}, u32[]{:S(2)}) collective-permute-start(bf16[2,128,256]{2,1,0:T(8,128)(2,1)S(1)} %pad_maximum_fusion.refs_3_), channel_id=1, source_target_pairs={{0,1},{1,0},{2,3},{3,2},{4,5},{5,4},{6,7},{7,6},{8,9},{9,8},{10,11... | collective-permute-start | bytes 393224 | tf_op jit(solution)/shard_map/ppermute | solution.py:20
  30.7 0.7 %multiply_convert_fusion = bf16[128,256]{1,0:T(8,128)(2,1)} fusion(f32[128,256]{1,0:T(8,128)S(1)} %get-tuple-element.37), kind=kLoop, calls=%fused_computation.5 | loop fusion | flops 163840 | bytes 196608 | tf_op jit(solution)/shard_map/convert_element_type | solution.py:206
  31.4 3.0 %collective-permute-done.11.refs_0_ = bf16[2,128,256]{2,1,0:T(8,128)(2,1)S(1)} collective-permute-done((bf16[2,128,256]{2,1,0:T(8,128)(2,1)S(1)}, bf16[2,128,256]{2,1,0:T(8,128)(2,1)S(1)}, u32[]{:S(2)}, u32[]{:S(2)}) %collective-permute-start.11) | collective-permute-done | bytes 131104 | tf_op jit(solution)/shard_map/ppermute | solution.py:20
  34.4 0.0 collective-permute-done.13.refs_2_
  34.4 0.0 collective-permute-done.12.refs_1_
  34.4 0.6 %shard_map.90 = (bf16[128,256]{1,0:T(8,128)(2,1)S(1)}, bf16[128,256]{1,0:T(8,128)(2,1)S(1)}, bf16[128,256]{1,0:T(8,128)(2,1)S(1)}, bf16[128,256]{1,0:T(8,128)(2,1)S(1)}) custom-call(bf16[2,128,256]{2,1,0:T(8,128)(2,1)S(1)} %collective-permute-done.11.refs_0_, bf16[2,128,256]{2,1,0:T(8,128)(2,1)S(1)} %collective-permute-done.12.refs_1_, ...), custom_call_target="tpu_custom_call" | custom-call | flops 268435456 | tf_op jit(solution)/shard_map/pallas_call | solution.py:172
  35.0 1.6 %collective-permute-start.14 = (bf16[128,256]{1,0:T(8,128)(2,1)S(1)}, bf16[128,256]{1,0:T(8,128)(2,1)S(1)}, u32[]{:S(2)}, u32[]{:S(2)}) collective-permute-start(bf16[128,256]{1,0:T(8,128)(2,1)S(1)} %get-tuple-element.41), channel_id=1, source_target_pairs={{0,16},{1,17},{2,18},{3,19},{4,20},{5,21},{6,22},{7,23},{8,24},{9,... | collective-permute-start | bytes 196616 | tf_op jit(solution)/shard_map/ppermute | solution.py:20
  36.6 0.0 collective-permute-start.15
  36.6 0.6 %collective-permute-start.16 = (bf16[128,256]{1,0:T(8,128)(2,1)S(1)}, bf16[128,256]{1,0:T(8,128)(2,1)S(1)}, u32[]{:S(2)}, u32[]{:S(2)}) collective-permute-start(bf16[128,256]{1,0:T(8,128)(2,1)S(1)} %get-tuple-element.43), channel_id=1, source_target_pairs={{0,24},{1,25},{2,26},{3,27},{4,28},{5,29},{6,30},{7,31},{8,16},{9,... | collective-permute-start | bytes 196616 | tf_op jit(solution)/shard_map/ppermute | solution.py:20
  37.2 2.1 %collective-permute-done.14 = bf16[128,256]{1,0:T(8,128)(2,1)S(1)} collective-permute-done((bf16[128,256]{1,0:T(8,128)(2,1)S(1)}, bf16[128,256]{1,0:T(8,128)(2,1)S(1)}, u32[]{:S(2)}, u32[]{:S(2)}) %collective-permute-start.14) | collective-permute-done | bytes 65568 | tf_op jit(solution)/shard_map/ppermute | solution.py:20
  39.3 0.0 collective-permute-done.15
  39.3 0.2 fusion.1
  39.5 0.8 %collective-permute-done.16 = bf16[128,256]{1,0:T(8,128)(2,1)S(1)} collective-permute-done((bf16[128,256]{1,0:T(8,128)(2,1)S(1)}, bf16[128,256]{1,0:T(8,128)(2,1)S(1)}, u32[]{:S(2)}, u32[]{:S(2)}) %collective-permute-start.16) | collective-permute-done | bytes 65568 | tf_op jit(solution)/shard_map/ppermute | solution.py:20
  40.3 0.6 %fusion.2 = bf16[1,1,128,256]{3,2,1,0:T(8,128)(2,1)} fusion(f32[128,256]{1,0:T(8,128)S(1)} %fusion.1, bf16[128,256]{1,0:T(8,128)(2,1)S(1)} %collective-permute-done.16), kind=kLoop, calls=%fused_computation.9 | loop fusion | flops 98304 | bytes 262144 | tf_op jit(solution)/shard_map/broadcast_in_dim | solution.py:220
  (2 shorter events, 0.1 us)
Async XLA Ops:
  0.6 3.0 %copy-start.5 = (s32[1,1,8,3]{2,1,3,0:T(1,128)S(1)}, s32[1,1,8,3]{2,1,3,0:T(1,128)}, u32[]{:S(2)}) copy-start(s32[1,1,8,3]{2,1,3,0:T(1,128)} %param.11) | copy-start | bytes 292
  0.6 3.1 %copy-start.3 = (s32[1,1,8]{2,1,0:T(1,128)S(1)}, s32[1,1,8]{2,1,0:T(1,128)}, u32[]{:S(2)}) copy-start(s32[1,1,8]{2,1,0:T(1,128)} %counts_hbm.1) | copy-start | bytes 100
  0.6 5.5 %collective-permute-start = (bf16[128,256]{1,0:T(8,128)(2,1)}, bf16[128,256]{1,0:T(8,128)(2,1)S(1)}, u32[]{:S(2)}, u32[]{:S(2)}) collective-permute-start(bf16[128,256]{1,0:T(8,128)(2,1)} %bitcast.10), channel_id=1, source_target_pairs={{0,16},{1,17},{2,18},{3,19},{4,20},{5,21},{6,22},{7,23},{8,24},{9,... | collective-permute-start | bytes 196616 | tf_op jit(solution)/shard_map/ppermute | solution.py:20
  3.7 3.3 %collective-permute-start.1 = (bf16[128,256]{1,0:T(8,128)(2,1)}, bf16[128,256]{1,0:T(8,128)(2,1)S(1)}, u32[]{:S(2)}, u32[]{:S(2)}) collective-permute-start(bf16[128,256]{1,0:T(8,128)(2,1)} %bitcast.11), channel_id=1, source_target_pairs={{0,8},{1,9},{2,10},{3,11},{4,12},{5,13},{6,14},{7,15},{8,0},{9,1},... | collective-permute-start | bytes 196616 | tf_op jit(solution)/shard_map/ppermute | solution.py:20
  3.7 1.1 %copy-start.1 = (bf16[1,1,8,3,128,128]{5,4,3,2,1,0:T(8,128)(2,1)S(1)}, bf16[1,1,8,3,128,128]{5,4,3,2,1,0:T(8,128)(2,1)}, u32[]{:S(2)}) copy-start(bf16[1,1,8,3,128,128]{5,4,3,2,1,0:T(8,128)(2,1)} %tiles_hbm.1) | copy-start | bytes 2359300
  4.9 1.7 %copy-start = (bf16[256,256]{1,0:T(8,128)(2,1)S(1)}, bf16[256,256]{1,0:T(8,128)(2,1)}, u32[]{:S(2)}) copy-start(bf16[256,256]{1,0:T(8,128)(2,1)} %refs_5_.1) | copy-start | bytes 393220
  4.9 1.7 %copy-start.2 = (bf16[1,1,128,256]{3,2,1,0:T(8,128)(2,1)S(1)}, bf16[1,1,128,256]{3,2,1,0:T(8,128)(2,1)}, u32[]{:S(2)}) copy-start(bf16[1,1,128,256]{3,2,1,0:T(8,128)(2,1)} %param.7) | copy-start | bytes 196612
  6.1 1.4 %collective-permute-start.2 = (bf16[128,256]{1,0:T(8,128)(2,1)S(1)}, bf16[128,256]{1,0:T(8,128)(2,1)S(1)}, u32[]{:S(2)}, u32[]{:S(2)}) collective-permute-start(bf16[128,256]{1,0:T(8,128)(2,1)S(1)} %collective-permute-done.refs_1_), channel_id=1, source_target_pairs={{0,8},{1,9},{2,10},{3,11},{4,12},{5,13},{6,14},{7,15},{8,0},{9,1},... | collective-permute-start | bytes 196616 | tf_op jit(solution)/shard_map/ppermute | solution.py:20
  7.9 7.4 %collective-permute-start.6 = (bf16[128,256]{1,0:T(8,128)(2,1)S(1)}, bf16[128,256]{1,0:T(8,128)(2,1)S(1)}, u32[]{:S(2)}, u32[]{:S(2)}) collective-permute-start(bf16[128,256]{1,0:T(8,128)(2,1)S(1)} %get-tuple-element.33), channel_id=1, source_target_pairs={{0,3},{1,2},{2,1},{3,0},{4,7},{5,6},{6,5},{7,4},{8,11},{9,10},{10,... | collective-permute-start | bytes 196616 | tf_op jit(solution)/shard_map/ppermute | solution.py:20
  10.9 4.9 %collective-permute-start.7 = (bf16[128,256]{1,0:T(8,128)(2,1)S(1)}, bf16[128,256]{1,0:T(8,128)(2,1)S(1)}, u32[]{:S(2)}, u32[]{:S(2)}) collective-permute-start(bf16[128,256]{1,0:T(8,128)(2,1)S(1)} %get-tuple-element.34), channel_id=1, source_target_pairs={{0,2},{1,3},{2,0},{3,1},{4,6},{5,7},{6,4},{7,5},{8,10},{9,11},{10,... | collective-permute-start | bytes 196616 | tf_op jit(solution)/shard_map/ppermute | solution.py:20
  11.4 5.0 %collective-permute-start.8 = (bf16[128,256]{1,0:T(8,128)(2,1)S(1)}, bf16[128,256]{1,0:T(8,128)(2,1)S(1)}, u32[]{:S(2)}, u32[]{:S(2)}) collective-permute-start(bf16[128,256]{1,0:T(8,128)(2,1)S(1)} %get-tuple-element.35), channel_id=1, source_target_pairs={{0,1},{1,0},{2,3},{3,2},{4,5},{5,4},{6,7},{7,6},{8,9},{9,8},{10,11... | collective-permute-start | bytes 196616 | tf_op jit(solution)/shard_map/ppermute | solution.py:20
  11.9 7.2 %collective-permute-start.3 = (bf16[128,256]{1,0:T(8,128)(2,1)S(1)}, bf16[128,256]{1,0:T(8,128)(2,1)S(1)}, u32[]{:S(2)}, u32[]{:S(2)}) collective-permute-start(bf16[128,256]{1,0:T(8,128)(2,1)S(1)} %get-tuple-element.29), channel_id=1, source_target_pairs={{0,3},{1,2},{2,1},{3,0},{4,7},{5,6},{6,5},{7,4},{8,11},{9,10},{10,... | collective-permute-start | bytes 196616 | tf_op jit(solution)/shard_map/ppermute | solution.py:20
  14.8 4.3 %collective-permute-start.4 = (bf16[128,256]{1,0:T(8,128)(2,1)S(1)}, bf16[128,256]{1,0:T(8,128)(2,1)S(1)}, u32[]{:S(2)}, u32[]{:S(2)}) collective-permute-start(bf16[128,256]{1,0:T(8,128)(2,1)S(1)} %get-tuple-element.30), channel_id=1, source_target_pairs={{0,1},{1,0},{2,3},{3,2},{4,5},{5,4},{6,7},{7,6},{8,9},{9,8},{10,11... | collective-permute-start | bytes 196616 | tf_op jit(solution)/shard_map/ppermute | solution.py:20
  15.3 4.3 %collective-permute-start.5 = (bf16[128,256]{1,0:T(8,128)(2,1)S(1)}, bf16[128,256]{1,0:T(8,128)(2,1)S(1)}, u32[]{:S(2)}, u32[]{:S(2)}) collective-permute-start(bf16[128,256]{1,0:T(8,128)(2,1)S(1)} %get-tuple-element.31), channel_id=1, source_target_pairs={{0,2},{1,3},{2,0},{3,1},{4,6},{5,7},{6,4},{7,5},{8,10},{9,11},{10,... | collective-permute-start | bytes 196616 | tf_op jit(solution)/shard_map/ppermute | solution.py:20
  16.3 5.3 %copy-start.4 = (bf16[1,1,128,256]{3,2,1,0:T(8,128)(2,1)S(1)}, bf16[1,1,128,256]{3,2,1,0:T(8,128)(2,1)}, u32[]{:S(2)}) copy-start(bf16[1,1,128,256]{3,2,1,0:T(8,128)(2,1)} %param.13) | copy-start | bytes 196612
  16.4 5.2 %copy-start.6 = (f32[256]{0:T(256)S(1)}, f32[256]{0:T(256)}, u32[]{:S(2)}) copy-start(f32[256]{0:T(256)} %param.9) | copy-start | bytes 3076
  16.4 5.2 %collective-permute-start.9 = (bf16[128,256]{1,0:T(8,128)(2,1)S(1)}, bf16[128,256]{1,0:T(8,128)(2,1)S(1)}, u32[]{:S(2)}, u32[]{:S(2)}) collective-permute-start(bf16[128,256]{1,0:T(8,128)(2,1)S(1)} %add_convert_fusion.2), channel_id=1, source_target_pairs={{0,4},{1,5},{2,6},{3,7},{4,0},{5,1},{6,2},{7,3},{8,12},{9,13},{10,... | collective-permute-start | bytes 196616 | tf_op jit(solution)/shard_map/ppermute | solution.py:20
  21.7 5.3 %collective-permute-start.10 = (bf16[128,256]{1,0:T(8,128)(2,1)S(1)}, bf16[128,256]{1,0:T(8,128)(2,1)S(1)}, u32[]{:S(2)}, u32[]{:S(2)}) collective-permute-start(bf16[128,256]{1,0:T(8,128)(2,1)S(1)} %get-tuple-element.44), channel_id=1, source_target_pairs={{0,4},{1,5},{2,6},{3,7},{4,0},{5,1},{6,2},{7,3},{8,12},{9,13},{10,... | collective-permute-start | bytes 196616 | tf_op jit(solution)/shard_map/ppermute | solution.py:20
  27.0 7.4 %collective-permute-start.13 = (bf16[2,128,256]{2,1,0:T(8,128)(2,1)S(1)}, bf16[2,128,256]{2,1,0:T(8,128)(2,1)S(1)}, u32[]{:S(2)}, u32[]{:S(2)}) collective-permute-start(bf16[2,128,256]{2,1,0:T(8,128)(2,1)S(1)} %pad_maximum_fusion.refs_3_), channel_id=1, source_target_pairs={{0,3},{1,2},{2,1},{3,0},{4,7},{5,6},{6,5},{7,4},{8,11},{9,10},{10,... | collective-permute-start | bytes 393224 | tf_op jit(solution)/shard_map/ppermute | solution.py:20
  29.4 5.0 %collective-permute-start.12 = (bf16[2,128,256]{2,1,0:T(8,128)(2,1)S(1)}, bf16[2,128,256]{2,1,0:T(8,128)(2,1)S(1)}, u32[]{:S(2)}, u32[]{:S(2)}) collective-permute-start(bf16[2,128,256]{2,1,0:T(8,128)(2,1)S(1)} %pad_maximum_fusion.refs_3_), channel_id=1, source_target_pairs={{0,2},{1,3},{2,0},{3,1},{4,6},{5,7},{6,4},{7,5},{8,10},{9,11},{10,... | collective-permute-start | bytes 393224 | tf_op jit(solution)/shard_map/ppermute | solution.py:20
  29.4 5.0 %collective-permute-start.11 = (bf16[2,128,256]{2,1,0:T(8,128)(2,1)S(1)}, bf16[2,128,256]{2,1,0:T(8,128)(2,1)S(1)}, u32[]{:S(2)}, u32[]{:S(2)}) collective-permute-start(bf16[2,128,256]{2,1,0:T(8,128)(2,1)S(1)} %pad_maximum_fusion.refs_3_), channel_id=1, source_target_pairs={{0,1},{1,0},{2,3},{3,2},{4,5},{5,4},{6,7},{7,6},{8,9},{9,8},{10,11... | collective-permute-start | bytes 393224 | tf_op jit(solution)/shard_map/ppermute | solution.py:20
  35.0 4.3 %collective-permute-start.14 = (bf16[128,256]{1,0:T(8,128)(2,1)S(1)}, bf16[128,256]{1,0:T(8,128)(2,1)S(1)}, u32[]{:S(2)}, u32[]{:S(2)}) collective-permute-start(bf16[128,256]{1,0:T(8,128)(2,1)S(1)} %get-tuple-element.41), channel_id=1, source_target_pairs={{0,16},{1,17},{2,18},{3,19},{4,20},{5,21},{6,22},{7,23},{8,24},{9,... | collective-permute-start | bytes 196616 | tf_op jit(solution)/shard_map/ppermute | solution.py:20
  36.6 2.8 %collective-permute-start.15 = (bf16[128,256]{1,0:T(8,128)(2,1)S(1)}, bf16[128,256]{1,0:T(8,128)(2,1)S(1)}, u32[]{:S(2)}, u32[]{:S(2)}) collective-permute-start(bf16[128,256]{1,0:T(8,128)(2,1)S(1)} %get-tuple-element.42), channel_id=1, source_target_pairs={{0,8},{1,9},{2,10},{3,11},{4,12},{5,13},{6,14},{7,15},{8,0},{9,1},... | collective-permute-start | bytes 196616 | tf_op jit(solution)/shard_map/ppermute | solution.py:20
  36.6 3.7 %collective-permute-start.16 = (bf16[128,256]{1,0:T(8,128)(2,1)S(1)}, bf16[128,256]{1,0:T(8,128)(2,1)S(1)}, u32[]{:S(2)}, u32[]{:S(2)}) collective-permute-start(bf16[128,256]{1,0:T(8,128)(2,1)S(1)} %get-tuple-element.43), channel_id=1, source_target_pairs={{0,24},{1,25},{2,26},{3,27},{4,28},{5,29},{6,30},{7,31},{8,16},{9,... | collective-permute-start | bytes 196616 | tf_op jit(solution)/shard_map/ppermute | solution.py:20

commit v7 on v6

--- a/solution.py
+++ b/solution.py
@@ -156,15 +156,18 @@
     for p, piece in zip(places, pieces):
         grads[p * tile : (p + 1) * tile] = piece[0]
         grads[half + p * tile : half + (p + 1) * tile] = piece[1]
+    values = [
+        lax.dot_general(
+            dense[:, j * tile : (j + 1) * tile], grads[...], (((0,), (0,)), ((), ())), preferred_element_type=jnp.float32
+        ).astype(outs[0].dtype)
+        for j in range(len(outs))
+    ]
     for j, out in enumerate(outs):
-        value = lax.dot_general(
-            dense[:, j * tile : (j + 1) * tile], grads[...], (((0,), (0,)), ((), ())), preferred_element_type=jnp.float32
-        )
         if j > len(outs) // 2:
-            value = lax.dot_general(
-                value.astype(out.dtype), weight[...], (((1,), (1,)), ((), ())), preferred_element_type=jnp.float32
-            )
-        out[...] = value.astype(out.dtype)
+            value = lax.dot_general(values[j], weight[...], (((1,), (1,)), ((), ())), preferred_element_type=jnp.float32)
+            out[...] = value.astype(out.dtype)
+        else:
+            out[...] = values[j]
 
 
 def backward(places, pieces, dense, weight):

time: 41.1 us -> 41.1 us (level)
  transfers between devices with their start and end apart: 17 -> 17, of which waited for: 9 -> 9; matrix products, arithmetic and copies ran while one was open for 2% -> 2% of each run, Pallas kernels for 5% -> 4%
where the time goes in v7:
time: 41.1 us; the launch traced here: 41 us
  starting transfers between devices  22.3 us (54%)
  waiting for transfers between devices  12.2 us (30%)
  Pallas kernels  2.82 us (7%)
  other arithmetic  1.47 us (4%)
  local copies, waits for them, and re-layouts  1.24 us (3%)
  between operations  0.73 us (2%)
    ppermute x17, starting transfers between devices, swap(): return lax.ppermute(value, BOTH, pairs)  22.3 us
    ppermute x17, waiting for transfers between devices, swap(): return lax.ppermute(value, BOTH, pairs)  12.2 us
    unnamed x15, local copies, waits for them, and re-layouts  1.24 us
    pallas_call x1, Pallas kernels, dense_block(): pl.pallas_call(dense_kernel, in_specs=[HBM] * 3, out_shape=jax.ShapeDtype...  1.11 us
  transfers between devices with their start and end apart: 17, of which 9 were waited for; matrix products, arithmetic and copies ran while one was open for 2% of the time, Pallas kernels for 4%

profile of v7, /device:TPU:0, one launch (start us, length us, event | category | flops | bytes accessed | tf_op | source)
XLA Modules:
  0.0 41.0 jit_solution(16706697905790467077)
XLA Ops:
  0.6 0.0 copy-start.5
  0.6 0.0 copy-start.3
  0.6 3.0 %collective-permute-start = (bf16[128,256]{1,0:T(8,128)(2,1)}, bf16[128,256]{1,0:T(8,128)(2,1)S(1)}, u32[]{:S(2)}, u32[]{:S(2)}) collective-permute-start(bf16[128,256]{1,0:T(8,128)(2,1)} %bitcast.10), channel_id=1, source_target_pairs={{0,16},{1,17},{2,18},{3,19},{4,20},{5,21},{6,22},{7,23},{8,24},{9,... | collective-permute-start | bytes 196616 | tf_op jit(solution)/shard_map/ppermute | solution.py:20
  3.7 0.0 collective-permute-start.1
  3.7 0.0 copy-done.5
  3.7 0.1 copy.9.cols_hbm
  3.7 0.0 copy-done.3
  3.7 0.0 copy-start.1
  3.7 1.1 %copy-done.1 = bf16[1,1,8,3,128,128]{5,4,3,2,1,0:T(8,128)(2,1)S(1)} copy-done((bf16[1,1,8,3,128,128]{5,4,3,2,1,0:T(8,128)(2,1)S(1)}, bf16[1,1,8,3,128,128]{5,4,3,2,1,0:T(8,128)(2,1)}, u32[]{:S(2)}) %copy-start.1) | copy-done | bytes 786456
  4.9 0.0 copy-start
  4.9 0.0 copy-start.2
  4.9 1.1 %shard_map.86.refs_3_.dense.refs_4_ = bf16[1024,512]{1,0:T(8,128)(2,1)S(1)} custom-call(s32[1,1,8,3]{3,2,1,0:T(8,128)S(1)} %copy.9.cols_hbm, s32[1,1,8]{2,1,0:T(1,128)S(1)} %copy-done.3, bf16[1,1,8,3,128,128]{5,4,3,2,1,0:T(8,128)(2,1)S(1)} %copy-done.1), custom_call_target="tpu_custom_call" | custom-call | bytes 786432 | tf_op jit(solution)/shard_map/pallas_call | solution.py:64
  6.0 0.1 collective-permute-done.refs_1_
  6.1 0.4 %collective-permute-start.2 = (bf16[128,256]{1,0:T(8,128)(2,1)S(1)}, bf16[128,256]{1,0:T(8,128)(2,1)S(1)}, u32[]{:S(2)}, u32[]{:S(2)}) collective-permute-start(bf16[128,256]{1,0:T(8,128)(2,1)S(1)} %collective-permute-done.refs_1_), channel_id=1, source_target_pairs={{0,8},{1,9},{2,10},{3,11},{4,12},{5,13},{6,14},{7,15},{8,0},{9,1},... | collective-permute-start | bytes 196616 | tf_op jit(solution)/shard_map/ppermute | solution.py:20
  6.6 0.0 copy-done
  6.6 0.0 copy-done.2
  6.6 0.4 shard_map.87
  7.0 0.0 collective-permute-done.1.refs_0_
  7.0 0.5 %collective-permute-done.2.refs_1_ = bf16[128,256]{1,0:T(8,128)(2,1)S(1)} collective-permute-done((bf16[128,256]{1,0:T(8,128)(2,1)S(1)}, bf16[128,256]{1,0:T(8,128)(2,1)S(1)}, u32[]{:S(2)}, u32[]{:S(2)}) %collective-permute-start.2) | collective-permute-done | bytes 65568 | tf_op jit(solution)/shard_map/ppermute | solution.py:20
  7.5 0.4 shard_map.88
  7.9 3.0 %collective-permute-start.6 = (bf16[128,256]{1,0:T(8,128)(2,1)S(1)}, bf16[128,256]{1,0:T(8,128)(2,1)S(1)}, u32[]{:S(2)}, u32[]{:S(2)}) collective-permute-start(bf16[128,256]{1,0:T(8,128)(2,1)S(1)} %get-tuple-element.33), channel_id=1, source_target_pairs={{0,3},{1,2},{2,1},{3,0},{4,7},{5,6},{6,5},{7,4},{8,11},{9,10},{10,... | collective-permute-start | bytes 196616 | tf_op jit(solution)/shard_map/ppermute | solution.py:20
  10.9 0.4 %collective-permute-start.7 = (bf16[128,256]{1,0:T(8,128)(2,1)S(1)}, bf16[128,256]{1,0:T(8,128)(2,1)S(1)}, u32[]{:S(2)}, u32[]{:S(2)}) collective-permute-start(bf16[128,256]{1,0:T(8,128)(2,1)S(1)} %get-tuple-element.34), channel_id=1, source_target_pairs={{0,2},{1,3},{2,0},{3,1},{4,6},{5,7},{6,4},{7,5},{8,10},{9,11},{10,... | collective-permute-start | bytes 196616 | tf_op jit(solution)/shard_map/ppermute | solution.py:20
  11.4 0.2 collective-permute-start.8
  11.5 0.3 shard_map.89
  11.9 2.9 %collective-permute-start.3 = (bf16[128,256]{1,0:T(8,128)(2,1)S(1)}, bf16[128,256]{1,0:T(8,128)(2,1)S(1)}, u32[]{:S(2)}, u32[]{:S(2)}) collective-permute-start(bf16[128,256]{1,0:T(8,128)(2,1)S(1)} %get-tuple-element.29), channel_id=1, source_target_pairs={{0,3},{1,2},{2,1},{3,0},{4,7},{5,6},{6,5},{7,4},{8,11},{9,10},{10,... | collective-permute-start | bytes 196616 | tf_op jit(solution)/shard_map/ppermute | solution.py:20
  14.8 0.5 %collective-permute-start.4 = (bf16[128,256]{1,0:T(8,128)(2,1)S(1)}, bf16[128,256]{1,0:T(8,128)(2,1)S(1)}, u32[]{:S(2)}, u32[]{:S(2)}) collective-permute-start(bf16[128,256]{1,0:T(8,128)(2,1)S(1)} %get-tuple-element.30), channel_id=1, source_target_pairs={{0,1},{1,0},{2,3},{3,2},{4,5},{5,4},{6,7},{7,6},{8,9},{9,8},{10,11... | collective-permute-start | bytes 196616 | tf_op jit(solution)/shard_map/ppermute | solution.py:20
  15.3 0.0 collective-permute-done.6
  15.3 0.5 %collective-permute-start.5 = (bf16[128,256]{1,0:T(8,128)(2,1)S(1)}, bf16[128,256]{1,0:T(8,128)(2,1)S(1)}, u32[]{:S(2)}, u32[]{:S(2)}) collective-permute-start(bf16[128,256]{1,0:T(8,128)(2,1)S(1)} %get-tuple-element.31), channel_id=1, source_target_pairs={{0,2},{1,3},{2,0},{3,1},{4,6},{5,7},{6,4},{7,5},{8,10},{9,11},{10,... | collective-permute-start | bytes 196616 | tf_op jit(solution)/shard_map/ppermute | solution.py:20
  15.8 0.0 collective-permute-done.7
  15.8 0.5 %collective-permute-done.8 = bf16[128,256]{1,0:T(8,128)(2,1)S(1)} collective-permute-done((bf16[128,256]{1,0:T(8,128)(2,1)S(1)}, bf16[128,256]{1,0:T(8,128)(2,1)S(1)}, u32[]{:S(2)}, u32[]{:S(2)}) %collective-permute-start.8) | collective-permute-done | bytes 65568 | tf_op jit(solution)/shard_map/ppermute | solution.py:20
  16.3 0.0 copy-start.4
  16.4 0.0 copy-start.6
  16.4 2.7 %collective-permute-start.9 = (bf16[128,256]{1,0:T(8,128)(2,1)S(1)}, bf16[128,256]{1,0:T(8,128)(2,1)S(1)}, u32[]{:S(2)}, u32[]{:S(2)}) collective-permute-start(bf16[128,256]{1,0:T(8,128)(2,1)S(1)} %add_convert_fusion.2), channel_id=1, source_target_pairs={{0,4},{1,5},{2,6},{3,7},{4,0},{5,1},{6,2},{7,3},{8,12},{9,13},{10,... | collective-permute-start | bytes 196616 | tf_op jit(solution)/shard_map/ppermute | solution.py:20
  19.0 0.0 collective-permute-done.3
  19.0 0.0 collective-permute-done.4
  19.0 0.5 %collective-permute-done.5 = bf16[128,256]{1,0:T(8,128)(2,1)S(1)} collective-permute-done((bf16[128,256]{1,0:T(8,128)(2,1)S(1)}, bf16[128,256]{1,0:T(8,128)(2,1)S(1)}, u32[]{:S(2)}, u32[]{:S(2)}) %collective-permute-start.5) | collective-permute-done | bytes 65568 | tf_op jit(solution)/shard_map/ppermute | solution.py:20
  19.5 2.1 %collective-permute-done.9 = bf16[128,256]{1,0:T(8,128)(2,1)S(1)} collective-permute-done((bf16[128,256]{1,0:T(8,128)(2,1)S(1)}, bf16[128,256]{1,0:T(8,128)(2,1)S(1)}, u32[]{:S(2)}, u32[]{:S(2)}) %collective-permute-start.9) | collective-permute-done | bytes 65568 | tf_op jit(solution)/shard_map/ppermute | solution.py:20
  21.6 0.0 copy-done.4
  21.6 0.0 copy-done.6
  21.6 0.1 fusion
  21.7 2.7 %collective-permute-start.10 = (bf16[128,256]{1,0:T(8,128)(2,1)S(1)}, bf16[128,256]{1,0:T(8,128)(2,1)S(1)}, u32[]{:S(2)}, u32[]{:S(2)}) collective-permute-start(bf16[128,256]{1,0:T(8,128)(2,1)S(1)} %get-tuple-element.44), channel_id=1, source_target_pairs={{0,4},{1,5},{2,6},{3,7},{4,0},{5,1},{6,2},{7,3},{8,12},{9,13},{10,... | collective-permute-start | bytes 196616 | tf_op jit(solution)/shard_map/ppermute | solution.py:20
  24.4 2.6 %collective-permute-done.10 = bf16[128,256]{1,0:T(8,128)(2,1)S(1)} collective-permute-done((bf16[128,256]{1,0:T(8,128)(2,1)S(1)}, bf16[128,256]{1,0:T(8,128)(2,1)S(1)}, u32[]{:S(2)}, u32[]{:S(2)}) %collective-permute-start.10) | collective-permute-done | bytes 65568 | tf_op jit(solution)/shard_map/ppermute | solution.py:20
  27.0 2.4 %collective-permute-start.13 = (bf16[2,128,256]{2,1,0:T(8,128)(2,1)S(1)}, bf16[2,128,256]{2,1,0:T(8,128)(2,1)S(1)}, u32[]{:S(2)}, u32[]{:S(2)}) collective-permute-start(bf16[2,128,256]{2,1,0:T(8,128)(2,1)S(1)} %pad_maximum_fusion.refs_3_), channel_id=1, source_target_pairs={{0,3},{1,2},{2,1},{3,0},{4,7},{5,6},{6,5},{7,4},{8,11},{9,10},{10,... | collective-permute-start | bytes 393224 | tf_op jit(solution)/shard_map/ppermute | solution.py:20
  29.4 0.1 collective-permute-start.12
  29.4 1.2 %collective-permute-start.11 = (bf16[2,128,256]{2,1,0:T(8,128)(2,1)S(1)}, bf16[2,128,256]{2,1,0:T(8,128)(2,1)S(1)}, u32[]{:S(2)}, u32[]{:S(2)}) collective-permute-start(bf16[2,128,256]{2,1,0:T(8,128)(2,1)S(1)} %pad_maximum_fusion.refs_3_), channel_id=1, source_target_pairs={{0,1},{1,0},{2,3},{3,2},{4,5},{5,4},{6,7},{7,6},{8,9},{9,8},{10,11... | collective-permute-start | bytes 393224 | tf_op jit(solution)/shard_map/ppermute | solution.py:20
  30.7 0.7 %multiply_convert_fusion = bf16[128,256]{1,0:T(8,128)(2,1)} fusion(f32[128,256]{1,0:T(8,128)S(1)} %get-tuple-element.37), kind=kLoop, calls=%fused_computation.5 | loop fusion | flops 163840 | bytes 196608 | tf_op jit(solution)/shard_map/convert_element_type | solution.py:209
  31.4 3.0 %collective-permute-done.11.refs_0_ = bf16[2,128,256]{2,1,0:T(8,128)(2,1)S(1)} collective-permute-done((bf16[2,128,256]{2,1,0:T(8,128)(2,1)S(1)}, bf16[2,128,256]{2,1,0:T(8,128)(2,1)S(1)}, u32[]{:S(2)}, u32[]{:S(2)}) %collective-permute-start.11) | collective-permute-done | bytes 131104 | tf_op jit(solution)/shard_map/ppermute | solution.py:20
  34.4 0.0 collective-permute-done.13.refs_2_
  34.4 0.0 collective-permute-done.12.refs_1_
  34.4 0.6 %shard_map.90 = (bf16[128,256]{1,0:T(8,128)(2,1)S(1)}, bf16[128,256]{1,0:T(8,128)(2,1)S(1)}, bf16[128,256]{1,0:T(8,128)(2,1)S(1)}, bf16[128,256]{1,0:T(8,128)(2,1)S(1)}) custom-call(bf16[2,128,256]{2,1,0:T(8,128)(2,1)S(1)} %collective-permute-done.11.refs_0_, bf16[2,128,256]{2,1,0:T(8,128)(2,1)S(1)} %collective-permute-done.12.refs_1_, ...), custom_call_target="tpu_custom_call" | custom-call | flops 268435456 | tf_op jit(solution)/shard_map/pallas_call | solution.py:175
  35.0 1.6 %collective-permute-start.14 = (bf16[128,256]{1,0:T(8,128)(2,1)S(1)}, bf16[128,256]{1,0:T(8,128)(2,1)S(1)}, u32[]{:S(2)}, u32[]{:S(2)}) collective-permute-start(bf16[128,256]{1,0:T(8,128)(2,1)S(1)} %get-tuple-element.41), channel_id=1, source_target_pairs={{0,16},{1,17},{2,18},{3,19},{4,20},{5,21},{6,22},{7,23},{8,24},{9,... | collective-permute-start | bytes 196616 | tf_op jit(solution)/shard_map/ppermute | solution.py:20
  36.6 0.0 collective-permute-start.15
  36.6 0.6 %collective-permute-start.16 = (bf16[128,256]{1,0:T(8,128)(2,1)S(1)}, bf16[128,256]{1,0:T(8,128)(2,1)S(1)}, u32[]{:S(2)}, u32[]{:S(2)}) collective-permute-start(bf16[128,256]{1,0:T(8,128)(2,1)S(1)} %get-tuple-element.43), channel_id=1, source_target_pairs={{0,24},{1,25},{2,26},{3,27},{4,28},{5,29},{6,30},{7,31},{8,16},{9,... | collective-permute-start | bytes 196616 | tf_op jit(solution)/shard_map/ppermute | solution.py:20
  37.2 2.1 %collective-permute-done.14 = bf16[128,256]{1,0:T(8,128)(2,1)S(1)} collective-permute-done((bf16[128,256]{1,0:T(8,128)(2,1)S(1)}, bf16[128,256]{1,0:T(8,128)(2,1)S(1)}, u32[]{:S(2)}, u32[]{:S(2)}) %collective-permute-start.14) | collective-permute-done | bytes 65568 | tf_op jit(solution)/shard_map/ppermute | solution.py:20
  39.3 0.0 collective-permute-done.15
  39.3 0.2 fusion.1
  39.5 0.8 %collective-permute-done.16 = bf16[128,256]{1,0:T(8,128)(2,1)S(1)} collective-permute-done((bf16[128,256]{1,0:T(8,128)(2,1)S(1)}, bf16[128,256]{1,0:T(8,128)(2,1)S(1)}, u32[]{:S(2)}, u32[]{:S(2)}) %collective-permute-start.16) | collective-permute-done | bytes 65568 | tf_op jit(solution)/shard_map/ppermute | solution.py:20
  40.3 0.6 %fusion.2 = bf16[1,1,128,256]{3,2,1,0:T(8,128)(2,1)} fusion(f32[128,256]{1,0:T(8,128)S(1)} %fusion.1, bf16[128,256]{1,0:T(8,128)(2,1)S(1)} %collective-permute-done.16), kind=kLoop, calls=%fused_computation.9 | loop fusion | flops 98304 | bytes 262144 | tf_op jit(solution)/shard_map/broadcast_in_dim | solution.py:223
  (2 shorter events, 0.1 us)
Async XLA Ops:
  0.6 3.0 %copy-start.5 = (s32[1,1,8,3]{2,1,3,0:T(1,128)S(1)}, s32[1,1,8,3]{2,1,3,0:T(1,128)}, u32[]{:S(2)}) copy-start(s32[1,1,8,3]{2,1,3,0:T(1,128)} %param.11) | copy-start | bytes 292
  0.6 3.1 %copy-start.3 = (s32[1,1,8]{2,1,0:T(1,128)S(1)}, s32[1,1,8]{2,1,0:T(1,128)}, u32[]{:S(2)}) copy-start(s32[1,1,8]{2,1,0:T(1,128)} %counts_hbm.1) | copy-start | bytes 100
  0.6 5.5 %collective-permute-start = (bf16[128,256]{1,0:T(8,128)(2,1)}, bf16[128,256]{1,0:T(8,128)(2,1)S(1)}, u32[]{:S(2)}, u32[]{:S(2)}) collective-permute-start(bf16[128,256]{1,0:T(8,128)(2,1)} %bitcast.10), channel_id=1, source_target_pairs={{0,16},{1,17},{2,18},{3,19},{4,20},{5,21},{6,22},{7,23},{8,24},{9,... | collective-permute-start | bytes 196616 | tf_op jit(solution)/shard_map/ppermute | solution.py:20
  3.7 3.3 %collective-permute-start.1 = (bf16[128,256]{1,0:T(8,128)(2,1)}, bf16[128,256]{1,0:T(8,128)(2,1)S(1)}, u32[]{:S(2)}, u32[]{:S(2)}) collective-permute-start(bf16[128,256]{1,0:T(8,128)(2,1)} %bitcast.11), channel_id=1, source_target_pairs={{0,8},{1,9},{2,10},{3,11},{4,12},{5,13},{6,14},{7,15},{8,0},{9,1},... | collective-permute-start | bytes 196616 | tf_op jit(solution)/shard_map/ppermute | solution.py:20
  3.7 1.1 %copy-start.1 = (bf16[1,1,8,3,128,128]{5,4,3,2,1,0:T(8,128)(2,1)S(1)}, bf16[1,1,8,3,128,128]{5,4,3,2,1,0:T(8,128)(2,1)}, u32[]{:S(2)}) copy-start(bf16[1,1,8,3,128,128]{5,4,3,2,1,0:T(8,128)(2,1)} %tiles_hbm.1) | copy-start | bytes 2359300
  4.9 1.7 %copy-start = (bf16[256,256]{1,0:T(8,128)(2,1)S(1)}, bf16[256,256]{1,0:T(8,128)(2,1)}, u32[]{:S(2)}) copy-start(bf16[256,256]{1,0:T(8,128)(2,1)} %refs_5_.1) | copy-start | bytes 393220
  4.9 1.7 %copy-start.2 = (bf16[1,1,128,256]{3,2,1,0:T(8,128)(2,1)S(1)}, bf16[1,1,128,256]{3,2,1,0:T(8,128)(2,1)}, u32[]{:S(2)}) copy-start(bf16[1,1,128,256]{3,2,1,0:T(8,128)(2,1)} %param.7) | copy-start | bytes 196612
  6.1 1.3 %collective-permute-start.2 = (bf16[128,256]{1,0:T(8,128)(2,1)S(1)}, bf16[128,256]{1,0:T(8,128)(2,1)S(1)}, u32[]{:S(2)}, u32[]{:S(2)}) collective-permute-start(bf16[128,256]{1,0:T(8,128)(2,1)S(1)} %collective-permute-done.refs_1_), channel_id=1, source_target_pairs={{0,8},{1,9},{2,10},{3,11},{4,12},{5,13},{6,14},{7,15},{8,0},{9,1},... | collective-permute-start | bytes 196616 | tf_op jit(solution)/shard_map/ppermute | solution.py:20
  7.9 7.4 %collective-permute-start.6 = (bf16[128,256]{1,0:T(8,128)(2,1)S(1)}, bf16[128,256]{1,0:T(8,128)(2,1)S(1)}, u32[]{:S(2)}, u32[]{:S(2)}) collective-permute-start(bf16[128,256]{1,0:T(8,128)(2,1)S(1)} %get-tuple-element.33), channel_id=1, source_target_pairs={{0,3},{1,2},{2,1},{3,0},{4,7},{5,6},{6,5},{7,4},{8,11},{9,10},{10,... | collective-permute-start | bytes 196616 | tf_op jit(solution)/shard_map/ppermute | solution.py:20
  10.9 4.9 %collective-permute-start.7 = (bf16[128,256]{1,0:T(8,128)(2,1)S(1)}, bf16[128,256]{1,0:T(8,128)(2,1)S(1)}, u32[]{:S(2)}, u32[]{:S(2)}) collective-permute-start(bf16[128,256]{1,0:T(8,128)(2,1)S(1)} %get-tuple-element.34), channel_id=1, source_target_pairs={{0,2},{1,3},{2,0},{3,1},{4,6},{5,7},{6,4},{7,5},{8,10},{9,11},{10,... | collective-permute-start | bytes 196616 | tf_op jit(solution)/shard_map/ppermute | solution.py:20
  11.4 5.0 %collective-permute-start.8 = (bf16[128,256]{1,0:T(8,128)(2,1)S(1)}, bf16[128,256]{1,0:T(8,128)(2,1)S(1)}, u32[]{:S(2)}, u32[]{:S(2)}) collective-permute-start(bf16[128,256]{1,0:T(8,128)(2,1)S(1)} %get-tuple-element.35), channel_id=1, source_target_pairs={{0,1},{1,0},{2,3},{3,2},{4,5},{5,4},{6,7},{7,6},{8,9},{9,8},{10,11... | collective-permute-start | bytes 196616 | tf_op jit(solution)/shard_map/ppermute | solution.py:20
  11.9 7.2 %collective-permute-start.3 = (bf16[128,256]{1,0:T(8,128)(2,1)S(1)}, bf16[128,256]{1,0:T(8,128)(2,1)S(1)}, u32[]{:S(2)}, u32[]{:S(2)}) collective-permute-start(bf16[128,256]{1,0:T(8,128)(2,1)S(1)} %get-tuple-element.29), channel_id=1, source_target_pairs={{0,3},{1,2},{2,1},{3,0},{4,7},{5,6},{6,5},{7,4},{8,11},{9,10},{10,... | collective-permute-start | bytes 196616 | tf_op jit(solution)/shard_map/ppermute | solution.py:20
  14.8 4.3 %collective-permute-start.4 = (bf16[128,256]{1,0:T(8,128)(2,1)S(1)}, bf16[128,256]{1,0:T(8,128)(2,1)S(1)}, u32[]{:S(2)}, u32[]{:S(2)}) collective-permute-start(bf16[128,256]{1,0:T(8,128)(2,1)S(1)} %get-tuple-element.30), channel_id=1, source_target_pairs={{0,1},{1,0},{2,3},{3,2},{4,5},{5,4},{6,7},{7,6},{8,9},{9,8},{10,11... | collective-permute-start | bytes 196616 | tf_op jit(solution)/shard_map/ppermute | solution.py:20
  15.3 4.3 %collective-permute-start.5 = (bf16[128,256]{1,0:T(8,128)(2,1)S(1)}, bf16[128,256]{1,0:T(8,128)(2,1)S(1)}, u32[]{:S(2)}, u32[]{:S(2)}) collective-permute-start(bf16[128,256]{1,0:T(8,128)(2,1)S(1)} %get-tuple-element.31), channel_id=1, source_target_pairs={{0,2},{1,3},{2,0},{3,1},{4,6},{5,7},{6,4},{7,5},{8,10},{9,11},{10,... | collective-permute-start | bytes 196616 | tf_op jit(solution)/shard_map/ppermute | solution.py:20
  16.3 5.3 %copy-start.4 = (bf16[1,1,128,256]{3,2,1,0:T(8,128)(2,1)S(1)}, bf16[1,1,128,256]{3,2,1,0:T(8,128)(2,1)}, u32[]{:S(2)}) copy-start(bf16[1,1,128,256]{3,2,1,0:T(8,128)(2,1)} %param.13) | copy-start | bytes 196612
  16.4 5.2 %copy-start.6 = (f32[256]{0:T(256)S(1)}, f32[256]{0:T(256)}, u32[]{:S(2)}) copy-start(f32[256]{0:T(256)} %param.9) | copy-start | bytes 3076
  16.4 5.2 %collective-permute-start.9 = (bf16[128,256]{1,0:T(8,128)(2,1)S(1)}, bf16[128,256]{1,0:T(8,128)(2,1)S(1)}, u32[]{:S(2)}, u32[]{:S(2)}) collective-permute-start(bf16[128,256]{1,0:T(8,128)(2,1)S(1)} %add_convert_fusion.2), channel_id=1, source_target_pairs={{0,4},{1,5},{2,6},{3,7},{4,0},{5,1},{6,2},{7,3},{8,12},{9,13},{10,... | collective-permute-start | bytes 196616 | tf_op jit(solution)/shard_map/ppermute | solution.py:20
  21.7 5.3 %collective-permute-start.10 = (bf16[128,256]{1,0:T(8,128)(2,1)S(1)}, bf16[128,256]{1,0:T(8,128)(2,1)S(1)}, u32[]{:S(2)}, u32[]{:S(2)}) collective-permute-start(bf16[128,256]{1,0:T(8,128)(2,1)S(1)} %get-tuple-element.44), channel_id=1, source_target_pairs={{0,4},{1,5},{2,6},{3,7},{4,0},{5,1},{6,2},{7,3},{8,12},{9,13},{10,... | collective-permute-start | bytes 196616 | tf_op jit(solution)/shard_map/ppermute | solution.py:20
  27.0 7.4 %collective-permute-start.13 = (bf16[2,128,256]{2,1,0:T(8,128)(2,1)S(1)}, bf16[2,128,256]{2,1,0:T(8,128)(2,1)S(1)}, u32[]{:S(2)}, u32[]{:S(2)}) collective-permute-start(bf16[2,128,256]{2,1,0:T(8,128)(2,1)S(1)} %pad_maximum_fusion.refs_3_), channel_id=1, source_target_pairs={{0,3},{1,2},{2,1},{3,0},{4,7},{5,6},{6,5},{7,4},{8,11},{9,10},{10,... | collective-permute-start | bytes 393224 | tf_op jit(solution)/shard_map/ppermute | solution.py:20
  29.4 5.0 %collective-permute-start.12 = (bf16[2,128,256]{2,1,0:T(8,128)(2,1)S(1)}, bf16[2,128,256]{2,1,0:T(8,128)(2,1)S(1)}, u32[]{:S(2)}, u32[]{:S(2)}) collective-permute-start(bf16[2,128,256]{2,1,0:T(8,128)(2,1)S(1)} %pad_maximum_fusion.refs_3_), channel_id=1, source_target_pairs={{0,2},{1,3},{2,0},{3,1},{4,6},{5,7},{6,4},{7,5},{8,10},{9,11},{10,... | collective-permute-start | bytes 393224 | tf_op jit(solution)/shard_map/ppermute | solution.py:20
  29.4 5.0 %collective-permute-start.11 = (bf16[2,128,256]{2,1,0:T(8,128)(2,1)S(1)}, bf16[2,128,256]{2,1,0:T(8,128)(2,1)S(1)}, u32[]{:S(2)}, u32[]{:S(2)}) collective-permute-start(bf16[2,128,256]{2,1,0:T(8,128)(2,1)S(1)} %pad_maximum_fusion.refs_3_), channel_id=1, source_target_pairs={{0,1},{1,0},{2,3},{3,2},{4,5},{5,4},{6,7},{7,6},{8,9},{9,8},{10,11... | collective-permute-start | bytes 393224 | tf_op jit(solution)/shard_map/ppermute | solution.py:20
  35.0 4.3 %collective-permute-start.14 = (bf16[128,256]{1,0:T(8,128)(2,1)S(1)}, bf16[128,256]{1,0:T(8,128)(2,1)S(1)}, u32[]{:S(2)}, u32[]{:S(2)}) collective-permute-start(bf16[128,256]{1,0:T(8,128)(2,1)S(1)} %get-tuple-element.41), channel_id=1, source_target_pairs={{0,16},{1,17},{2,18},{3,19},{4,20},{5,21},{6,22},{7,23},{8,24},{9,... | collective-permute-start | bytes 196616 | tf_op jit(solution)/shard_map/ppermute | solution.py:20
  36.6 2.8 %collective-permute-start.15 = (bf16[128,256]{1,0:T(8,128)(2,1)S(1)}, bf16[128,256]{1,0:T(8,128)(2,1)S(1)}, u32[]{:S(2)}, u32[]{:S(2)}) collective-permute-start(bf16[128,256]{1,0:T(8,128)(2,1)S(1)} %get-tuple-element.42), channel_id=1, source_target_pairs={{0,8},{1,9},{2,10},{3,11},{4,12},{5,13},{6,14},{7,15},{8,0},{9,1},... | collective-permute-start | bytes 196616 | tf_op jit(solution)/shard_map/ppermute | solution.py:20
  36.6 3.7 %collective-permute-start.16 = (bf16[128,256]{1,0:T(8,128)(2,1)S(1)}, bf16[128,256]{1,0:T(8,128)(2,1)S(1)}, u32[]{:S(2)}, u32[]{:S(2)}) collective-permute-start(bf16[128,256]{1,0:T(8,128)(2,1)S(1)} %get-tuple-element.43), channel_id=1, source_target_pairs={{0,24},{1,25},{2,26},{3,27},{4,28},{5,29},{6,30},{7,31},{8,16},{9,... | collective-permute-start | bytes 196616 | tf_op jit(solution)/shard_map/ppermute | solution.py:20

commit v8 on v6

--- a/solution.py
+++ b/solution.py
@@ -203,16 +203,17 @@
     grads = {0: (cotangent[0, 0].astype(jnp.float32) * silu_slope(preact)[1]).astype(jnp.bfloat16)}
     grads[far] = swap(grads[0], col=far)
     preact, grads[far] = lax.optimization_barrier((preact, grads[far]))
-    activated = silu_slope(preact)[0].astype(jnp.bfloat16)
     pair = jnp.stack([grads[0], grads[far]])
     places = [1, 2, 3, 0] if far == 4 else list(range(far))
-    messages = [swap(pair, col=p) if p else pair for p in places]
-    messages[0], activated = lax.optimization_barrier((messages[0], activated))
-    back = backward(places, messages, dense, weight)
+    back = backward(places, [swap(pair, col=p) if p else pair for p in places], dense, weight)
     back = dict(zip([0, *even, *(s for s in rows if s % 2)], back))
     spread = back[0].astype(jnp.float32)
     for s in (*even, 1):
-        spread = spread + swap(back[s], row=s).astype(jnp.float32)
+        got = swap(back[s], row=s)
+        if s == even[-1]:
+            preact, got = lax.optimization_barrier((preact, got))
+        spread = spread + got.astype(jnp.float32)
+    activated = silu_slope(preact)[0].astype(jnp.bfloat16)
     ready = jnp.dot(spread.astype(jnp.bfloat16), weight.T, preferred_element_type=jnp.float32)
     ready = lax.optimization_barrier(ready)
     for s in even:

time: 41.1 us -> 41.1 us (level)
    broadcast_in_dim x1 -> x2, other arithmetic: 0.64 us -> 1.32 us  [shards(): return (activated[None, None], ready.astype(jnp.bfloat16)[None, None])]
    convert_element_type x1 -> x0, other arithmetic: 0.67 us -> none  [shards(): activated = silu_slope(preact)[0].astype(jnp.bfloat16)]
  transfers between devices with their start and end apart: 17 -> 17, of which waited for: 9 -> 11; matrix products, arithmetic and copies ran while one was open for 2% -> 2% of each run, Pallas kernels for 5% -> 5%
where the time goes in v8:
time: 41.1 us; the launch traced here: 41 us
  starting transfers between devices  22.3 us (54%)
  waiting for transfers between devices  12.2 us (30%)
  Pallas kernels  2.87 us (7%)
  other arithmetic  1.48 us (4%)
  local copies, waits for them, and re-layouts  1.24 us (3%)
  between operations  0.73 us (2%)
    ppermute x17, starting transfers between devices, swap(): return lax.ppermute(value, BOTH, pairs)  22.3 us
    ppermute x17, waiting for transfers between devices, swap(): return lax.ppermute(value, BOTH, pairs)  12.2 us
    broadcast_in_dim x2, other arithmetic, shards(): return (activated[None, None], ready.astype(jnp.bfloat16)[None, None])  1.32 us
    unnamed x15, local copies, waits for them, and re-layouts  1.24 us
    pallas_call x1, Pallas kernels, dense_block(): pl.pallas_call(dense_kernel, in_specs=[HBM] * 3, out_shape=jax.ShapeDtype...  1.16 us
  transfers between devices with their start and end apart: 17, of which 11 were waited for; matrix products, arithmetic and copies ran while one was open for 2% of the time, Pallas kernels for 5%

profile of v8, /device:TPU:0, one launch (start us, length us, event | category | flops | bytes accessed | tf_op | source)
XLA Modules:
  0.0 41.0 jit_solution(18101668999063935221)
XLA Ops:
  0.6 0.0 copy-start.5
  0.6 0.0 copy-start.3
  0.6 3.0 %collective-permute-start = (bf16[128,256]{1,0:T(8,128)(2,1)}, bf16[128,256]{1,0:T(8,128)(2,1)S(1)}, u32[]{:S(2)}, u32[]{:S(2)}) collective-permute-start(bf16[128,256]{1,0:T(8,128)(2,1)} %bitcast.11), channel_id=1, source_target_pairs={{0,16},{1,17},{2,18},{3,19},{4,20},{5,21},{6,22},{7,23},{8,24},{9,... | collective-permute-start | bytes 196616 | tf_op jit(solution)/shard_map/ppermute | solution.py:20
  3.7 0.0 collective-permute-start.1
  3.7 0.0 copy-done.5
  3.7 0.1 copy.9.cols_hbm
  3.7 0.0 copy-done.3
  3.7 0.0 copy-start.1
  3.7 1.1 %copy-done.1 = bf16[1,1,8,3,128,128]{5,4,3,2,1,0:T(8,128)(2,1)S(1)} copy-done((bf16[1,1,8,3,128,128]{5,4,3,2,1,0:T(8,128)(2,1)S(1)}, bf16[1,1,8,3,128,128]{5,4,3,2,1,0:T(8,128)(2,1)}, u32[]{:S(2)}) %copy-start.1) | copy-done | bytes 786456
  4.9 0.0 copy-start
  4.9 0.0 copy-start.2
  4.9 1.2 %shard_map.86.refs_3_.dense.refs_4_ = bf16[1024,512]{1,0:T(8,128)(2,1)S(1)} custom-call(s32[1,1,8,3]{3,2,1,0:T(8,128)S(1)} %copy.9.cols_hbm, s32[1,1,8]{2,1,0:T(1,128)S(1)} %copy-done.3, bf16[1,1,8,3,128,128]{5,4,3,2,1,0:T(8,128)(2,1)S(1)} %copy-done.1), custom_call_target="tpu_custom_call" | custom-call | bytes 786432 | tf_op jit(solution)/shard_map/pallas_call | solution.py:64
  6.1 0.1 collective-permute-done.refs_1_
  6.1 0.4 %collective-permute-start.2 = (bf16[128,256]{1,0:T(8,128)(2,1)S(1)}, bf16[128,256]{1,0:T(8,128)(2,1)S(1)}, u32[]{:S(2)}, u32[]{:S(2)}) collective-permute-start(bf16[128,256]{1,0:T(8,128)(2,1)S(1)} %collective-permute-done.refs_1_), channel_id=1, source_target_pairs={{0,8},{1,9},{2,10},{3,11},{4,12},{5,13},{6,14},{7,15},{8,0},{9,1},... | collective-permute-start | bytes 196616 | tf_op jit(solution)/shard_map/ppermute | solution.py:20
  6.5 0.0 copy-done
  6.5 0.0 copy-done.2
  6.5 0.4 shard_map.87
  7.0 0.0 collective-permute-done.1.refs_0_
  7.0 0.5 %collective-permute-done.2.refs_1_ = bf16[128,256]{1,0:T(8,128)(2,1)S(1)} collective-permute-done((bf16[128,256]{1,0:T(8,128)(2,1)S(1)}, bf16[128,256]{1,0:T(8,128)(2,1)S(1)}, u32[]{:S(2)}, u32[]{:S(2)}) %collective-permute-start.2) | collective-permute-done | bytes 65568 | tf_op jit(solution)/shard_map/ppermute | solution.py:20
  7.4 0.4 shard_map.88
  7.8 3.1 %collective-permute-start.6 = (bf16[128,256]{1,0:T(8,128)(2,1)S(1)}, bf16[128,256]{1,0:T(8,128)(2,1)S(1)}, u32[]{:S(2)}, u32[]{:S(2)}) collective-permute-start(bf16[128,256]{1,0:T(8,128)(2,1)S(1)} %get-tuple-element.33), channel_id=1, source_target_pairs={{0,3},{1,2},{2,1},{3,0},{4,7},{5,6},{6,5},{7,4},{8,11},{9,10},{10,... | collective-permute-start | bytes 196616 | tf_op jit(solution)/shard_map/ppermute | solution.py:20
  10.9 0.4 %collective-permute-start.7 = (bf16[128,256]{1,0:T(8,128)(2,1)S(1)}, bf16[128,256]{1,0:T(8,128)(2,1)S(1)}, u32[]{:S(2)}, u32[]{:S(2)}) collective-permute-start(bf16[128,256]{1,0:T(8,128)(2,1)S(1)} %get-tuple-element.34), channel_id=1, source_target_pairs={{0,2},{1,3},{2,0},{3,1},{4,6},{5,7},{6,4},{7,5},{8,10},{9,11},{10,... | collective-permute-start | bytes 196616 | tf_op jit(solution)/shard_map/ppermute | solution.py:20
  11.4 0.2 collective-permute-start.8
  11.5 0.3 shard_map.89
  11.9 2.9 %collective-permute-start.3 = (bf16[128,256]{1,0:T(8,128)(2,1)S(1)}, bf16[128,256]{1,0:T(8,128)(2,1)S(1)}, u32[]{:S(2)}, u32[]{:S(2)}) collective-permute-start(bf16[128,256]{1,0:T(8,128)(2,1)S(1)} %get-tuple-element.29), channel_id=1, source_target_pairs={{0,3},{1,2},{2,1},{3,0},{4,7},{5,6},{6,5},{7,4},{8,11},{9,10},{10,... | collective-permute-start | bytes 196616 | tf_op jit(solution)/shard_map/ppermute | solution.py:20
  14.8 0.5 %collective-permute-start.4 = (bf16[128,256]{1,0:T(8,128)(2,1)S(1)}, bf16[128,256]{1,0:T(8,128)(2,1)S(1)}, u32[]{:S(2)}, u32[]{:S(2)}) collective-permute-start(bf16[128,256]{1,0:T(8,128)(2,1)S(1)} %get-tuple-element.30), channel_id=1, source_target_pairs={{0,1},{1,0},{2,3},{3,2},{4,5},{5,4},{6,7},{7,6},{8,9},{9,8},{10,11... | collective-permute-start | bytes 196616 | tf_op jit(solution)/shard_map/ppermute | solution.py:20
  15.3 0.0 collective-permute-done.6
  15.3 0.5 %collective-permute-start.5 = (bf16[128,256]{1,0:T(8,128)(2,1)S(1)}, bf16[128,256]{1,0:T(8,128)(2,1)S(1)}, u32[]{:S(2)}, u32[]{:S(2)}) collective-permute-start(bf16[128,256]{1,0:T(8,128)(2,1)S(1)} %get-tuple-element.31), channel_id=1, source_target_pairs={{0,2},{1,3},{2,0},{3,1},{4,6},{5,7},{6,4},{7,5},{8,10},{9,11},{10,... | collective-permute-start | bytes 196616 | tf_op jit(solution)/shard_map/ppermute | solution.py:20
  15.8 0.0 collective-permute-done.7
  15.8 0.5 %collective-permute-done.8 = bf16[128,256]{1,0:T(8,128)(2,1)S(1)} collective-permute-done((bf16[128,256]{1,0:T(8,128)(2,1)S(1)}, bf16[128,256]{1,0:T(8,128)(2,1)S(1)}, u32[]{:S(2)}, u32[]{:S(2)}) %collective-permute-start.8) | collective-permute-done | bytes 65568 | tf_op jit(solution)/shard_map/ppermute | solution.py:20
  16.3 0.0 copy-start.4
  16.4 0.0 copy-start.6
  16.4 2.7 %collective-permute-start.9 = (bf16[128,256]{1,0:T(8,128)(2,1)S(1)}, bf16[128,256]{1,0:T(8,128)(2,1)S(1)}, u32[]{:S(2)}, u32[]{:S(2)}) collective-permute-start(bf16[128,256]{1,0:T(8,128)(2,1)S(1)} %add_convert_fusion.2), channel_id=1, source_target_pairs={{0,4},{1,5},{2,6},{3,7},{4,0},{5,1},{6,2},{7,3},{8,12},{9,13},{10,... | collective-permute-start | bytes 196616 | tf_op jit(solution)/shard_map/ppermute | solution.py:20
  19.0 0.0 collective-permute-done.3
  19.0 0.0 collective-permute-done.4
  19.0 0.5 %collective-permute-done.5 = bf16[128,256]{1,0:T(8,128)(2,1)S(1)} collective-permute-done((bf16[128,256]{1,0:T(8,128)(2,1)S(1)}, bf16[128,256]{1,0:T(8,128)(2,1)S(1)}, u32[]{:S(2)}, u32[]{:S(2)}) %collective-permute-start.5) | collective-permute-done | bytes 65568 | tf_op jit(solution)/shard_map/ppermute | solution.py:20
  19.5 2.1 %collective-permute-done.9 = bf16[128,256]{1,0:T(8,128)(2,1)S(1)} collective-permute-done((bf16[128,256]{1,0:T(8,128)(2,1)S(1)}, bf16[128,256]{1,0:T(8,128)(2,1)S(1)}, u32[]{:S(2)}, u32[]{:S(2)}) %collective-permute-start.9) | collective-permute-done | bytes 65568 | tf_op jit(solution)/shard_map/ppermute | solution.py:20
  21.6 0.0 copy-done.4
  21.6 0.0 copy-done.6
  21.6 0.1 fusion
  21.7 2.7 %collective-permute-start.10 = (bf16[128,256]{1,0:T(8,128)(2,1)S(1)}, bf16[128,256]{1,0:T(8,128)(2,1)S(1)}, u32[]{:S(2)}, u32[]{:S(2)}) collective-permute-start(bf16[128,256]{1,0:T(8,128)(2,1)S(1)} %get-tuple-element.44), channel_id=1, source_target_pairs={{0,4},{1,5},{2,6},{3,7},{4,0},{5,1},{6,2},{7,3},{8,12},{9,13},{10,... | collective-permute-start | bytes 196616 | tf_op jit(solution)/shard_map/ppermute | solution.py:20
  24.4 2.6 %collective-permute-done.10 = bf16[128,256]{1,0:T(8,128)(2,1)S(1)} collective-permute-done((bf16[128,256]{1,0:T(8,128)(2,1)S(1)}, bf16[128,256]{1,0:T(8,128)(2,1)S(1)}, u32[]{:S(2)}, u32[]{:S(2)}) %collective-permute-start.10) | collective-permute-done | bytes 65568 | tf_op jit(solution)/shard_map/ppermute | solution.py:20
  27.0 2.4 %collective-permute-start.13 = (bf16[2,128,256]{2,1,0:T(8,128)(2,1)S(1)}, bf16[2,128,256]{2,1,0:T(8,128)(2,1)S(1)}, u32[]{:S(2)}, u32[]{:S(2)}) collective-permute-start(bf16[2,128,256]{2,1,0:T(8,128)(2,1)S(1)} %pad_maximum_fusion.refs_3_), channel_id=1, source_target_pairs={{0,3},{1,2},{2,1},{3,0},{4,7},{5,6},{6,5},{7,4},{8,11},{9,10},{10,... | collective-permute-start | bytes 393224 | tf_op jit(solution)/shard_map/ppermute | solution.py:20
  29.4 0.1 collective-permute-start.12
  29.4 1.2 %collective-permute-start.11 = (bf16[2,128,256]{2,1,0:T(8,128)(2,1)S(1)}, bf16[2,128,256]{2,1,0:T(8,128)(2,1)S(1)}, u32[]{:S(2)}, u32[]{:S(2)}) collective-permute-start(bf16[2,128,256]{2,1,0:T(8,128)(2,1)S(1)} %pad_maximum_fusion.refs_3_), channel_id=1, source_target_pairs={{0,1},{1,0},{2,3},{3,2},{4,5},{5,4},{6,7},{7,6},{8,9},{9,8},{10,11... | collective-permute-start | bytes 393224 | tf_op jit(solution)/shard_map/ppermute | solution.py:20
  30.7 2.2 %collective-permute-done.13.refs_2_ = bf16[2,128,256]{2,1,0:T(8,128)(2,1)S(1)} collective-permute-done((bf16[2,128,256]{2,1,0:T(8,128)(2,1)S(1)}, bf16[2,128,256]{2,1,0:T(8,128)(2,1)S(1)}, u32[]{:S(2)}, u32[]{:S(2)}) %collective-permute-start.13) | collective-permute-done | bytes 131104 | tf_op jit(solution)/shard_map/ppermute | solution.py:20
  32.9 1.4 %collective-permute-done.12.refs_1_ = bf16[2,128,256]{2,1,0:T(8,128)(2,1)S(1)} collective-permute-done((bf16[2,128,256]{2,1,0:T(8,128)(2,1)S(1)}, bf16[2,128,256]{2,1,0:T(8,128)(2,1)S(1)}, u32[]{:S(2)}, u32[]{:S(2)}) %collective-permute-start.12) | collective-permute-done | bytes 131104 | tf_op jit(solution)/shard_map/ppermute | solution.py:20
  34.3 0.1 collective-permute-done.11.refs_0_
  34.4 0.6 %shard_map.90 = (bf16[128,256]{1,0:T(8,128)(2,1)S(1)}, bf16[128,256]{1,0:T(8,128)(2,1)S(1)}, bf16[128,256]{1,0:T(8,128)(2,1)S(1)}, bf16[128,256]{1,0:T(8,128)(2,1)S(1)}) custom-call(bf16[2,128,256]{2,1,0:T(8,128)(2,1)S(1)} %collective-permute-done.11.refs_0_, bf16[2,128,256]{2,1,0:T(8,128)(2,1)S(1)} %collective-permute-done.12.refs_1_, ...), custom_call_target="tpu_custom_call" | custom-call | flops 268435456 | tf_op jit(solution)/shard_map/pallas_call | solution.py:172
  35.0 1.6 %collective-permute-start.14 = (bf16[128,256]{1,0:T(8,128)(2,1)S(1)}, bf16[128,256]{1,0:T(8,128)(2,1)S(1)}, u32[]{:S(2)}, u32[]{:S(2)}) collective-permute-start(bf16[128,256]{1,0:T(8,128)(2,1)S(1)} %get-tuple-element.38), channel_id=1, source_target_pairs={{0,16},{1,17},{2,18},{3,19},{4,20},{5,21},{6,22},{7,23},{8,24},{9,... | collective-permute-start | bytes 196616 | tf_op jit(solution)/shard_map/ppermute | solution.py:20
  36.6 0.0 collective-permute-start.15
  36.6 0.6 %collective-permute-start.16 = (bf16[128,256]{1,0:T(8,128)(2,1)S(1)}, bf16[128,256]{1,0:T(8,128)(2,1)S(1)}, u32[]{:S(2)}, u32[]{:S(2)}) collective-permute-start(bf16[128,256]{1,0:T(8,128)(2,1)S(1)} %get-tuple-element.43), channel_id=1, source_target_pairs={{0,24},{1,25},{2,26},{3,27},{4,28},{5,29},{6,30},{7,31},{8,16},{9,... | collective-permute-start | bytes 196616 | tf_op jit(solution)/shard_map/ppermute | solution.py:20
  37.2 2.1 %collective-permute-done.14 = bf16[128,256]{1,0:T(8,128)(2,1)S(1)} collective-permute-done((bf16[128,256]{1,0:T(8,128)(2,1)S(1)}, bf16[128,256]{1,0:T(8,128)(2,1)S(1)}, u32[]{:S(2)}, u32[]{:S(2)}) %collective-permute-start.14) | collective-permute-done | bytes 65568 | tf_op jit(solution)/shard_map/ppermute | solution.py:20
  39.3 0.0 collective-permute-done.15
  39.3 0.2 fusion.1
  39.5 0.7 %fusion.3 = bf16[1,1,128,256]{3,2,1,0:T(8,128)(2,1)} fusion(f32[128,256]{1,0:T(8,128)S(1)} %get-tuple-element.39), kind=kLoop, calls=%fused_computation.10 | loop fusion | flops 163840 | bytes 196608 | tf_op jit(solution)/shard_map/broadcast_in_dim | solution.py:221
  40.2 0.1 collective-permute-done.16
  40.3 0.6 %fusion.2 = bf16[1,1,128,256]{3,2,1,0:T(8,128)(2,1)} fusion(f32[128,256]{1,0:T(8,128)S(1)} %fusion.1, bf16[128,256]{1,0:T(8,128)(2,1)S(1)} %collective-permute-done.16), kind=kLoop, calls=%fused_computation.9 | loop fusion | flops 98304 | bytes 262144 | tf_op jit(solution)/shard_map/broadcast_in_dim | solution.py:221
  (2 shorter events, 0.1 us)
Async XLA Ops:
  0.6 3.0 %copy-start.5 = (s32[1,1,8,3]{2,1,3,0:T(1,128)S(1)}, s32[1,1,8,3]{2,1,3,0:T(1,128)}, u32[]{:S(2)}) copy-start(s32[1,1,8,3]{2,1,3,0:T(1,128)} %param.11) | copy-start | bytes 292
  0.6 3.1 %copy-start.3 = (s32[1,1,8]{2,1,0:T(1,128)S(1)}, s32[1,1,8]{2,1,0:T(1,128)}, u32[]{:S(2)}) copy-start(s32[1,1,8]{2,1,0:T(1,128)} %counts_hbm.1) | copy-start | bytes 100
  0.6 5.5 %collective-permute-start = (bf16[128,256]{1,0:T(8,128)(2,1)}, bf16[128,256]{1,0:T(8,128)(2,1)S(1)}, u32[]{:S(2)}, u32[]{:S(2)}) collective-permute-start(bf16[128,256]{1,0:T(8,128)(2,1)} %bitcast.11), channel_id=1, source_target_pairs={{0,16},{1,17},{2,18},{3,19},{4,20},{5,21},{6,22},{7,23},{8,24},{9,... | collective-permute-start | bytes 196616 | tf_op jit(solution)/shard_map/ppermute | solution.py:20
  3.7 3.3 %collective-permute-start.1 = (bf16[128,256]{1,0:T(8,128)(2,1)}, bf16[128,256]{1,0:T(8,128)(2,1)S(1)}, u32[]{:S(2)}, u32[]{:S(2)}) collective-permute-start(bf16[128,256]{1,0:T(8,128)(2,1)} %bitcast.12), channel_id=1, source_target_pairs={{0,8},{1,9},{2,10},{3,11},{4,12},{5,13},{6,14},{7,15},{8,0},{9,1},... | collective-permute-start | bytes 196616 | tf_op jit(solution)/shard_map/ppermute | solution.py:20
  3.7 1.1 %copy-start.1 = (bf16[1,1,8,3,128,128]{5,4,3,2,1,0:T(8,128)(2,1)S(1)}, bf16[1,1,8,3,128,128]{5,4,3,2,1,0:T(8,128)(2,1)}, u32[]{:S(2)}) copy-start(bf16[1,1,8,3,128,128]{5,4,3,2,1,0:T(8,128)(2,1)} %tiles_hbm.1) | copy-start | bytes 2359300
  4.9 1.7 %copy-start = (bf16[256,256]{1,0:T(8,128)(2,1)S(1)}, bf16[256,256]{1,0:T(8,128)(2,1)}, u32[]{:S(2)}) copy-start(bf16[256,256]{1,0:T(8,128)(2,1)} %refs_5_.1) | copy-start | bytes 393220
  4.9 1.7 %copy-start.2 = (bf16[1,1,128,256]{3,2,1,0:T(8,128)(2,1)S(1)}, bf16[1,1,128,256]{3,2,1,0:T(8,128)(2,1)}, u32[]{:S(2)}) copy-start(bf16[1,1,128,256]{3,2,1,0:T(8,128)(2,1)} %param.7) | copy-start | bytes 196612
  6.1 1.3 %collective-permute-start.2 = (bf16[128,256]{1,0:T(8,128)(2,1)S(1)}, bf16[128,256]{1,0:T(8,128)(2,1)S(1)}, u32[]{:S(2)}, u32[]{:S(2)}) collective-permute-start(bf16[128,256]{1,0:T(8,128)(2,1)S(1)} %collective-permute-done.refs_1_), channel_id=1, source_target_pairs={{0,8},{1,9},{2,10},{3,11},{4,12},{5,13},{6,14},{7,15},{8,0},{9,1},... | collective-permute-start | bytes 196616 | tf_op jit(solution)/shard_map/ppermute | solution.py:20
  7.8 7.4 %collective-permute-start.6 = (bf16[128,256]{1,0:T(8,128)(2,1)S(1)}, bf16[128,256]{1,0:T(8,128)(2,1)S(1)}, u32[]{:S(2)}, u32[]{:S(2)}) collective-permute-start(bf16[128,256]{1,0:T(8,128)(2,1)S(1)} %get-tuple-element.33), channel_id=1, source_target_pairs={{0,3},{1,2},{2,1},{3,0},{4,7},{5,6},{6,5},{7,4},{8,11},{9,10},{10,... | collective-permute-start | bytes 196616 | tf_op jit(solution)/shard_map/ppermute | solution.py:20
  10.9 4.9 %collective-permute-start.7 = (bf16[128,256]{1,0:T(8,128)(2,1)S(1)}, bf16[128,256]{1,0:T(8,128)(2,1)S(1)}, u32[]{:S(2)}, u32[]{:S(2)}) collective-permute-start(bf16[128,256]{1,0:T(8,128)(2,1)S(1)} %get-tuple-element.34), channel_id=1, source_target_pairs={{0,2},{1,3},{2,0},{3,1},{4,6},{5,7},{6,4},{7,5},{8,10},{9,11},{10,... | collective-permute-start | bytes 196616 | tf_op jit(solution)/shard_map/ppermute | solution.py:20
  11.4 5.0 %collective-permute-start.8 = (bf16[128,256]{1,0:T(8,128)(2,1)S(1)}, bf16[128,256]{1,0:T(8,128)(2,1)S(1)}, u32[]{:S(2)}, u32[]{:S(2)}) collective-permute-start(bf16[128,256]{1,0:T(8,128)(2,1)S(1)} %get-tuple-element.35), channel_id=1, source_target_pairs={{0,1},{1,0},{2,3},{3,2},{4,5},{5,4},{6,7},{7,6},{8,9},{9,8},{10,11... | collective-permute-start | bytes 196616 | tf_op jit(solution)/shard_map/ppermute | solution.py:20
  11.9 7.2 %collective-permute-start.3 = (bf16[128,256]{1,0:T(8,128)(2,1)S(1)}, bf16[128,256]{1,0:T(8,128)(2,1)S(1)}, u32[]{:S(2)}, u32[]{:S(2)}) collective-permute-start(bf16[128,256]{1,0:T(8,128)(2,1)S(1)} %get-tuple-element.29), channel_id=1, source_target_pairs={{0,3},{1,2},{2,1},{3,0},{4,7},{5,6},{6,5},{7,4},{8,11},{9,10},{10,... | collective-permute-start | bytes 196616 | tf_op jit(solution)/shard_map/ppermute | solution.py:20
  14.8 4.3 %collective-permute-start.4 = (bf16[128,256]{1,0:T(8,128)(2,1)S(1)}, bf16[128,256]{1,0:T(8,128)(2,1)S(1)}, u32[]{:S(2)}, u32[]{:S(2)}) collective-permute-start(bf16[128,256]{1,0:T(8,128)(2,1)S(1)} %get-tuple-element.30), channel_id=1, source_target_pairs={{0,1},{1,0},{2,3},{3,2},{4,5},{5,4},{6,7},{7,6},{8,9},{9,8},{10,11... | collective-permute-start | bytes 196616 | tf_op jit(solution)/shard_map/ppermute | solution.py:20
  15.3 4.3 %collective-permute-start.5 = (bf16[128,256]{1,0:T(8,128)(2,1)S(1)}, bf16[128,256]{1,0:T(8,128)(2,1)S(1)}, u32[]{:S(2)}, u32[]{:S(2)}) collective-permute-start(bf16[128,256]{1,0:T(8,128)(2,1)S(1)} %get-tuple-element.31), channel_id=1, source_target_pairs={{0,2},{1,3},{2,0},{3,1},{4,6},{5,7},{6,4},{7,5},{8,10},{9,11},{10,... | collective-permute-start | bytes 196616 | tf_op jit(solution)/shard_map/ppermute | solution.py:20
  16.3 5.3 %copy-start.4 = (bf16[1,1,128,256]{3,2,1,0:T(8,128)(2,1)S(1)}, bf16[1,1,128,256]{3,2,1,0:T(8,128)(2,1)}, u32[]{:S(2)}) copy-start(bf16[1,1,128,256]{3,2,1,0:T(8,128)(2,1)} %param.13) | copy-start | bytes 196612
  16.4 5.2 %copy-start.6 = (f32[256]{0:T(256)S(1)}, f32[256]{0:T(256)}, u32[]{:S(2)}) copy-start(f32[256]{0:T(256)} %param.9) | copy-start | bytes 3076
  16.4 5.2 %collective-permute-start.9 = (bf16[128,256]{1,0:T(8,128)(2,1)S(1)}, bf16[128,256]{1,0:T(8,128)(2,1)S(1)}, u32[]{:S(2)}, u32[]{:S(2)}) collective-permute-start(bf16[128,256]{1,0:T(8,128)(2,1)S(1)} %add_convert_fusion.2), channel_id=1, source_target_pairs={{0,4},{1,5},{2,6},{3,7},{4,0},{5,1},{6,2},{7,3},{8,12},{9,13},{10,... | collective-permute-start | bytes 196616 | tf_op jit(solution)/shard_map/ppermute | solution.py:20
  21.7 5.3 %collective-permute-start.10 = (bf16[128,256]{1,0:T(8,128)(2,1)S(1)}, bf16[128,256]{1,0:T(8,128)(2,1)S(1)}, u32[]{:S(2)}, u32[]{:S(2)}) collective-permute-start(bf16[128,256]{1,0:T(8,128)(2,1)S(1)} %get-tuple-element.44), channel_id=1, source_target_pairs={{0,4},{1,5},{2,6},{3,7},{4,0},{5,1},{6,2},{7,3},{8,12},{9,13},{10,... | collective-permute-start | bytes 196616 | tf_op jit(solution)/shard_map/ppermute | solution.py:20
  27.0 5.9 %collective-permute-start.13 = (bf16[2,128,256]{2,1,0:T(8,128)(2,1)S(1)}, bf16[2,128,256]{2,1,0:T(8,128)(2,1)S(1)}, u32[]{:S(2)}, u32[]{:S(2)}) collective-permute-start(bf16[2,128,256]{2,1,0:T(8,128)(2,1)S(1)} %pad_maximum_fusion.refs_3_), channel_id=1, source_target_pairs={{0,3},{1,2},{2,1},{3,0},{4,7},{5,6},{6,5},{7,4},{8,11},{9,10},{10,... | collective-permute-start | bytes 393224 | tf_op jit(solution)/shard_map/ppermute | solution.py:20
  29.4 5.0 %collective-permute-start.12 = (bf16[2,128,256]{2,1,0:T(8,128)(2,1)S(1)}, bf16[2,128,256]{2,1,0:T(8,128)(2,1)S(1)}, u32[]{:S(2)}, u32[]{:S(2)}) collective-permute-start(bf16[2,128,256]{2,1,0:T(8,128)(2,1)S(1)} %pad_maximum_fusion.refs_3_), channel_id=1, source_target_pairs={{0,2},{1,3},{2,0},{3,1},{4,6},{5,7},{6,4},{7,5},{8,10},{9,11},{10,... | collective-permute-start | bytes 393224 | tf_op jit(solution)/shard_map/ppermute | solution.py:20
  29.4 5.0 %collective-permute-start.11 = (bf16[2,128,256]{2,1,0:T(8,128)(2,1)S(1)}, bf16[2,128,256]{2,1,0:T(8,128)(2,1)S(1)}, u32[]{:S(2)}, u32[]{:S(2)}) collective-permute-start(bf16[2,128,256]{2,1,0:T(8,128)(2,1)S(1)} %pad_maximum_fusion.refs_3_), channel_id=1, source_target_pairs={{0,1},{1,0},{2,3},{3,2},{4,5},{5,4},{6,7},{7,6},{8,9},{9,8},{10,11... | collective-permute-start | bytes 393224 | tf_op jit(solution)/shard_map/ppermute | solution.py:20
  35.0 4.3 %collective-permute-start.14 = (bf16[128,256]{1,0:T(8,128)(2,1)S(1)}, bf16[128,256]{1,0:T(8,128)(2,1)S(1)}, u32[]{:S(2)}, u32[]{:S(2)}) collective-permute-start(bf16[128,256]{1,0:T(8,128)(2,1)S(1)} %get-tuple-element.38), channel_id=1, source_target_pairs={{0,16},{1,17},{2,18},{3,19},{4,20},{5,21},{6,22},{7,23},{8,24},{9,... | collective-permute-start | bytes 196616 | tf_op jit(solution)/shard_map/ppermute | solution.py:20
  36.6 2.8 %collective-permute-start.15 = (bf16[128,256]{1,0:T(8,128)(2,1)S(1)}, bf16[128,256]{1,0:T(8,128)(2,1)S(1)}, u32[]{:S(2)}, u32[]{:S(2)}) collective-permute-start(bf16[128,256]{1,0:T(8,128)(2,1)S(1)} %get-tuple-element.42), channel_id=1, source_target_pairs={{0,8},{1,9},{2,10},{3,11},{4,12},{5,13},{6,14},{7,15},{8,0},{9,1},... | collective-permute-start | bytes 196616 | tf_op jit(solution)/shard_map/ppermute | solution.py:20
  36.6 3.7 %collective-permute-start.16 = (bf16[128,256]{1,0:T(8,128)(2,1)S(1)}, bf16[128,256]{1,0:T(8,128)(2,1)S(1)}, u32[]{:S(2)}, u32[]{:S(2)}) collective-permute-start(bf16[128,256]{1,0:T(8,128)(2,1)S(1)} %get-tuple-element.43), channel_id=1, source_target_pairs={{0,24},{1,25},{2,26},{3,27},{4,28},{5,29},{6,30},{7,31},{8,16},{9,... | collective-permute-start | bytes 196616 | tf_op jit(solution)/shard_map/ppermute | solution.py:20
